TPU v7x, 32 devices: a whole 2x2x4 slice. The times are simulated.
32 devices in a mesh: dp: 8 (over z, y), tensor: 4 (over x, core).
Axes of the slice: x: 2, y: 2, z: 4, core: 2. Of those that a mesh axis runs over, the one named last changes fastest.
Arguments:
- hidden: float32 [16384, 1024], P(('dp', 'tensor')), may hold values from -6 to 6
- segment_ids: int32 [8, 2048], P('dp'), may hold values from 0 to 4, never falling along the last dimension, each value on 1 to 1024 neighbouring positions
- in_gain: bfloat16 [2, 1024], P(None, 'dp'), may hold values from 0.5 to 1.5
- w_zx: bfloat16 [2, 1024, 2, 2048], P(None, 'dp', None, 'tensor'), may hold values from -0.1875 to 0.1875
- w_bcdt: bfloat16 [2, 1024, 288], P(None, 'dp'), may hold values from -0.1875 to 0.1875
- w_out: bfloat16 [2, 1024, 2048], P(None, 'dp', 'tensor'), may hold values from -0.125 to 0.125
- conv_x: float32 [2, 4, 2048], P(None, None, 'tensor'), may hold values from -3 to 3
- conv_x_bias: float32 [2, 2048], P(None, 'tensor'), may hold values from -3 to 3
- conv_bc: float32 [2, 4, 256], replicated, may hold values from -3 to 3
- conv_bc_bias: float32 [2, 256], replicated, may hold values from -3 to 3
- dt_bias: float32 [2, 32], P(None, 'tensor'), may hold values from -6 to -2
- a_log: float32 [2, 32], P(None, 'tensor'), may hold values from -4 to 1
- d_skip: float32 [2, 32], P(None, 'tensor'), may hold values from 0.5 to 1.5
- out_gain: float32 [2, 2048], P(None, 'tensor'), may hold values from 0.5 to 1.5
- cotangent: float32 [16384, 1024], P(('dp', 'tensor')), may hold values from -6 to 6
Outputs:
- result: float32 [16384, 1024], P(('dp', 'tensor'))
- grad_hidden: float32 [16384, 1024], P(('dp', 'tensor'))
- grad_in_gain: float32 [2, 1024], P(None, ('dp', 'tensor'))
- grad_w_zx: float32 [2, 1024, 2, 2048], P(None, 'dp', None, 'tensor')
- grad_w_bcdt: float32 [2, 1024, 288], P(None, ('dp', 'tensor'))
- grad_w_out: float32 [2, 1024, 2048], P(None, 'dp', 'tensor')
- grad_conv_x: float32 [2, 4, 2048], P(None, None, 'tensor')
- grad_conv_x_bias: float32 [2, 2048], P(None, 'tensor')
- grad_conv_bc: float32 [2, 4, 256], replicated
- grad_conv_bc_bias: float32 [2, 256], replicated
- grad_dt_bias: float32 [2, 32], P(None, 'tensor')
- grad_a_log: float32 [2, 32], P(None, 'tensor')
- grad_d_skip: float32 [2, 32], P(None, 'tensor')
- grad_out_gain: float32 [2, 2048], P(None, 'tensor')
All inputs are finite; a program needn't handle non-finite values.
Results may differ from a plain program's by a relative error of at most 0.03.
Values may be sent and summed in bfloat16 or wider, within the bound.
No kernel may reach another device: no remote copies, remote signals or barrier semaphores. Data moves between devices by JAX's collectives and lax.ppermute only.
A program may use at most 256 MiB of HBM per device.

v0:
```python
from functools import partial

import jax
import jax.numpy as jnp
from jax import lax
from jax.sharding import PartitionSpec as P

SPAN = 256


epsilon = 1e-05
highest = lax.Precision.HIGHEST


def conv_silu(values, weights, biases, segment):
    seq_len = values.shape[1]
    summed = biases + weights[0] * values
    for offset in range(1, weights.shape[0]):
        shifted = jnp.pad(values, ((0, 0), (offset, 0), (0, 0)))[:, :seq_len]
        earlier = jnp.pad(segment, ((0, 0), (offset, 0)), constant_values=-1)[:, :seq_len]
        keeping = (earlier == segment).astype(jnp.float32)[:, :, None]
        summed = summed + weights[offset] * shifted * keeping
    return jax.nn.silu(summed)


def ssd_scan(values, steps_dt, decay_rate, keys_b, reads_c, segment):
    seq_count, seq_len, head_count, head_dim = values.shape
    blocks = seq_len // SPAN

    def to_blocks(source):
        reshaped = source.reshape((seq_count, blocks, SPAN) + source.shape[2:])
        return jnp.moveaxis(reshaped, 1, 0)

    lower_tri = lax.broadcasted_iota(jnp.int32, (SPAN, SPAN), 0) >= lax.broadcasted_iota(
        jnp.int32, (SPAN, SPAN), 1
    )

    def block_step(carried_in, block_in):
        state_now, previous = carried_in
        block_x, block_dt, block_b, block_c, block_seg = block_in
        cumulative = jnp.cumsum(block_dt * decay_rate, axis=1)
        same_doc = (block_seg[:, :, None] == block_seg[:, None, :]) & lower_tri
        between = cumulative[:, :, None, :] - cumulative[:, None, :, :]
        mixing = jnp.where(same_doc[:, :, :, None], jnp.exp(jnp.minimum(between, 0.0)), 0.0)
        intersection = jnp.einsum("sin,sjn->sij", block_c, block_b, precision=highest)
        weighted = mixing * intersection[:, :, :, None] * block_dt[:, None, :, :]
        output = jnp.einsum("sijh,sjhp->sihp", weighted, block_x, precision=highest)
        carried = (block_seg == previous[:, None]).astype(jnp.float32)
        factor = jnp.exp(cumulative) * carried[:, :, None]
        output = (
            output
            + jnp.einsum("sin,shpn->sihp", block_c, state_now, precision=highest)
            * factor[:, :, :, None]
        )
        ending = (
            jnp.exp(cumulative[:, -1:, :] - cumulative)
            * (block_seg == block_seg[:, -1:]).astype(jnp.float32)[:, :, None]
            * block_dt
        )
        state_now = state_now * factor[:, -1][:, :, None, None] + jnp.einsum(
            "sjh,sjhp,sjn->shpn", ending, block_x, block_b, precision=highest
        )
        return ((state_now, block_seg[:, -1]), output)

    initial = (
        jnp.zeros((seq_count, head_count, head_dim, keys_b.shape[-1]), jnp.float32),
        jnp.full((seq_count,), -1, jnp.int32),
    )
    unused, outputs = lax.scan(
        jax.checkpoint(block_step),
        initial,
        (
            to_blocks(values),
            to_blocks(steps_dt),
            to_blocks(keys_b),
            to_blocks(reads_c),
            to_blocks(segment),
        ),
    )
    return jnp.moveaxis(outputs, 0, 1).reshape(values.shape)


def mixer(
    gate_z,
    inner_x,
    state_bc,
    step_pre,
    conv_xw,
    conv_xb,
    conv_bcw,
    conv_bcb,
    dt_shift,
    log_rate,
    skip_scale,
    segment,
):
    seq_count, seq_len = segment.shape
    row_count = gate_z.shape[0]
    head_count = step_pre.shape[1]
    conv_out = conv_silu(inner_x.reshape(seq_count, seq_len, -1), conv_xw, conv_xb, segment)
    state_in = conv_silu(state_bc.reshape(seq_count, seq_len, -1), conv_bcw, conv_bcb, segment)
    half_bc = state_in.shape[-1] // 2
    step_dt = jax.nn.softplus(step_pre.reshape(seq_count, seq_len, head_count) + dt_shift)
    heads_x = conv_out.reshape(seq_count, seq_len, head_count, -1)
    scanned = ssd_scan(
        heads_x,
        step_dt,
        -jnp.exp(log_rate),
        state_in[..., :half_bc],
        state_in[..., half_bc:],
        segment,
    )
    scanned = scanned + skip_scale[:, None] * heads_x
    return scanned.reshape(row_count, -1) * jax.nn.silu(gate_z)


def stacked(items):
    return jnp.stack(items[::-1], axis=0)


def body(
    hidden,
    segment_ids,
    in_gain,
    w_zx,
    w_bcdt,
    w_out,
    conv_x,
    conv_x_bias,
    conv_bc,
    conv_bc_bias,
    dt_bias,
    a_log,
    d_skip,
    out_gain,
    cotangent,
):
    layer_count = in_gain.shape[0]
    bc_width = conv_bc.shape[2]
    heads_own = dt_bias.shape[1]
    all_heads = w_bcdt.shape[2] - bc_width
    head_start = lax.axis_index("tensor") * heads_own
    full_inner = out_gain.shape[1] * lax.axis_size("tensor")
    local_rows = hidden.shape[0]
    local_mixer = partial(mixer, segment=segment_ids)
    stream = hidden
    saved = []
    for layer_at in range(layer_count):
        fetched = (
            lax.all_gather(w_zx[layer_at], "dp", axis=0, tiled=True),
            lax.all_gather(w_bcdt[layer_at], "dp", axis=0, tiled=True),
            lax.all_gather(w_out[layer_at], "dp", axis=0, tiled=True),
            lax.all_gather(in_gain[layer_at], "dp", axis=0, tiled=True),
        )
        proj_zx, proj_bcdt, proj_out, in_scale = fetched
        inv_rms = lax.rsqrt(jnp.mean(stream * stream, axis=-1, keepdims=True) + epsilon)
        normed = lax.all_gather(
            (stream * inv_rms * in_scale).astype(jnp.bfloat16), "tensor", axis=0, tiled=True
        )
        both = jnp.einsum("td,dki->tki", normed, proj_zx, preferred_element_type=jnp.float32)
        shared = jnp.dot(normed, proj_bcdt, preferred_element_type=jnp.float32)
        step_pre = lax.dynamic_slice_in_dim(shared, bc_width + head_start, heads_own, 1)
        inputs = (
            both[:, 0],
            both[:, 1],
            shared[:, :bc_width],
            step_pre,
            conv_x[layer_at],
            conv_x_bias[layer_at],
            conv_bc[layer_at],
            conv_bc_bias[layer_at],
            dt_bias[layer_at],
            a_log[layer_at],
            d_skip[layer_at],
        )
        gated = local_mixer(*inputs)
        squares = lax.psum(jnp.sum(gated * gated, axis=-1), "tensor")
        gate_rms = lax.rsqrt(squares / full_inner + epsilon)[:, None]
        mixed = (gated * gate_rms * out_gain[layer_at]).astype(jnp.bfloat16)

        def project_out(first_row, row_count, mixed=mixed, proj_out=proj_out):
            return jnp.einsum("ti,di->td", mixed, proj_out, preferred_element_type=jnp.float32)

        branch = lax.psum_scatter(
            project_out(jnp.int32(0), local_rows * lax.axis_size("tensor")).astype(jnp.bfloat16),
            "tensor",
            scatter_dimension=0,
            tiled=True,
        ).astype(jnp.float32)
        kept_rows = None
        saved.append((stream, inv_rms, normed, inputs, gate_rms, mixed, kept_rows))
        stream = stream + branch
    grad_stream = cotangent
    zx_grads, out_grads, bcdt_grads, gain_grads, head_parts, state_parts = ([], [], [], [], [], [])
    for layer_at in reversed(range(layer_count)):
        stream_in, inv_rms, normed, inputs, gate_rms, mixed, kept_rows = saved[layer_at]
        proj_zx, proj_bcdt, proj_out, in_scale = (
            lax.all_gather(w_zx[layer_at], "dp", axis=0, tiled=True),
            lax.all_gather(w_bcdt[layer_at], "dp", axis=0, tiled=True),
            lax.all_gather(w_out[layer_at], "dp", axis=0, tiled=True),
            lax.all_gather(in_gain[layer_at], "dp", axis=0, tiled=True),
        )
        out_grad = lax.all_gather(grad_stream.astype(jnp.bfloat16), "tensor", axis=0, tiled=True)
        grad_proj_out = jnp.einsum("td,ti->di", out_grad, mixed, preferred_element_type=jnp.float32)
        grad_mixed = jnp.dot(out_grad, proj_out, preferred_element_type=jnp.float32)
        gated, pullback = jax.vjp(local_mixer, *inputs)
        grad_out_scale = jnp.sum(grad_mixed * gated * gate_rms, axis=0)
        grad_hat = grad_mixed * out_gain[layer_at]
        inner_prod = lax.psum(jnp.sum(grad_hat * gated, axis=-1), "tensor")
        grad_gated = gate_rms * grad_hat - gated * gate_rms**3 * (inner_prod / full_inner)[:, None]
        pieces = pullback(grad_gated)
        grad_zx = jnp.stack([pieces[0], pieces[1]], axis=1).astype(jnp.bfloat16)
        grad_dt_full = lax.dynamic_update_slice_in_dim(
            jnp.zeros((pieces[3].shape[0], all_heads), jnp.float32), pieces[3], head_start, 1
        )
        grad_shared = jnp.concatenate([pieces[2], grad_dt_full], axis=1).astype(jnp.bfloat16)
        grad_proj_zx = jnp.einsum(
            "td,tki->dki", normed, grad_zx, preferred_element_type=jnp.float32
        )
        grad_proj_bcdt = jnp.einsum(
            "td,tc->dc", normed, grad_shared, preferred_element_type=jnp.float32
        )

        def project_back(
            first_row,
            row_count,
            grad_zx=grad_zx,
            grad_shared=grad_shared,
            proj_zx=proj_zx,
            proj_bcdt=proj_bcdt,
        ):
            first_term = jnp.einsum(
                "tki,dki->td", grad_zx, proj_zx, preferred_element_type=jnp.float32
            )
            return first_term + jnp.einsum(
                "tc,dc->td", grad_shared, proj_bcdt, preferred_element_type=jnp.float32
            )

        grad_normed = lax.psum_scatter(
            project_back(jnp.int32(0), local_rows * lax.axis_size("tensor")).astype(jnp.bfloat16),
            "tensor",
            scatter_dimension=0,
            tiled=True,
        ).astype(jnp.float32)
        scaled_in = stream_in * inv_rms
        grad_in_scale = jnp.sum(grad_normed * scaled_in, axis=0)
        grad_scaled = grad_normed * in_scale
        grad_stream = grad_stream + inv_rms * (
            grad_scaled - scaled_in * jnp.mean(grad_scaled * scaled_in, axis=-1, keepdims=True)
        )
        reduced_zx, reduced_out = (
            lax.psum_scatter(grad_proj_zx, "dp", scatter_dimension=0, tiled=True),
            lax.psum_scatter(grad_proj_out, "dp", scatter_dimension=0, tiled=True),
        )
        zx_grads.append(reduced_zx)
        out_grads.append(reduced_out)
        bcdt_grads.append(grad_proj_bcdt)
        gain_grads.append(grad_in_scale)
        head_parts.append((pieces[4], pieces[5], grad_out_scale, pieces[8], pieces[9], pieces[10]))
        state_parts.append((pieces[6], pieces[7]))
    grad_w_zx = stacked(zx_grads)
    grad_w_out = stacked(out_grads)
    grad_w_bcdt, grad_in_gain = (
        lax.psum_scatter(stacked(bcdt_grads), ("dp", "tensor"), scatter_dimension=1, tiled=True),
        lax.psum_scatter(stacked(gain_grads), ("dp", "tensor"), scatter_dimension=1, tiled=True),
    )
    conv_x_part = stacked([part[0] for part in head_parts])
    conv_xb_part = stacked([part[1] for part in head_parts])
    out_gain_part = stacked([part[2] for part in head_parts])
    dt_part = stacked([part[3] for part in head_parts])
    rate_part = stacked([part[4] for part in head_parts])
    skip_part = stacked([part[5] for part in head_parts])
    grad_conv_x, grad_conv_x_bias, grad_out_gain, grad_dt_bias, grad_a_log, grad_d_skip = lax.psum(
        (conv_x_part, conv_xb_part, out_gain_part, dt_part, rate_part, skip_part), "dp"
    )
    conv_bc_part = stacked([part[0] for part in state_parts])
    conv_bcb_part = stacked([part[1] for part in state_parts])
    grad_conv_bc, grad_conv_bc_bias = lax.psum((conv_bc_part, conv_bcb_part), ("dp", "tensor"))
    return (
        stream,
        grad_stream,
        grad_in_gain,
        grad_w_zx,
        grad_w_bcdt,
        grad_w_out,
        grad_conv_x,
        grad_conv_x_bias,
        grad_conv_bc,
        grad_conv_bc_bias,
        grad_dt_bias,
        grad_a_log,
        grad_d_skip,
        grad_out_gain,
    )


def solution(mesh):
    placed = (
        P(("dp", "tensor"), None),
        P("dp", None),
        P(None, "dp"),
        P(None, "dp", None, "tensor"),
        P(None, "dp", None),
        P(None, "dp", "tensor"),
        P(None, None, "tensor"),
        P(None, "tensor"),
        P(),
        P(),
        P(None, "tensor"),
        P(None, "tensor"),
        P(None, "tensor"),
        P(None, "tensor"),
        P(("dp", "tensor"), None),
    )
    return jax.shard_map(
        body,
        mesh=mesh,
        in_specs=placed,
        out_specs=(
            P(("dp", "tensor"), None),
            P(("dp", "tensor"), None),
            P(None, ("dp", "tensor")),
            P(None, "dp", None, "tensor"),
            P(None, ("dp", "tensor"), None),
            P(None, "dp", "tensor"),
            P(None, None, "tensor"),
            P(None, "tensor"),
            P(),
            P(),
            P(None, "tensor"),
            P(None, "tensor"),
            P(None, "tensor"),
            P(None, "tensor"),
        ),
        check_vma=False,
    )
```

profile of v0, /device:TPU:0, one launch (start us, length us, event | category | flops | bytes accessed | tf_op | source)
XLA Modules:
  0.0 2288.8 jit_solution(839149176405608295)
XLA Ops:
  8.5 22.1 all-gather
  38.2 27.8 %all-gather.1 = bf16[1,1024,288]{1,2,0:T(8,128)(2,1)S(1)} all-gather(bf16[1,128,288]{1,2,0:T(8,128)(2,1)S(1)} %get-tuple-element.2104), channel_id=3, replica_groups=mesh['dp'=8,'tensor'=4] {'dp'}, dimensions={1}, use_global_device_ids=true | all-gather | bytes 663552 | tf_op jit(solution)/shard_map/all_gather | solution.py:151
  85.6 33.9 %all-gather.25.cloned.1.call-done = bf16[1,1024,2,512]{3,1,2,0:T(8,128)(2,1)} async-done(((bf16[1,128,2,512]{3,1,2,0:T(8,128)(2,1)}), bf16[1,1024,2,512]{3,1,2,0:T(8,128)(2,1)}) %all-gather.25.cloned.1.call-update) | async-done | bytes 2097168 | tf_op jit(solution)/shard_map/all_gather | solution.py:150
  151.9 99.1 %while.120 = (s32[]{:T(128)}, f32[1,8,64,128]{3,2,1,0:T(8,128)S(1)}, s32[1]{0:T(128)}, f32[8,1,256,8,64]{2,4,3,1,0:T(8,128)}, f32[8,1,256,8]{2,3,1,0:T(8,128)S(1...) while((s32[]{:T(128)}, f32[1,8,64,128]{3,2,1,0:T(8,128)S(1)}, ...), condition=%wide.region_4.5_spmd.clone, body=%wide.region_1.4_spmd.clone.sunk | while | flops 909718528 | bytes 4757948 | solution.py:69
  298.7 19.3 all-gather.4
  318.0 23.6 %reduce-scatter.12.cloned.1.call-done = bf16[512,1024]{1,0:T(8,128)(2,1)} async-done(((bf16[2048,1024]{1,0:T(8,128)(2,1)}), bf16[512,1024]{1,0:T(8,128)(2,1)}) %reduce-scatter.12.cloned.1.call-update) | async-done | bytes 1048592 | tf_op jit(solution)/shard_map/reduce_scatter | solution.py:184
  350.8 28.0 %all-gather.5 = bf16[1,1024,288]{1,2,0:T(8,128)(2,1)S(1)} all-gather(bf16[1,128,288]{1,2,0:T(8,128)(2,1)S(1)} %copy-done.57), channel_id=7, replica_groups=mesh['dp'=8,'tensor'=4] {'dp'}, dimensions={1}, use_global_device_ids=true | all-gather | bytes 663552 | tf_op jit(solution)/shard_map/all_gather | solution.py:151
  393.4 39.2 %all-gather.29.cloned.1.call-done = bf16[1,1024,2,512]{3,1,2,0:T(8,128)(2,1)} async-done(((bf16[1,128,2,512]{3,1,2,0:T(8,128)(2,1)}), bf16[1,1024,2,512]{3,1,2,0:T(8,128)(2,1)}) %all-gather.29.cloned.1.call-update) | async-done | bytes 2097168 | tf_op jit(solution)/shard_map/all_gather | solution.py:150
  467.2 130.3 %while.122 = (s32[]{:T(128)}, f32[1,8,64,128]{3,2,1,0:T(8,128)S(1)}, s32[1]{0:T(128)}, f32[8,1,256,8,64]{2,4,3,1,0:T(8,128)}, f32[8,1,8,64,128]{4,3,2,1,0:T(8,12...) while((s32[]{:T(128)}, f32[1,8,64,128]{3,2,1,0:T(8,128)S(1)}, ...), condition=%wide.region_19.21_spmd.clone, body=%wide.region_16.20_spmd.clone.sunk | while | flops 909784064 | bytes 5283257 | solution.py:69
  600.0 102.3 %while.121 = (s32[]{:T(128)}, f32[1,8,64,128]{3,2,1,0:T(8,128)S(1)}, s32[1]{0:T(128)}, f32[8,1,256,8,64]{2,4,3,1,0:T(8,128)}, f32[8,1,256,8]{2,3,1,0:T(8,128)S(1...) while((s32[]{:T(128)}, f32[1,8,64,128]{3,2,1,0:T(8,128)S(1)}, ...), condition=%wide.region_12.13_spmd.clone, body=%wide.region_9.12_spmd.clone.sunk | while | flops 909718528 | bytes 4758428 | solution.py:69
  802.2 272.5 %while.123 = (s32[]{:T(128)}, f32[8]{0:T(128)}, f32[1,8,64,128]{3,2,1,0:T(8,128)S(1)}, f32[8,1,256,8,64]{2,4,3,1,0:T(8,128)}, f32[8,1,256,8]{2,3,1,0:T(8,128)}, ...) while((s32[]{:T(128)}, f32[8]{0:T(128)}, ...), condition=%wide.region_35.37_spmd.clone, body=%wide.region_22.36_spmd.clone.sunk | while | flops 2128796672 | bytes 17127912 | solution.py:69
  1127.2 41.1 %reduce-scatter.16.cloned.1.call-done = bf16[512,1024]{1,0:T(8,128)(2,1)} async-done(((bf16[2048,1024]{1,0:T(8,128)(2,1)}), bf16[512,1024]{1,0:T(8,128)(2,1)}) %reduce-scatter.16.cloned.1.call-update) | async-done | bytes 1048592 | tf_op jit(solution)/shard_map/reduce_scatter | solution.py:239
  1176.9 104.6 %while.124 = (s32[]{:T(128)}, f32[1,8,64,128]{3,2,1,0:T(8,128)S(1)}, s32[1]{0:T(128)}, f32[8,1,256,8,64]{2,4,3,1,0:T(8,128)}, f32[8,1,8,64,128]{4,3,2,1,0:T(8,12...) while((s32[]{:T(128)}, f32[1,8,64,128]{3,2,1,0:T(8,128)S(1)}, ...), condition=%wide.region_41.43_spmd.clone, body=%wide.region_38.42_spmd.clone.sunk | while | flops 909784064 | bytes 5282777 | solution.py:69
  1349.3 214.6 %while.125 = (s32[]{:T(128)}, f32[8]{0:T(128)S(1)}, f32[1,8,64,128]{3,2,1,0:T(8,128)S(1)}, f32[8,1,256,8,64]{2,4,3,1,0:T(8,128)}, f32[8,1,256,8]{2,3,1,0:T(8,128...) while((s32[]{:T(128)}, f32[8]{0:T(128)S(1)}, ...), condition=%wide.region_57.59_spmd.clone, body=%wide.region_44.58_spmd.clone.sunk | while | flops 2128796672 | bytes 16047004 | solution.py:69
  1618.3 20.3 multiply_reduce_fusion.7
  1681.0 40.9 %all-reduce.52 = (f32[2,4,256]{2,1,0:T(4,128)}, f32[2,256]{1,0:T(2,128)}) all-reduce(f32[2,4,256]{2,1,0:T(4,128)S(1)} %pad_maximum_fusion.17, f32[2,256]{1,0:T(2,128)S(1)} %pad_maximum_fusion.20), channel_id=1, replica_groups=mesh['dp'=8,'tensor'=4] {'dp','tensor'}, use_global_device_ids=true, to_apply=%region_88.90 | all-reduce | flops 2560 | bytes 20480 | tf_op jit(solution)/shard_map/psum | solution.py:278
  1723.2 38.5 %all-reduce.53 = (f32[2,4,512]{2,1,0:T(4,128)}, f32[2,512]{1,0:T(2,128)}, f32[2,8]{1,0:T(2,128)}, f32[2,8]{1,0:T(2,128)}, f32[2,8]{1,0:T(2,128)}, /*index=5*/f32[2,512]{1,0:T(2,128)}) all-reduce(f32[2,4,512]{2,1,0:T(4,128)S(1)} %pad_maximum_fusion.15, ...), channel_id=1, replica_groups=mesh['dp'=8,'tensor'=4] {'dp'}, use_global_device_ids=true, to_apply=%region_76.78 | all-reduce | flops 6192 | bytes 49536 | tf_op jit(solution)/shard_map/psum | solution.py:273
  1763.3 34.2 %reduce-scatter.26.cloned.1.call-done = f32[128,512]{1,0:T(8,128)} async-done(((f32[1024,512]{1,0:T(8,128)}), f32[128,512]{1,0:T(8,128)}) %reduce-scatter.26.cloned.1.call-update) | async-done | bytes 262160 | tf_op jit(solution)/shard_map/reduce_scatter | solution.py:253
  1797.4 70.8 %reduce-scatter.24.cloned.1.call-done = f32[128,512]{1,0:T(8,128)} async-done(((f32[1024,512]{1,0:T(8,128)}), f32[128,512]{1,0:T(8,128)}) %reduce-scatter.24.cloned.1.call-update) | async-done | bytes 262160 | tf_op jit(solution)/shard_map/reduce_scatter | solution.py:253
  1870.1 44.2 %reduce-scatter.18.cloned.1.call-done = bf16[512,1024]{1,0:T(8,128)(2,1)} async-done(((bf16[2048,1024]{1,0:T(8,128)(2,1)}), bf16[512,1024]{1,0:T(8,128)(2,1)}) %reduce-scatter.18.cloned.1.call-update) | async-done | bytes 1048592 | tf_op jit(solution)/shard_map/reduce_scatter | solution.py:239
  1917.4 43.8 %reduce-scatter.14.cloned.1.call-done = bf16[512,1024]{1,0:T(8,128)(2,1)} async-done(((bf16[2048,1024]{1,0:T(8,128)(2,1)}), bf16[512,1024]{1,0:T(8,128)(2,1)}) %reduce-scatter.14.cloned.1.call-update) | async-done | bytes 1048592 | tf_op jit(solution)/shard_map/reduce_scatter | solution.py:184
  1965.7 87.5 %reduce-scatter.22.cloned.1.call-done = f32[128,2,512]{2,0,1:T(8,128)} async-done(((f32[1024,2,512]{2,0,1:T(8,128)}), f32[128,2,512]{2,0,1:T(8,128)}) %reduce-scatter.22.cloned.1.call-update) | async-done | bytes 524304 | tf_op jit(solution)/shard_map/reduce_scatter | solution.py:252
  2053.2 91.2 %reduce-scatter.20.cloned.1.call-done = f32[128,2,512]{2,0,1:T(8,128)} async-done(((f32[1024,2,512]{2,0,1:T(8,128)}), f32[128,2,512]{2,0,1:T(8,128)}) %reduce-scatter.20.cloned.1.call-update) | async-done | bytes 524304 | tf_op jit(solution)/shard_map/reduce_scatter | solution.py:252
  2147.5 132.9 %reduce-scatter.28.cloned.1.call-done = f32[32,2]{1,0:T(8,128)} async-done(((f32[1024,2]{1,0:T(8,128)}), f32[32,2]{1,0:T(8,128)}) %reduce-scatter.28.cloned.1.call-update) | async-done | bytes 272
  (1956 shorter events, 1408.7 us)
Async XLA Ops:
  7.2 64.3 %all-gather.17.cloned.1.call-start = ((), (), s32[]{:S(2)}) async-start(), calls=%async_computation.9 | async-start | bytes 5242880 | tf_op jit(solution)/shard_map/all_gather | solution.py:157
  35.5 84.0 %all-gather.25.cloned.1.call-start = ((), (), s32[]{:S(2)}) async-start(), calls=%async_computation.21 | async-start | bytes 2359296 | tf_op jit(solution)/shard_map/all_gather | solution.py:150
  36.7 254.6 %all-gather.27.cloned.1.call-start = ((), (), s32[]{:S(2)}) async-start(), calls=%async_computation.22 | async-start | bytes 1179648 | tf_op jit(solution)/shard_map/all_gather | solution.py:152
  37.5 304.1 %reduce-scatter.12.cloned.1.call-start = ((), (), s32[]{:S(2)}) async-start(), calls=%async_computation.10 | async-start | bytes 5242880 | tf_op jit(solution)/shard_map/reduce_scatter | solution.py:184
  68.0 375.9 %copy-start.87 = (f32[1,1,512]{2,1,0:T(1,128)}, f32[1,1,512]{2,1,0:T(1,128)S(1)}, u32[]{:S(2)}) copy-start(f32[1,1,512]{2,1,0:T(1,128)S(1)} %get-tuple-element.2105) | copy-start | bytes 6148
  68.0 375.9 %copy-start.89 = (f32[1,1,512]{2,1,0:T(1,128)}, f32[1,1,512]{2,1,0:T(1,128)S(1)}, u32[]{:S(2)}) copy-start(f32[1,1,512]{2,1,0:T(1,128)S(1)} %get-tuple-element.2106) | copy-start | bytes 6148
  68.0 375.9 %copy-start.91 = (f32[1,1,512]{2,1,0:T(1,128)}, f32[1,1,512]{2,1,0:T(1,128)S(1)}, u32[]{:S(2)}) copy-start(f32[1,1,512]{2,1,0:T(1,128)S(1)} %get-tuple-element.2112) | copy-start | bytes 6148
  298.1 82.3 %all-gather.19.cloned.1.call-start = ((), (), s32[]{:S(2)}) async-start(), calls=%async_computation.11 | async-start | bytes 5242880 | tf_op jit(solution)/shard_map/all_gather | solution.py:157
  345.8 86.8 %all-gather.29.cloned.1.call-start = ((), (), s32[]{:S(2)}) async-start(), calls=%async_computation.23 | async-start | bytes 2359296 | tf_op jit(solution)/shard_map/all_gather | solution.py:150
  346.6 403.8 %all-gather.31.cloned.1.call-start = ((), (), s32[]{:S(2)}) async-start(), calls=%async_computation.24 | async-start | bytes 1179648 | tf_op jit(solution)/shard_map/all_gather | solution.py:152
  347.3 403.0 %all-gather.21.cloned.1.call-start = ((), (), s32[]{:S(2)}) async-start(), calls=%async_computation.13 | async-start | bytes 5242880 | tf_op jit(solution)/shard_map/all_gather | solution.py:203
  350.1 818.2 %reduce-scatter.16.cloned.1.call-start = ((), (), s32[]{:S(2)}) async-start(), calls=%async_computation.14 | async-start | bytes 5242880 | tf_op jit(solution)/shard_map/reduce_scatter | solution.py:239
  379.0 391.9 %copy-start.93 = (f32[512]{0:T(512)}, f32[512]{0:T(512)S(1)}, u32[]{:S(2)}) copy-start(f32[512]{0:T(512)S(1)} %mul.2282) | copy-start | bytes 6148
  1125.3 175.4 %all-gather.23.cloned.1.call-start = ((), (), s32[]{:S(2)}) async-start(), calls=%async_computation.15 | async-start | bytes 5242880 | tf_op jit(solution)/shard_map/all_gather | solution.py:203
  1172.8 588.9 %all-reduce.56.cloned.1.call-start = ((), (), s32[]{:S(2)}) async-start(), calls=%async_computation.26 | async-start | bytes 6291456
  1587.2 210.3 %reduce-scatter.26.cloned.1.call-start = ((), (), s32[]{:S(2)}) async-start(), calls=%async_computation.20 | async-start | bytes 2359296 | tf_op jit(solution)/shard_map/reduce_scatter | solution.py:253
  1593.7 274.5 %reduce-scatter.24.cloned.1.call-start = ((), (), s32[]{:S(2)}) async-start(), calls=%async_computation.19 | async-start | bytes 2359296 | tf_op jit(solution)/shard_map/reduce_scatter | solution.py:253
  1618.2 296.1 %reduce-scatter.18.cloned.1.call-start = ((), (), s32[]{:S(2)}) async-start(), calls=%async_computation.16 | async-start | bytes 5242880 | tf_op jit(solution)/shard_map/reduce_scatter | solution.py:239
  1650.2 311.0 %reduce-scatter.14.cloned.1.call-start = ((), (), s32[]{:S(2)}) async-start(), calls=%async_computation.12 | async-start | bytes 5242880 | tf_op jit(solution)/shard_map/reduce_scatter | solution.py:184
  1656.5 396.7 %reduce-scatter.22.cloned.1.call-start = ((), (), s32[]{:S(2)}) async-start(), calls=%async_computation.18 | async-start | bytes 4718592 | tf_op jit(solution)/shard_map/reduce_scatter | solution.py:252
  1667.5 476.9 %reduce-scatter.20.cloned.1.call-start = ((), (), s32[]{:S(2)}) async-start(), calls=%async_computation.17 | async-start | bytes 4718592 | tf_op jit(solution)/shard_map/reduce_scatter | solution.py:252
  1678.6 282.6 %copy-start.18 = (bf16[512,1024]{1,0:T(8,128)(2,1)S(1)}, bf16[512,1024]{1,0:T(8,128)(2,1)}, u32[]{:S(2)}) copy-start(bf16[512,1024]{1,0:T(8,128)(2,1)} %reduce-scatter.12.cloned.1.call-done) | copy-start | bytes 3145732
  1678.6 282.6 %copy-start.66 = (f32[1,1024]{1,0:T(1,128)S(1)}, f32[1,1024]{1,0:T(1,128)}, u32[]{:S(2)}) copy-start(f32[1,1024]{1,0:T(1,128)} %copy-done.64) | copy-start | bytes 12292
  1678.6 601.8 %reduce-scatter.28.cloned.1.call-start = ((), (), s32[]{:S(2)}) async-start(), calls=%async_computation.25 | async-start | bytes 540672
  (188 other events, 3973.9 us)
Sparse Core Ops, SparseCore 0:
  35.6 31.7 all-gather.16
  70.1 49.2 all-gather.24
  121.6 38.6 all-gather.26
  298.2 43.2 reduce-scatter.11
  345.9 34.4 all-gather.18
  383.3 49.2 all-gather.28
  434.9 38.6 all-gather.30
  475.3 33.2 all-gather.20
  1125.5 42.7 reduce-scatter.15
  1172.9 34.4 all-gather.22
  1587.3 138.9 all-reduce.55
  1730.6 66.7 reduce-scatter.25
  1801.4 66.8 reduce-scatter.23
  1870.8 43.4 reduce-scatter.17
  1916.7 44.4 reduce-scatter.13
  1965.1 88.0 reduce-scatter.21
  2056.7 87.6 reduce-scatter.19
  2146.6 133.7 reduce-scatter.27
where the time goes:
time: 2310 us; the launch traced here: 2290 us
  waiting for transfers between devices  645 us (28%)
  matrix products  600 us (26%)
  local copies, waits for them, and re-layouts  464 us (20%)
  other arithmetic  337 us (15%)
  blocking collectives  201 us (9%)
  loops' own time  24.4 us (1%)
    dot_general x64, matrix products, block_step(): output = jnp.einsum('sijh,sjhp->sihp', weighted, block_x, precision=highest)  260 us
    reduce_scatter x2, waiting for transfers between devices, body(): lax.psum_scatter(grad_proj_zx, 'dp', scatter_dimension=0, tiled=True)  179 us
    unnamed x20, waiting for transfers between devices  134 us
    another operation x232, other arithmetic  110 us
    reduce_scatter x2, waiting for transfers between devices, body(): lax.psum_scatter(grad_proj_out, 'dp', scatter_dimension=0, tiled=True)  105 us
    reduce_scatter x2, waiting for transfers between devices, body(): lax.psum_scatter(project_back(jnp.int32(0), local_rows * lax.axis_size('t...  85.3 us
    dot_general x80, matrix products, block_step(): jnp.einsum('sin,shpn->sihp', block_c, state_now, precision=highest)  82.5 us
    dynamic_update_slice x48, local copies, waits for them, and re-layouts, ssd_scan(): lax.scan(jax.checkpoint(block_step), initial, (to_blocks(values), to_bloc...  78.5 us
  transfers between devices with their start and end apart: 18, of which 12 were waited for; matrix products, arithmetic and copies ran while one was open for 32% of the time, Pallas kernels for 0%

commit v1 on v0

v1 whole, which is shorter than its diff:
```python
from functools import partial

import jax
import jax.numpy as jnp
from jax import lax
from jax.experimental import pallas as pl
from jax.experimental.pallas import tpu as pltpu
from jax.sharding import PartitionSpec as P

bf16 = jnp.bfloat16
f32 = jnp.float32
epsilon = 1e-05
SPAN = 256
HALO = 16
LANES = 128
NEG = -1e30
VMEM = 56 * 1024 * 1024


def mm(a, b):
    return lax.dot_general(a, b, (((1,), (0,)), ((), ())), preferred_element_type=f32)


def mmt(a, b):
    return lax.dot_general(a, b, (((1,), (1,)), ((), ())), preferred_element_type=f32)


def mmf(a, b):
    return lax.dot_general(
        a, b, (((1,), (0,)), ((), ())), precision=lax.Precision.HIGHEST, preferred_element_type=f32
    )


def two(x):
    first = low(x)
    return first, low(x - first.astype(f32))


def mm3(a, b):
    a0, a1 = two(a)
    b0, b1 = two(b)
    return mm(a0, b0) + (mm(a0, b1) + mm(a1, b0))


def mmt3(a, b):
    a0, a1 = two(a)
    b0, b1 = two(b)
    return mmt(a0, b0) + (mmt(a0, b1) + mmt(a1, b0))


def iota(shape, axis):
    return lax.broadcasted_iota(jnp.int32, shape, axis)


def low(x):
    return x.astype(bf16)


def three(x):
    first = low(x).astype(f32)
    rest = x - first
    second = low(rest).astype(f32)
    return first, second, rest - second


def split_heads(x, heads):
    first, second, third = three(x)
    part = iota(x.shape, 1) // heads
    zero = jnp.zeros_like(x)
    return low(
        jnp.where(part == 0, first, jnp.where(part == 1, second, jnp.where(part == 2, third, zero)))
    )


def spread(group, heads, own, width):
    row, col = iota((LANES, width), 0), iota((LANES, width), 1)
    return low(
        ((row % heads == group * own + col // (width // own)) & (row < 3 * heads)).astype(f32)
    )


def pick(group, heads, own):
    row, col = iota((LANES, LANES), 0), iota((LANES, LANES), 1)
    return low(((row % heads == group * own + col) & (col < own) & (row < 3 * heads)).astype(f32))


def gather_heads(x, group, own):
    width = x.shape[1]
    row, col = iota((width, LANES), 0), iota((width, LANES), 1)
    fold = low((col == group * own + row // (width // own)).astype(f32))
    first, second, third = three(x)
    return mm(low(first), fold) + mm(low(second), fold) + mm(low(third), fold)


def keeps(segc, rows):
    now = segc[HALO : HALO + rows]
    return [None] + [
        (segc[HALO - j : HALO - j + rows] == now).astype(f32) for j in range(1, 4)
    ]


def conv(ext, taps, keep, rows, count):
    total = taps[count : count + 1] + taps[0:1] * ext[HALO : HALO + rows]
    for j in range(1, count):
        total = total + taps[j : j + 1] * (ext[HALO - j : HALO - j + rows] * keep[j])
    return total


def triangle(rows, lower):
    row, col = iota((rows, rows), 0), iota((rows, rows), 1)
    return ((row >= col) if lower else (row <= col)).astype(f32)


def scan_in_kernel(
    heads,
    own,
    taps_n,
    nrm,
    w,
    wb,
    prm,
    cbc,
    hp,
    segc,
    segr,
    y,
    xin,
    state,
    ftot,
    shared,
    b_out,
    c_out,
    bt_out,
    ct_out,
    dtp_out,
    cumt_out,
    dts_out,
    es_out,
    fs_out,
    fd_out,
    cums_out,
    g_scr,
    m_scr,
):
    group = pl.program_id(0)
    rows = y.shape[0]
    width = y.shape[1]
    chunks = rows // SPAN
    keep = keeps(segc[...], rows)

    @pl.when(group == 0)
    def _():
        sh = mm(nrm[...], wb[...])
        shared[...] = sh
        half = cbc.shape[1] // 2
        act = conv(sh[:, : 2 * half], cbc[...], keep, rows, taps_n)
        act = act * jax.nn.sigmoid(act)
        bmat, cmat = act[:, :half], act[:, half:]
        b_out[...] = bmat
        c_out[...] = cmat
        bt_out[...] = bmat.T
        ct_out[...] = cmat.T
        dtp = sh[HALO:, 2 * half :] + hp[0:1]
        dtp_out[...] = dtp
        dt = jnp.maximum(dtp, 0.0) + jnp.log1p(jnp.exp(-jnp.abs(dtp)))
        cum = mmf(triangle(rows, True), dt * hp[1:2])
        cumt_out[...] = cum.T
        dts_out[...] = split_heads(dt, heads)
        cums_out[...] = split_heads(cum, heads)
        seg = segc[...]
        here = seg[HALO:]
        fd_out[...] = split_heads(
            jnp.exp(cum) * (here == seg[HALO - 1 : HALO]).astype(f32), heads
        )
        for c in range(chunks):
            lo, hi = c * SPAN, (c + 1) * SPAN
            block = cum[lo:hi]
            base = jnp.zeros_like(cum[0:1]) if c == 0 else cum[lo - 1 : lo]
            before = seg[HALO + lo - 1 : HALO + lo]
            last = here[hi - 1 : hi]
            fs_out[lo:hi] = split_heads(
                jnp.exp(block - base) * (here[lo:hi] == before).astype(f32), heads
            )
            es_out[lo:hi] = split_heads(
                jnp.exp(cum[hi - 1 : hi] - block) * (here[lo:hi] == last).astype(f32), heads
            )
            g_scr[c] = mmt3(cmat[lo:hi], bmat[lo:hi])
            ok = (here[lo:hi] == segr[0:1, lo:hi]) & (
                iota((SPAN, SPAN), 0) >= iota((SPAN, SPAN), 1)
            )
            m_scr[c] = jnp.where(ok, 0.0, NEG)

    weight = w[...].reshape(-1, width)
    ext = mm(nrm[...], weight)
    xin[...] = ext
    u = conv(ext, prm[0], keep, rows, taps_n)
    xc = u * jax.nn.sigmoid(u)
    grow = spread(group, heads, own, width)
    xd = xc * mm(dts_out[...], grow)
    xd0, xd1 = two(xd)
    exd = xd * mm(es_out[...], grow)
    fx = mm(fs_out[...], grow)
    cols = mm(cums_out[...], pick(group, heads, own))
    rowsum = cumt_out[pl.ds(pl.multiple_of(group * own, own), own), :]
    per = width // own
    side = iota((SPAN, 2 * per), 1) < per
    now = None
    for c in range(chunks):
        lo, hi = c * SPAN, (c + 1) * SPAN
        m, g = m_scr[c], g_scr[c]
        for pair in range(own // 2):
            at = slice(2 * per * pair, 2 * per * (pair + 1))
            x2 = jnp.concatenate([xd0[lo:hi, at], xd1[lo:hi, at]], axis=1)
            out = []
            for h in (2 * pair, 2 * pair + 1):
                decay = jnp.exp(cols[lo:hi, h : h + 1] - rowsum[h : h + 1, lo:hi] + m)
                both = mm(low(decay * g), x2)
                out.append(both[:, : 2 * per] + both[:, 2 * per :])
            y[lo:hi, at] = (
                jnp.where(side, out[0], out[1]) + prm[0, 6:7, at] * xc[lo:hi, at]
            )
        local = mm3(bt_out[:, lo:hi], exd[lo:hi])
        if c > 0:
            y[lo:hi] += fx[lo:hi] * mm3(c_out[lo:hi], now)
            now = fx[hi - 1 : hi] * now + local
        else:
            now = local
    state[...] = low(now)
    ftot[...] = jnp.broadcast_to(mm(fd_out[...], grow)[rows - 1 : rows], ftot.shape)


def gate_kernel(
    heads,
    own,
    full,
    nrm,
    wz,
    wo,
    y_loc,
    c_in,
    fd,
    s_in,
    prm,
    hid,
    z_out,
    y_out,
    branch,
    grms,
    nxt,
    ss,
):
    group = pl.program_id(0)
    width = y_loc.shape[1]
    z = mm(nrm[HALO:], wz[...].reshape(-1, width))
    y = y_loc[...] + mm(fd[...], spread(group, heads, own, width)) * (
        lambda parts: mm(parts[0], s_in[...]) + mm(parts[1], s_in[...])
    )(two(c_in[...]))
    z_out[...] = z
    y_out[...] = y
    gated = y * (z * jax.nn.sigmoid(z))
    squares = jnp.sum(gated * gated, axis=1, keepdims=True)
    part = mmt(low(gated * prm[0, 5:6]), wo[...].reshape(-1, width))

    @pl.when(group == 0)
    def _():
        ss[...] = jnp.broadcast_to(squares, ss.shape)
        branch[...] = part

    @pl.when(group > 0)
    def _():
        ss[...] += jnp.broadcast_to(squares, ss.shape)
        branch[...] += part

    @pl.when(group == pl.num_programs(0) - 1)
    def _():
        scale = lax.rsqrt(ss[...] / full + epsilon)
        grms[...] = scale
        total = branch[...] * scale[:, 0:1]
        branch[...] = total
        nxt[...] = hid[...] + total


def gate_back_kernel(
    heads,
    own,
    full,
    dbr,
    dbrt,
    branch,
    wo,
    wz,
    z_in,
    y_in,
    grms,
    nrmt,
    ct,
    fd,
    prm,
    g_out,
    g_z,
    dy_out,
    dn,
    dstate,
    g_gain,
    q_scr,
):
    group = pl.program_id(0)
    rows, width = z_in.shape

    @pl.when(group == 0)
    def _():
        inner = jnp.sum(dbr[...].astype(f32) * branch[...], axis=1, keepdims=True)
        q_scr[...] = grms[...] * grms[...] * (inner / full)

    rms = grms[:, 0:1]
    dm = mm(dbr[...], wo[...].reshape(-1, width))
    z, y = z_in[...], y_in[...]
    sg = jax.nn.sigmoid(z)
    sz = z * sg
    gated = y * sz
    scaled = gated * rms
    gain = prm[0, 5:6]
    g_out[...] = low(mm(dbrt[...], low(scaled * gain))).reshape(g_out.shape)
    g_gain[...] = jnp.broadcast_to(jnp.sum(dm * scaled, axis=0, keepdims=True), g_gain.shape)
    dg = rms * (dm * gain) - gated * q_scr[:, 0:1]
    dy = dg * sz
    dy_out[...] = dy
    dz = low(dg * y * (sg + sz * (1.0 - sg)))
    g_z[...] = low(mm(nrmt[:, :rows], dz)).reshape(g_z.shape)
    part = mmt(dz, wz[...].reshape(-1, width))

    @pl.when(group == 0)
    def _():
        dn[...] = part

    @pl.when(group > 0)
    def _():
        dn[...] += part

    dstate[...] = low(mm3(ct[...], mm(fd[...], spread(group, heads, own, width)) * dy))


def conv_back(du, ext, taps, keep, rows, count, dest):
    dest[...] = jnp.zeros_like(dest)
    dest[0:rows] = taps[0:1] * du
    sums = [jnp.sum(du * ext[HALO : HALO + rows], axis=0, keepdims=True)]
    for j in range(1, count):
        kept = du * keep[j]
        sums.append(jnp.sum(kept * ext[HALO - j : HALO - j + rows], axis=0, keepdims=True))
        moved = taps[j : j + 1] * kept
        dest[0 : rows - j] += moved[j:]
        dest[rows + HALO - j : rows + HALO] += moved[:j]
    return sums, jnp.sum(du, axis=0, keepdims=True)


def scan_back_kernel(
    heads,
    own,
    taps_n,
    xin,
    dy_in,
    y_in,
    s_in,
    ds_in,
    w,
    wb,
    prm,
    cbc,
    hp,
    segc,
    segr,
    nrmt,
    shared,
    b_in,
    c_in,
    bt,
    ct,
    dtp,
    cumt,
    dts,
    es,
    fs,
    cums,
    g_x,
    g_b,
    dn,
    g_prm,
    g_cbc,
    g_hp,
    gt_scr,
    mt_scr,
    dgt_scr,
    db_scr,
    dc_scr,
    dcum_scr,
    ddt_scr,
    dx_scr,
    dbc_scr,
    dxc_scr,
):
    group = pl.program_id(0)
    rows, width = dy_in.shape
    chunks = rows // SPAN
    keep = keeps(segc[...], rows)

    @pl.when(group == 0)
    def _():
        here = segc[HALO:]
        for c in range(chunks):
            lo, hi = c * SPAN, (c + 1) * SPAN
            gt_scr[c] = mmt3(b_in[lo:hi], c_in[lo:hi])
            ok = (here[lo:hi] == segr[0:1, lo:hi]) & (
                iota((SPAN, SPAN), 0) <= iota((SPAN, SPAN), 1)
            )
            mt_scr[c] = jnp.where(ok, 0.0, NEG)
        for ref in (dgt_scr, db_scr, dc_scr, dcum_scr, ddt_scr):
            ref[...] = jnp.zeros_like(ref)

    u = conv(xin[...], prm[0], keep, rows, taps_n)
    sg = jax.nn.sigmoid(u)
    xc = u * sg
    grow = spread(group, heads, own, width)
    dtx = mm(dts[...], grow)
    ex = mm(es[...], grow)
    fx = mm(fs[...], grow)
    xd = xc * dtx
    xd0, xd1 = two(xd)
    exd = xd * ex
    cols = mm(cums[...], pick(group, heads, own))
    rowsum = cumt[pl.ds(pl.multiple_of(group * own, own), own), :]
    dy = dy_in[...]
    dyb = low(dy)
    fdy = fx * dy
    skip = prm[0, 6:7]
    per = width // own
    side = iota((SPAN, 2 * per), 1) < per
    wide_side = (iota((SPAN, 4 * per), 1) // per) % 2 == 0
    states = [s_in[...].astype(f32)]
    for c in range(chunks - 1):
        lo, hi = c * SPAN, (c + 1) * SPAN
        states.append(fx[hi - 1 : hi] * states[-1] + mm3(bt[:, lo:hi], exd[lo:hi]))
    ds = ds_in[...].astype(f32)
    for c in reversed(range(chunks)):
        lo, hi = c * SPAN, (c + 1) * SPAN
        dxs = ex[lo:hi] * mm3(b_in[lo:hi], ds)
        db_scr[lo:hi] += mmt3(exd[lo:hi], ds)
        dc_scr[lo:hi] += mmt3(fdy[lo:hi], states[c])
        mt, gt = mt_scr[c], gt_scr[c]
        parts = []
        dgt = None
        for pair in range(own // 2):
            at = slice(2 * per * pair, 2 * per * (pair + 1))
            x2 = jnp.concatenate([xd0[lo:hi, at], xd1[lo:hi, at]], axis=1)
            dy2 = dyb[lo:hi, at]
            dy4 = jnp.concatenate([dy2, dy2], axis=1)
            out = []
            for k, h in enumerate((2 * pair, 2 * pair + 1)):
                decay = jnp.exp(rowsum[h : h + 1, lo:hi] - cols[lo:hi, h : h + 1] + mt)
                out.append(mm(low(decay * gt), dy2))
                mine = wide_side if k == 0 else jnp.logical_not(wide_side)
                dw = mmt(jnp.where(mine, x2, jnp.zeros_like(x2)), dy4) * decay
                dgt = dw if dgt is None else dgt + dw
            parts.append(jnp.where(side, out[0], out[1]))
        dgt_scr[c] += dgt
        dxd = jnp.concatenate(parts, axis=1) + dxs
        xcc = xc[lo:hi]
        xdf = xd[lo:hi]
        scanned = y_in[lo:hi] - skip * xcc
        dcum_scr[lo:hi] += gather_heads(
            dyb[lo:hi].astype(f32) * scanned - xdf * dxd, group, own
        )
        tail = jnp.sum(xdf * dxs, axis=0, keepdims=True) + fx[hi - 1 : hi] * jnp.sum(
            ds * states[c], axis=0, keepdims=True
        )
        tail8 = gather_heads(jnp.broadcast_to(tail, (8, width)), group, own)
        lastrow = (iota((8, LANES), 0) == 7).astype(f32)
        dcum_scr[hi - 8 : hi] += tail8 * lastrow
        ddt_scr[lo:hi] += gather_heads(xcc * dxd, group, own)
        dxc_scr[lo:hi] = dtx[lo:hi] * dxd + skip * dy[lo:hi]
        ds = fx[hi - 1 : hi] * ds + mm3(ct[:, lo:hi], fdy[lo:hi])
    du = dxc_scr[...] * (sg + xc * (1.0 - sg))
    sums, bias = conv_back(du, xin[...], prm[0], keep, rows, taps_n, dx_scr)
    g_skip = jnp.sum(dy * xc, axis=0, keepdims=True)
    for j in range(taps_n):
        g_prm[0, j : j + 1] = sums[j]
    g_prm[0, taps_n : taps_n + 1] = bias
    g_prm[0, 5:6] = jnp.zeros_like(bias)
    g_prm[0, 6:7] = g_skip
    g_prm[0, 7:8] = jnp.zeros_like(bias)
    dxb = low(dx_scr[...])
    g_x[...] = low(mm(nrmt[...], dxb)).reshape(g_x.shape)
    part = mmt(dxb[: rows + HALO], w[...].reshape(-1, width))

    @pl.when(group == 0)
    def _():
        dn[...] = part

    @pl.when(group > 0)
    def _():
        dn[...] += part

    @pl.when(group == pl.num_programs(0) - 1)
    def _():
        half = cbc.shape[1] // 2
        dact = []
        for c in range(chunks):
            lo, hi = c * SPAN, (c + 1) * SPAN
            dgt = dgt_scr[c]
            db_scr[lo:hi] += mm3(dgt, c_in[lo:hi])
            dc_scr[lo:hi] += mm3(dgt.T, b_in[lo:hi])
        sh = shared[:, : 2 * half]
        ubc = conv(sh, cbc[...], keep, rows, taps_n)
        sgb = jax.nn.sigmoid(ubc)
        dact = jnp.concatenate([db_scr[...], dc_scr[...]], axis=1)
        dub = dact * (sgb + ubc * sgb * (1.0 - sgb))
        bsums, bbias = conv_back(dub, sh, cbc[...], keep, rows, taps_n, dbc_scr)
        for j in range(taps_n):
            g_cbc[j : j + 1] = bsums[j]
        g_cbc[taps_n : taps_n + 1] = bbias
        g_cbc[taps_n + 1 :] = jnp.zeros_like(g_cbc[taps_n + 1 :])
        raw = dtp[...]
        dt = jnp.maximum(raw, 0.0) + jnp.log1p(jnp.exp(-jnp.abs(raw)))
        upper = triangle(SPAN, False)
        for c in range(chunks):
            lo, hi = c * SPAN, (c + 1) * SPAN
            dcum_scr[lo:hi] = mmf(upper, dcum_scr[lo:hi])
        da = dcum_scr[...]
        rate = hp[1:2]
        first = iota((rows, LANES), 1) < heads
        ddtp = jnp.where(first, (rate * da + ddt_scr[...]) * jax.nn.sigmoid(raw), 0.0)
        g_hp[...] = jnp.zeros_like(g_hp)
        g_hp[0:1] = jnp.sum(ddtp, axis=0, keepdims=True)
        g_hp[1:2] = jnp.sum(jnp.where(first, da * dt * rate, 0.0), axis=0, keepdims=True)
        dsh = low(
            jnp.concatenate(
                [dbc_scr[...], jnp.concatenate([ddtp, jnp.zeros((LANES, LANES), f32)], axis=0)],
                axis=1,
            )
        )
        g_b[...] = mm(nrmt[...], dsh)
        dn[...] += mmt(dsh[: rows + HALO], wb[...])


def whole(shape):
    return pl.BlockSpec(shape, lambda g: (0,) * len(shape))


def by_column(rows, width):
    return pl.BlockSpec((rows, width), lambda g: (0, g))


def kind_block(weights, kind):
    shape = weights.shape
    return pl.BlockSpec((None, shape[1], None, shape[3], shape[4]), lambda g: (g, 0, kind, 0, 0))


def params(flops, moved):
    return dict(
        compiler_params=pltpu.CompilerParams(vmem_limit_bytes=VMEM),
        cost_estimate=pl.CostEstimate(flops=flops, bytes_accessed=moved, transcendentals=0),
    )


def struct(*shape, dtype=f32):
    return jax.ShapeDtypeStruct(shape, dtype)


def shift(x, axis, step):
    size = lax.axis_size(axis)
    return lax.ppermute(
        x, axis, [(i, i + step) for i in range(size) if 0 <= i + step < size]
    )


def bits_of(axis):
    return [(axis, b) for b in range(lax.axis_size(axis).bit_length() - 1)]


def exchange(x, axis, bit):
    return lax.ppermute(x, axis, [(i, i ^ (1 << bit)) for i in range(lax.axis_size(axis))])


def all_sum(x, order):
    for axis, bit in order:
        x = x + exchange(x, axis, bit)
    return x


def scatter_sum(x, axes, order, kind):
    names = [pair for axis in axes for pair in reversed(bits_of(axis))]
    x = x.reshape((2,) * len(names) + x.shape[len(axes) :])
    for n, (axis, bit) in enumerate(order):
        dim = names.index((axis, bit))
        mine = (lax.axis_index(axis) >> bit) & 1
        got = exchange(lax.dynamic_index_in_dim(x, 1 - mine, dim, False), axis, bit)
        x = lax.dynamic_index_in_dim(x, mine, dim, False).astype(f32) + got.astype(f32)
        if n + 1 < len(order):
            x = x.astype(kind)
        names.pop(dim)
    return x


def carry_states(state, factor, axis, backward):
    size, at = lax.axis_size(axis), lax.axis_index(axis)
    total = state.astype(f32)
    prefix = jnp.zeros_like(total)
    prefix_factor = jnp.ones_like(factor)
    step = 1
    while step < size:
        first = low(factor)
        second = low(factor - first.astype(f32))
        packed = jnp.concatenate(
            [low(total), first, second, jnp.zeros((14, factor.shape[1]), bf16)], axis=0
        )
        upper = ((at // step) % 2) == 1
        follows = jnp.logical_not(upper) if backward else upper
        pairs = [(i, i ^ step) for i in range(size)]
        final = 2 * step >= size
        if final:
            pairs = [p for p in pairs if (p[0] > p[1]) == backward]
        got = lax.ppermute(packed, axis, pairs)
        other = got[: state.shape[0]].astype(f32)
        other_factor = got[state.shape[0] : state.shape[0] + 1].astype(f32) + got[
            state.shape[0] + 1 : state.shape[0] + 2
        ].astype(f32)
        prefix = jnp.where(follows, prefix_factor * other + prefix, prefix)
        if not final:
            prefix_factor = jnp.where(follows, prefix_factor * other_factor, prefix_factor)
            total = jnp.where(follows, factor * other + total, other_factor * total + other)
            factor = factor * other_factor
        step *= 2
    return low(prefix)


def body(
    hidden,
    segment_ids,
    in_gain,
    w_zx,
    w_bcdt,
    w_out,
    conv_x,
    conv_x_bias,
    conv_bc,
    conv_bc_bias,
    dt_bias,
    a_log,
    d_skip,
    out_gain,
    cotangent,
):
    layers, taps_n = conv_x.shape[0], conv_x.shape[1]
    groups, shards = lax.axis_size("tensor"), lax.axis_size("dp")
    at_t = lax.axis_index("tensor")
    at_d = lax.axis_index("dp")
    own = dt_bias.shape[1]
    heads = own * groups
    width = out_gain.shape[1]
    full = width * groups
    rows, model = hidden.shape
    bc = conv_bc.shape[2]
    state_n = bc // 2
    depth = w_zx.shape[1]
    ext = rows + HALO
    chunks = rows // SPAN
    wide = bc + LANES
    copies = LANES // heads

    padded = jnp.pad(segment_ids.reshape(-1), (HALO, 0), constant_values=-1)
    seg = lax.dynamic_slice_in_dim(padded, at_t * rows, ext).astype(f32)
    segc = seg[:, None]
    segr = jnp.broadcast_to(seg[None, HALO:], (8, rows))

    heads_row = jnp.pad(
        jnp.concatenate([dt_bias, a_log, d_skip], axis=1), ((0, 0), (0, width - 3 * own))
    )
    pack = jnp.concatenate(
        [
            conv_x,
            conv_x_bias[:, None],
            out_gain[:, None],
            heads_row[:, None],
            jnp.zeros((layers, 1, width), f32),
        ],
        axis=1,
    )
    prm = lax.all_gather(pack, "tensor", axis=0, tiled=False)
    by_head = prm[:, :, 6]
    dtb = jnp.moveaxis(by_head[:, :, :own], 0, 1).reshape(layers, heads)
    alog = jnp.moveaxis(by_head[:, :, own : 2 * own], 0, 1).reshape(layers, heads)
    skip_ch = jnp.repeat(by_head[:, :, 2 * own : 3 * own], width // own, axis=2)
    prm = jnp.concatenate([prm[:, :, :6], skip_ch[:, :, None], prm[:, :, 7:]], axis=2)
    rate = -jnp.exp(alog)
    hp = jnp.concatenate(
        [
            jnp.tile(dtb, (1, copies))[:, None],
            jnp.tile(rate, (1, copies))[:, None],
            jnp.zeros((layers, 6, LANES), f32),
        ],
        axis=1,
    )
    cbc = jnp.concatenate(
        [conv_bc, conv_bc_bias[:, None], jnp.zeros((layers, 3, bc), f32)], axis=1
    )

    gains = lax.all_gather(in_gain, "dp", axis=1, tiled=True).astype(f32)
    weights, wbs = [], []
    for i in range(layers):
        local = jnp.concatenate(
            [jnp.moveaxis(w_zx[i], 1, 0), w_out[i][None]], axis=0
        )
        got = lax.all_gather(local, ("tensor", "dp"), axis=0, tiled=False)
        weights.append(got.reshape(groups, shards, 3, depth, width))
        wb = lax.all_gather(w_bcdt[i], "dp", axis=0, tiled=True)
        wbs.append(jnp.concatenate([wb[:, :bc], jnp.tile(wb[:, bc:], (1, copies))], axis=1))

    small = [
        ((ext, wide), f32),
        ((rows, state_n), f32),
        ((rows, state_n), f32),
        ((state_n, rows), f32),
        ((state_n, rows), f32),
        ((rows, LANES), f32),
        ((LANES, rows), f32),
        ((rows, LANES), bf16),
        ((rows, LANES), bf16),
        ((rows, LANES), bf16),
        ((rows, LANES), bf16),
        ((rows, LANES), bf16),
    ]
    prm_spec = pl.BlockSpec((1, 8, width), lambda g: (g, 0, 0))
    saved = []
    stream = hidden
    for i in range(layers):
        rinv = lax.rsqrt(jnp.mean(stream * stream, axis=-1, keepdims=True) + epsilon)
        normed = (stream * rinv * gains[i]).astype(bf16)
        before = shift(normed[rows - HALO :], "tensor", 1)
        nrm = jnp.concatenate([before, normed], axis=0)
        nrmt = jnp.concatenate(
            [normed, before, jnp.zeros((LANES - HALO, model), bf16)], axis=0
        ).T
        w, wb, pr = weights[i], wbs[i], prm[:, i]
        flops = 2 * ext * model * (full + wide)
        outs = pl.pallas_call(
            partial(scan_in_kernel, heads, own, taps_n),
            grid=(groups,),
            in_specs=[
                whole((ext, model)),
                kind_block(w, 1),
                whole((model, wide)),
                prm_spec,
                whole((8, bc)),
                whole((8, LANES)),
                whole((ext, 1)),
                whole((8, rows)),
            ],
            out_specs=[
                by_column(rows, width),
                by_column(ext, width),
                by_column(state_n, width),
                by_column(8, width),
            ]
            + [whole(s) for s, _ in small],
            out_shape=[
                struct(rows, full),
                struct(ext, full),
                struct(state_n, full, dtype=bf16),
                struct(8, full),
            ]
            + [struct(*s, dtype=d) for s, d in small],
            scratch_shapes=[
                pltpu.VMEM((chunks, SPAN, SPAN), f32),
                pltpu.VMEM((chunks, SPAN, SPAN), f32),
            ],
            name="scan_in",
            **params(3 * flops, 4 * rows * full * 3),
        )(nrm, w, wb, pr, cbc[i], hp[i], segc, segr)
        y_loc, xin, state, ftot = outs[:4]
        rest = outs[4:]
        shared, b_m, c_m, b_t, c_t, dtp, cumt, dts, es, fs, fd, cums = rest
        s_in = carry_states(state, ftot[0:1], "tensor", False)
        z, y, branch, grms, nxt = pl.pallas_call(
            partial(gate_kernel, heads, own, full),
            grid=(groups,),
            in_specs=[
                whole((ext, model)),
                kind_block(w, 0),
                kind_block(w, 2),
                by_column(rows, width),
                whole((rows, state_n)),
                whole((rows, LANES)),
                by_column(state_n, width),
                prm_spec,
                whole((rows, model)),
            ],
            out_specs=[
                by_column(rows, width),
                by_column(rows, width),
                whole((rows, model)),
                whole((rows, LANES)),
                whole((rows, model)),
            ],
            out_shape=[
                struct(rows, full),
                struct(rows, full),
                struct(rows, model),
                struct(rows, LANES),
                struct(rows, model),
            ],
            scratch_shapes=[pltpu.VMEM((rows, LANES), f32)],
            name="gate",
            **params(4 * rows * model * full, 4 * rows * full * 5),
        )(nrm, w, w, y_loc, c_m, fd, s_in, pr, stream)
        saved.append((stream, rinv, nrmt, xin, ftot, rest, s_in, z, y, branch, grms))
        stream = nxt

    grad = cotangent
    big, shared_grads, gain_grads, prm_grads, cbc_grads, hp_grads = [], [], [], [], [], []
    in_gain_grads = []
    tb, db = bits_of("tensor"), bits_of("dp")
    order_x = tb + db
    order_y = tb[:1] + db[:1] + tb[1:] + db[1:]
    for i in reversed(range(layers)):
        stream_in, rinv, nrmt, xin, ftot, rest, s_in, z, y, branch, grms = saved[i]
        shared, b_m, c_m, b_t, c_t, dtp, cumt, dts, es, fs, fd, cums = rest
        w, wb, pr = weights[i], wbs[i], prm[:, i]
        dbr = grad.astype(bf16)
        grad_block = pl.BlockSpec((None, shards, depth, width), lambda g: (g, 0, 0, 0))
        grad_shape = struct(groups, shards, depth, width, dtype=bf16)
        g_out, g_z, dy, dnz, dstate, g_gain = pl.pallas_call(
            partial(gate_back_kernel, heads, own, full),
            grid=(groups,),
            in_specs=[
                whole((rows, model)),
                whole((model, rows)),
                whole((rows, model)),
                kind_block(w, 2),
                kind_block(w, 0),
                by_column(rows, width),
                by_column(rows, width),
                whole((rows, LANES)),
                whole((model, rows + LANES)),
                whole((state_n, rows)),
                whole((rows, LANES)),
                prm_spec,
            ],
            out_specs=[
                grad_block,
                grad_block,
                by_column(rows, width),
                whole((rows, model)),
                by_column(state_n, width),
                by_column(8, width),
            ],
            out_shape=[
                grad_shape,
                grad_shape,
                struct(rows, full),
                struct(rows, model),
                struct(state_n, full, dtype=bf16),
                struct(8, full),
            ],
            scratch_shapes=[pltpu.VMEM((rows, LANES), f32)],
            name="gate_back",
            **params(8 * rows * model * full, 4 * rows * full * 6),
        )(dbr, dbr.T, branch, w, w, z, y, grms, nrmt, c_t, fd, pr)
        ds_in = carry_states(dstate, ftot[0:1], "tensor", True)
        g_x, g_b, dn, g_prm, g_cbc, g_hp = pl.pallas_call(
            partial(scan_back_kernel, heads, own, taps_n),
            grid=(groups,),
            in_specs=[
                by_column(ext, width),
                by_column(rows, width),
                by_column(rows, width),
                by_column(state_n, width),
                by_column(state_n, width),
                kind_block(w, 1),
                whole((model, wide)),
                prm_spec,
                whole((8, bc)),
                whole((8, LANES)),
                whole((ext, 1)),
                whole((8, rows)),
                whole((model, rows + LANES)),
            ]
            + [whole(s) for n, (s, _) in enumerate(small) if n != 10],
            out_specs=[
                grad_block,
                whole((model, wide)),
                whole((ext, model)),
                pl.BlockSpec((1, 8, width), lambda g: (g, 0, 0)),
                whole((8, bc)),
                whole((8, LANES)),
            ],
            out_shape=[
                grad_shape,
                struct(model, wide),
                struct(ext, model),
                struct(groups, 8, width),
                struct(8, bc),
                struct(8, LANES),
            ],
            scratch_shapes=[
                pltpu.VMEM((chunks, SPAN, SPAN), f32),
                pltpu.VMEM((chunks, SPAN, SPAN), f32),
                pltpu.VMEM((chunks, SPAN, SPAN), f32),
                pltpu.VMEM((rows, state_n), f32),
                pltpu.VMEM((rows, state_n), f32),
                pltpu.VMEM((rows, LANES), f32),
                pltpu.VMEM((rows, LANES), f32),
                pltpu.VMEM((rows + LANES, width), f32),
                pltpu.VMEM((rows + LANES, bc), f32),
                pltpu.VMEM((rows, width), f32),
            ],
            name="scan_back",
            **params(8 * rows * model * full, 4 * rows * full * 6),
        )(
            xin, dy, y, s_in, ds_in, w, wb, pr, cbc[i], hp[i], segc, segr, nrmt,
            shared, b_m, c_m, b_t, c_t, dtp, cumt, dts, es, fs, cums,
        )
        after = shift(dn[rows:], "tensor", -1)
        dnormed = dnz + dn[:rows]
        dnormed = jnp.concatenate(
            [dnormed[: rows - HALO], dnormed[rows - HALO :] + after], axis=0
        )
        scaled_in = stream_in * rinv
        gain_grads.append(jnp.sum(dnormed * scaled_in, axis=0))
        scaled = dnormed * gains[i]
        grad = grad + rinv * (
            scaled - scaled_in * jnp.mean(scaled * scaled_in, axis=-1, keepdims=True)
        )

        rows_b = depth // groups
        parts_b = jnp.pad(
            low(g_b[:, : bc + heads]), ((0, 0), (0, wide - bc - heads))
        ).reshape(shards, groups, rows_b * wide // width, width)
        with_b = jnp.concatenate([g_x, jnp.moveaxis(parts_b, 1, 0)], axis=2)
        half = width // 2
        left = scatter_sum(with_b[..., :half], ("tensor", "dp"), order_x, bf16)
        right = scatter_sum(with_b[..., half:], ("tensor", "dp"), order_y, bf16)
        with_b = jnp.concatenate([left, right], axis=1)
        big.append(
            (
                scatter_sum(g_z, ("tensor", "dp"), order_x, bf16),
                with_b[:depth],
                scatter_sum(g_out, ("tensor", "dp"), order_y, bf16),
            )
        )
        shared_grads.append(with_b[depth:].reshape(rows_b, wide)[:, : bc + heads])
        g_prm = g_prm.at[:, 5].set(g_gain[0].reshape(groups, width))
        g_prm = scatter_sum(g_prm, ("tensor",), bits_of("tensor"), f32)
        rest_sum = jnp.concatenate([gain_grads[-1], g_cbc.reshape(-1), g_hp.reshape(-1)])
        rest_sum = all_sum(rest_sum.reshape(-1, width), bits_of("tensor"))
        rest_sum = all_sum(jnp.concatenate([g_prm, rest_sum], axis=0), bits_of("dp"))
        prm_grads.append(rest_sum[:8])
        rest_sum = rest_sum[8:].reshape(-1)
        gain_all = rest_sum[:model]
        cbc_grads.append(rest_sum[model : model + 8 * bc].reshape(8, bc))
        hp_grads.append(rest_sum[model + 8 * bc :].reshape(8, LANES))
        per = model // (groups * shards)
        in_gain_grads.append(
            lax.dynamic_slice_in_dim(gain_all, (at_d * groups + at_t) * per, per, 0)
        )

    def stacked(items):
        return jnp.stack(items[::-1], axis=0)

    grad_w_zx = jnp.stack([stacked([b[0] for b in big]), stacked([b[1] for b in big])], axis=2)
    grad_w_out = stacked([b[2] for b in big])
    grad_w_bcdt = stacked(shared_grads)
    grad_in_gain = stacked(in_gain_grads)
    mine = stacked(prm_grads)
    cbc_all = stacked(cbc_grads)
    hp_all = stacked(hp_grads)
    heads_mine = lax.dynamic_slice_in_dim(hp_all, at_t * own, own, 2)
    return (
        stream,
        grad,
        grad_in_gain,
        grad_w_zx,
        grad_w_bcdt,
        grad_w_out,
        mine[:, :taps_n],
        mine[:, taps_n],
        cbc_all[:, :taps_n],
        cbc_all[:, taps_n],
        heads_mine[:, 0],
        heads_mine[:, 1],
        mine[:, 6].reshape(layers, own, width // own).sum(axis=-1),
        mine[:, 5],
    )


def solution(mesh):
    placed = (
        P(("dp", "tensor"), None),
        P("dp", None),
        P(None, "dp"),
        P(None, "dp", None, "tensor"),
        P(None, "dp", None),
        P(None, "dp", "tensor"),
        P(None, None, "tensor"),
        P(None, "tensor"),
        P(),
        P(),
        P(None, "tensor"),
        P(None, "tensor"),
        P(None, "tensor"),
        P(None, "tensor"),
        P(("dp", "tensor"), None),
    )
    return jax.shard_map(
        body,
        mesh=mesh,
        in_specs=placed,
        out_specs=(
            P(("dp", "tensor"), None),
            P(("dp", "tensor"), None),
            P(None, ("dp", "tensor")),
            P(None, "dp", None, "tensor"),
            P(None, ("dp", "tensor"), None),
            P(None, "dp", "tensor"),
            P(None, None, "tensor"),
            P(None, "tensor"),
            P(),
            P(),
            P(None, "tensor"),
            P(None, "tensor"),
            P(None, "tensor"),
            P(None, "tensor"),
        ),
        check_vma=False,
    )
```

time: 2310 us -> 841 us (0.36)
  matrix products: 600 us -> 0 us
  waiting for transfers between devices: 645 us -> 212 us
  local copies, waits for them, and re-layouts: 464 us -> 120 us
  other arithmetic: 337 us -> 98.1 us
  Pallas kernels: 0 us -> 212 us
  blocking collectives: 201 us -> 97.3 us
  starting transfers between devices: 1.32 us -> 74.5 us
  loops' own time: 24.4 us -> 0 us
    dot_general x306 -> x0, matrix products: 600 us -> none  [the longest x64 260 us: block_step(): output = jnp.einsum('sijh,sjhp->sihp', weighted, block_x, precision=highest)]
    reduce_scatter x8 -> x0, waiting for transfers between devices: 436 us -> none  [the longest x2 179 us: body(): lax.psum_scatter(grad_proj_zx, 'dp', scatter_dimension=0, tiled=True)]
    pallas_call x0 -> x8, Pallas kernels: none -> 212 us  [the longest x2 94.6 us: body(): pl.pallas_call(partial(scan_back_kernel, heads, own, taps_n), grid=(group...]
    ppermute x0 -> x66, waiting for transfers between devices: none -> 207 us  [the longest x54 168 us: exchange(): lax.ppermute(x, axis, [(i, i ^ 1 << bit) for i in range(lax.axis_size(axi...]
    unnamed x20 -> x2, waiting for transfers between devices: 134 us -> 0.03 us
    another operation x248 -> x3, other arithmetic: 110 us -> 1.09 us  [body(): jnp.stack([stacked([b[0] for b in big]), stacked([b[1] for b in big])], a...]
    psum x6 -> x0, blocking collectives: 103 us -> none  [the longest x1 40.9 us: body(): lax.psum((conv_bc_part, conv_bcb_part), ('dp', 'tensor'))]
    dynamic_update_slice x48 -> x0, local copies, waits for them, and re-layouts: 78.5 us -> none  [ssd_scan(): lax.scan(jax.checkpoint(block_step), initial, (to_blocks(values), to_bloc...]
  transfers between devices with their start and end apart: 18 -> 68, of which waited for: 12 -> 32; matrix products, arithmetic and copies ran while one was open for 32% -> 22% of each run, Pallas kernels for 0% -> 13%
where the time goes in v1:
time: 841 us; the launch traced here: 829 us
  waiting for transfers between devices  212 us (25%)
  Pallas kernels  212 us (25%)
  local copies, waits for them, and re-layouts  120 us (14%)
  other arithmetic  98.1 us (12%)
  blocking collectives  97.3 us (12%)
  starting transfers between devices  74.5 us (9%)
  between operations  16 us (2%)
    ppermute x54, waiting for transfers between devices, exchange(): lax.ppermute(x, axis, [(i, i ^ 1 << bit) for i in range(lax.axis_size(axi...  168 us
    pallas_call x2, Pallas kernels, body(): pl.pallas_call(partial(scan_back_kernel, heads, own, taps_n), grid=(group...  94.6 us
    all_gather x2, blocking collectives, body(): wb = lax.all_gather(w_bcdt[i], 'dp', axis=0, tiled=True)  68.6 us
    ppermute x54, starting transfers between devices, exchange(): lax.ppermute(x, axis, [(i, i ^ 1 << bit) for i in range(lax.axis_size(axi...  56.6 us
    pallas_call x2, Pallas kernels, body(): pl.pallas_call(partial(scan_in_kernel, heads, own, taps_n), grid=(groups,...  45.3 us
    pallas_call x2, Pallas kernels, body(): pl.pallas_call(partial(gate_back_kernel, heads, own, full), grid=(groups,...  41.9 us
    ppermute x8, waiting for transfers between devices, carry_states(): got = lax.ppermute(packed, axis, pairs)  37.8 us
    pallas_call x2, Pallas kernels, body(): pl.pallas_call(partial(gate_kernel, heads, own, full), grid=(groups,), in...  30.3 us
  transfers between devices with their start and end apart: 68, of which 32 were waited for; matrix products, arithmetic and copies ran while one was open for 22% of the time, Pallas kernels for 13%

profile of v1, /device:TPU:0, one launch (start us, length us, event | category | flops | bytes accessed | tf_op | source)
XLA Modules:
  0.0 829.4 jit_solution(1838178287677677029)
XLA Ops:
  13.3 22.3 %all_gather.27 = bf16[2,1024]{1,0:T(2,128)(2,1)S(1)} all-gather(bf16[2,128]{1,0:T(2,128)(2,1)S(1)} %copy-done.52), channel_id=1, replica_groups=mesh['dp'=8,'tensor'=4] {'dp'}, dimensions={1}, use_global_device_ids=true | all-gather | bytes 4608 | tf_op jit(solution)/shard_map/all_gather | solution.py:706
  42.0 34.6 %all-gather.1 = bf16[1,1024,288]{2,1,0:T(8,128)(2,1)S(1)} all-gather(bf16[1,128,288]{2,1,0:T(8,128)(2,1)S(1)} %copy.201), channel_id=3, replica_groups=mesh['dp'=8,'tensor'=4] {'dp'}, dimensions={1}, use_global_device_ids=true | all-gather | bytes 663552 | tf_op jit(solution)/shard_map/all_gather | solution.py:714
  82.5 6.4 all-gather.2
  109.8 5.0 all-gather.8.cloned.1.call-done
  115.4 22.7 %scan_in.2 = (f32[512,2048]{1,0:T(8,128)}, f32[528,2048]{1,0:T(8,128)}, bf16[128,2048]{1,0:T(8,128)(2,1)}, f32[8,2048]{1,0:T(8,128)}, f32[528,384]{1,0:T(8,128)}...) custom-call(bf16[528,1024]{1,0:T(8,128)(2,1)} %copy.152.nrm, ...), custom_call_target="tpu_custom_call" | custom-call | flops 7889485824 | bytes 12582912 | tf_op jit(solution)/shard_map/scan_in/pallas_call | solution.py:744
  152.9 33.9 %all-gather.4 = bf16[1,1024,288]{2,1,0:T(8,128)(2,1)S(1)} all-gather(bf16[1,128,288]{2,1,0:T(8,128)(2,1)S(1)} %copy.205), channel_id=6, replica_groups=mesh['dp'=8,'tensor'=4] {'dp'}, dimensions={1}, use_global_device_ids=true | all-gather | bytes 663552 | tf_op jit(solution)/shard_map/all_gather | solution.py:714
  194.2 15.2 %gate.2 = (f32[512,2048]{1,0:T(8,128)}, f32[512,2048]{1,0:T(8,128)}, f32[512,1024]{1,0:T(8,128)}, f32[512,128]{1,0:T(8,128)}, f32[512,1024]{1,0:T(8,128)}) custom-call(bf16[528,1024]{1,0:T(8,128)(2,1)} %copy.152.nrm, bf16[4,8,3,128,512]{4,3,2,1,0:T(8,128)(2,1)} %bitcast.375, bf16[4,8,3,128,512]{4,3,2,1,0:T(8,128)(2,1)} %bitcast.376, ...), custom_call_target="tpu_custom_call" | custom-call | flops 4294967296 | bytes 20971520 | tf_op jit(solution)/shard_map/gate/pallas_call | solution.py:782
  222.7 22.7 %scan_in.3 = (f32[512,2048]{1,0:T(8,128)}, f32[528,2048]{1,0:T(8,128)}, bf16[128,2048]{1,0:T(8,128)(2,1)}, f32[8,2048]{1,0:T(8,128)}, f32[528,384]{1,0:T(8,128)}...) custom-call(bf16[528,1024]{1,0:T(8,128)(2,1)} %copy.160.nrm, ...), custom_call_target="tpu_custom_call" | custom-call | flops 7889485824 | bytes 12582912 | tf_op jit(solution)/shard_map/scan_in/pallas_call | solution.py:744
  269.3 9.6 %collective-permute-done.5 = bf16[144,2048]{1,0:T(8,128)(2,1)S(1)} collective-permute-done((bf16[144,2048]{1,0:T(8,128)(2,1)S(1)}, bf16[144,2048]{1,0:T(8,128)(2,1)S(1)}, u32[]{:S(2)}, u32[]{:S(2)}) %collective-permute-start.5) | collective-permute-done | bytes 589856 | tf_op jit(solution)/shard_map/ppermute | solution.py:621
  281.0 15.1 %gate.3 = (f32[512,2048]{1,0:T(8,128)}, f32[512,2048]{1,0:T(8,128)}, f32[512,1024]{1,0:T(8,128)}, f32[512,128]{1,0:T(8,128)}, f32[512,1024]{1,0:T(8,128)}) custom-call(bf16[528,1024]{1,0:T(8,128)(2,1)} %copy.160.nrm, bf16[4,8,3,128,512]{4,3,2,1,0:T(8,128)(2,1)} %bitcast.381, bf16[4,8,3,128,512]{4,3,2,1,0:T(8,128)(2,1)} %bitcast.382, ...), custom_call_target="tpu_custom_call" | custom-call | flops 4294967296 | bytes 20971520 | tf_op jit(solution)/shard_map/gate/pallas_call | solution.py:782
  296.2 20.9 %gate_back.2 = (bf16[4,8,128,512]{3,2,1,0:T(8,128)(2,1)}, bf16[4,8,128,512]{3,2,1,0:T(8,128)(2,1)}, f32[512,2048]{1,0:T(8,128)}, f32[512,1024]{1,0:T(8,128)}, bf...) custom-call(bf16[512,1024]{1,0:T(8,128)(2,1)} %copy.162.dbr, bf16[1024,512]{1,0:T(8,128)(2,1)} %convert_bitcast_fusion.dbrt, ...), custom_call_target="tpu_custom_call" | custom-call | flops 8589934592 | bytes 25165824 | tf_op jit(solution)/shard_map/gate_back/pallas_call | solution.py:830
  324.9 15.3 %collective-permute-done.7 = bf16[144,2048]{1,0:T(8,128)(2,1)} collective-permute-done((bf16[144,2048]{1,0:T(8,128)(2,1)S(1)}, bf16[144,2048]{1,0:T(8,128)(2,1)}, u32[]{:S(2)}, u32[]{:S(2)}) %collective-permute-start.7) | collective-permute-done | bytes 589856 | tf_op jit(solution)/shard_map/ppermute | solution.py:621
  342.3 47.1 %scan_back.2 = (bf16[4,8,128,512]{3,2,1,0:T(8,128)(2,1)}, f32[1024,384]{1,0:T(8,128)}, f32[528,1024]{1,0:T(8,128)}, f32[4,8,512]{2,1,0:T(8,128)}, f32[8,256]{1,0:T(8,128)}, /*index=5*/f32[8,128]{1,0:T(8,128)}) custom-call(f32[528,2048]{1,0:T(8,128)} %get-tuple-element.122.xin, f32[512,2048]{1,0:T(8,128)} %get-tuple-element.123.dy_in, ...), custom_call_target="tpu_custom_call" | custom-call | flops 8589934592 | bytes 25165824 | tf_op jit(solution)/shard_map/scan_back/pallas_call | solution.py:868
  415.5 20.9 %gate_back.3 = (bf16[4,8,128,512]{3,2,1,0:T(8,128)(2,1)}, bf16[4,8,128,512]{3,2,1,0:T(8,128)(2,1)}, f32[512,2048]{1,0:T(8,128)}, f32[512,1024]{1,0:T(8,128)}, bf...) custom-call(bf16[512,1024]{1,0:T(8,128)(2,1)} %copy.168.dbr, bf16[1024,512]{1,0:T(8,128)(2,1)} %bitcast.394, ...), custom_call_target="tpu_custom_call" | custom-call | flops 8589934592 | bytes 25165824 | tf_op jit(solution)/shard_map/gate_back/pallas_call | solution.py:830
  444.3 7.0 constant_dynamic-slice_fusion.15
  471.5 8.8 %collective-permute-done.10 = bf16[144,2048]{1,0:T(8,128)(2,1)} collective-permute-done((bf16[144,2048]{1,0:T(8,128)(2,1)S(1)}, bf16[144,2048]{1,0:T(8,128)(2,1)}, u32[]{:S(2)}, u32[]{:S(2)}) %collective-permute-start.10) | collective-permute-done | bytes 589856 | tf_op jit(solution)/shard_map/ppermute | solution.py:621
  482.4 47.4 %scan_back.3 = (bf16[4,8,128,512]{3,2,1,0:T(8,128)(2,1)}, f32[1024,384]{1,0:T(8,128)}, f32[528,1024]{1,0:T(8,128)}, f32[4,8,512]{2,1,0:T(8,128)}, f32[8,256]{1,0:T(8,128)}, /*index=5*/f32[8,128]{1,0:T(8,128)}) custom-call(f32[528,2048]{1,0:T(8,128)} %get-tuple-element.141.xin, f32[512,2048]{1,0:T(8,128)} %get-tuple-element.142.dy_in, ...), custom_call_target="tpu_custom_call" | custom-call | flops 8589934592 | bytes 25165824 | tf_op jit(solution)/shard_map/scan_back/pallas_call | solution.py:868
  611.5 50.8 %collective-permute-done.47 = bf16[2,2,2,152,256]{4,3,0,1,2:T(8,128)(2,1)S(1)} collective-permute-done((bf16[2,2,2,152,256]{4,3,0,1,2:T(8,128)(2,1)S(1)}, bf16[2,2,2,152,256]{4,3,0,1,2:T(8,128)(2,1)S(1)}, u32[]{:S(2)}, u32[]{:S(2)}) %collective-permute-start.47) | collective-permute-done | bytes 622624 | tf_op jit(solution)/shard_map/ppermute | solution.py:580
  662.7 12.5 %collective-permute-done.37 = bf16[2,2,2,152,256]{4,3,0,1,2:T(8,128)(2,1)S(1)} collective-permute-done((bf16[2,2,2,152,256]{4,3,0,1,2:T(8,128)(2,1)S(1)}, bf16[2,2,2,152,256]{4,3,0,1,2:T(8,128)(2,1)S(1)}, u32[]{:S(2)}, u32[]{:S(2)}) %collective-permute-start.37) | collective-permute-done | bytes 622624 | tf_op jit(solution)/shard_map/ppermute | solution.py:580
  677.8 24.0 %collective-permute-done.42 = bf16[2,2,2,152,256]{4,3,1,2,0:T(8,128)(2,1)S(1)} collective-permute-done((bf16[2,2,2,152,256]{4,3,1,2,0:T(8,128)(2,1)S(1)}, bf16[2,2,2,152,256]{4,3,1,2,0:T(8,128)(2,1)S(1)}, u32[]{:S(2)}, u32[]{:S(2)}) %collective-permute-start.42) | collective-permute-done | bytes 622624 | tf_op jit(solution)/shard_map/ppermute | solution.py:580
  708.0 16.2 %collective-permute-done.57 = bf16[2,2,2,128,512]{4,3,1,2,0:T(8,128)(2,1)S(1)} collective-permute-done((bf16[2,2,2,128,512]{4,3,1,2,0:T(8,128)(2,1)S(1)}, bf16[2,2,2,128,512]{4,3,1,2,0:T(8,128)(2,1)S(1)}, u32[]{:S(2)}, u32[]{:S(2)}) %collective-permute-start.57) | collective-permute-done | bytes 1048608 | tf_op jit(solution)/shard_map/ppermute | solution.py:580
  740.0 5.7 collective-permute-done.49
  746.6 5.0 collective-permute-done.54
  806.2 5.0 collective-permute-done.64
  (524 shorter events, 339.1 us)
Async XLA Ops:
  7.2 107.6 %all-gather.8.cloned.1.call-start = ((), (), s32[]{:S(2)}) async-start(), calls=%async_computation | async-start | bytes 12976128 | tf_op jit(solution)/shard_map/all_gather | solution.py:712
  10.5 212.2 %all-gather.10.cloned.1.call-start = ((), (), s32[]{:S(2)}) async-start(), calls=%async_computation.1 | async-start | bytes 12976128 | tf_op jit(solution)/shard_map/all_gather | solution.py:712
  38.9 66.9 %collective-permute-start = (bf16[16,1024]{0,1:T(8,128)(2,1)}, bf16[16,1024]{0,1:T(8,128)(2,1)S(1)}, u32[]{:S(2)}, u32[]{:S(2)}) collective-permute-start(bf16[16,1024]{0,1:T(8,128)(2,1)} %slice.401), channel_id=1, source_target_pairs={{0,1},{1,2},{2,3},{4,5},{5,6},{6,7},{8,9},{9,10},{10,11},{12,13},{... | collective-permute-start | bytes 98312 | tf_op jit(solution)/shard_map/ppermute | solution.py:570
  148.3 43.7 %collective-permute-start.2 = (bf16[144,2048]{1,0:T(8,128)(2,1)}, bf16[144,2048]{1,0:T(8,128)(2,1)}, u32[]{:S(2)}, u32[]{:S(2)}) collective-permute-start(bf16[144,2048]{1,0:T(8,128)(2,1)} %maximum_maximum_fusion), channel_id=1, source_target_pairs={{0,2},{1,3},{4,6},{5,7},{8,10},{9,11},{12,14},{13,15},{16,18},{17,... | collective-permute-start | bytes 1769480 | tf_op jit(solution)/shard_map/ppermute | solution.py:621
  458.3 132.0 %collective-permute-start.31 = (bf16[2,2,2,2,128,512]{5,4,1,2,3,0:T(8,128)(2,1)}, bf16[2,2,2,2,128,512]{5,4,1,2,3,0:T(8,128)(2,1)}, u32[]{:S(2)}, u32[]{:S(2)}) collective-permute-start(bf16[2,2,2,2,128,512]{5,4,1,2,3,0:T(8,128)(2,1)} %bitcast.361), channel_id=1, source_target_pairs={{0,1},{1,0},{2,3},{3,2},{4,5},{5,4},{6,7},{7,6},{8,9},{9,8},{10,11... | collective-permute-start | bytes 6291464 | tf_op jit(solution)/shard_map/ppermute | solution.py:580
  459.9 134.0 %collective-permute-start.26 = (bf16[2,2,2,2,128,512]{5,4,1,2,3,0:T(8,128)(2,1)}, bf16[2,2,2,2,128,512]{5,4,1,2,3,0:T(8,128)(2,1)}, u32[]{:S(2)}, u32[]{:S(2)}) collective-permute-start(bf16[2,2,2,2,128,512]{5,4,1,2,3,0:T(8,128)(2,1)} %bitcast.362), channel_id=1, source_target_pairs={{0,1},{1,0},{2,3},{3,2},{4,5},{5,4},{6,7},{7,6},{8,9},{9,8},{10,11... | collective-permute-start | bytes 6291464 | tf_op jit(solution)/shard_map/ppermute | solution.py:580
  469.2 127.4 %collective-permute-start.61 = (bf16[2,2,2,2,128,512]{5,4,1,2,0,3:T(8,128)(2,1)}, bf16[2,2,2,2,128,512]{5,4,1,2,0,3:T(8,128)(2,1)}, u32[]{:S(2)}, u32[]{:S(2)}) collective-permute-start(bf16[2,2,2,2,128,512]{5,4,1,2,0,3:T(8,128)(2,1)} %bitcast.359), channel_id=1, source_target_pairs={{0,1},{1,0},{2,3},{3,2},{4,5},{5,4},{6,7},{7,6},{8,9},{9,8},{10,11... | collective-permute-start | bytes 6291464 | tf_op jit(solution)/shard_map/ppermute | solution.py:580
  562.9 37.6 %collective-permute-start.56 = (bf16[2,2,2,2,128,512]{5,4,1,2,0,3:T(8,128)(2,1)}, bf16[2,2,2,2,128,512]{5,4,1,2,0,3:T(8,128)(2,1)}, u32[]{:S(2)}, u32[]{:S(2)}) collective-permute-start(bf16[2,2,2,2,128,512]{5,4,1,2,0,3:T(8,128)(2,1)} %bitcast.360), channel_id=1, source_target_pairs={{0,1},{1,0},{2,3},{3,2},{4,5},{5,4},{6,7},{7,6},{8,9},{9,8},{10,11... | collective-permute-start | bytes 6291464 | tf_op jit(solution)/shard_map/ppermute | solution.py:580
  600.5 101.7 %collective-permute-start.32 = (bf16[2,2,2,128,512]{4,3,0,1,2:T(8,128)(2,1)S(1)}, bf16[2,2,2,128,512]{4,3,0,1,2:T(8,128)(2,1)S(1)}, u32[]{:S(2)}, u32[]{:S(2)}) collective-permute-start(bf16[2,2,2,128,512]{4,3,0,1,2:T(8,128)(2,1)S(1)} %dynamic-slice_bitcast_fusion.2), channel_id=1, source_target_pairs={{0,2},{1,3},{2,0},{3,1},{4,6},{5,7},{6,4},{7,5},{8,10},{9,11},{10,... | collective-permute-start | bytes 3145736 | tf_op jit(solution)/shard_map/ppermute | solution.py:580
  604.5 100.9 %collective-permute-start.27 = (bf16[2,2,2,128,512]{4,3,0,1,2:T(8,128)(2,1)S(1)}, bf16[2,2,2,128,512]{4,3,0,1,2:T(8,128)(2,1)S(1)}, u32[]{:S(2)}, u32[]{:S(2)}) collective-permute-start(bf16[2,2,2,128,512]{4,3,0,1,2:T(8,128)(2,1)S(1)} %dynamic-slice_bitcast_fusion.3), channel_id=1, source_target_pairs={{0,2},{1,3},{2,0},{3,1},{4,6},{5,7},{6,4},{7,5},{8,10},{9,11},{10,... | collective-permute-start | bytes 3145736 | tf_op jit(solution)/shard_map/ppermute | solution.py:580
  607.3 55.1 %collective-permute-start.47 = (bf16[2,2,2,152,256]{4,3,0,1,2:T(8,128)(2,1)S(1)}, bf16[2,2,2,152,256]{4,3,0,1,2:T(8,128)(2,1)S(1)}, u32[]{:S(2)}, u32[]{:S(2)}) collective-permute-start(bf16[2,2,2,152,256]{4,3,0,1,2:T(8,128)(2,1)S(1)} %dynamic-slice_bitcast_fusion.5), channel_id=1, source_target_pairs={{0,2},{1,3},{2,0},{3,1},{4,6},{5,7},{6,4},{7,5},{8,10},{9,11},{10,... | collective-permute-start | bytes 1867784 | tf_op jit(solution)/shard_map/ppermute | solution.py:580
  608.7 67.1 %collective-permute-start.52 = (bf16[2,2,2,152,256]{4,3,1,2,0:T(8,128)(2,1)S(1)}, bf16[2,2,2,152,256]{4,3,1,2,0:T(8,128)(2,1)S(1)}, u32[]{:S(2)}, u32[]{:S(2)}) collective-permute-start(bf16[2,2,2,152,256]{4,3,1,2,0:T(8,128)(2,1)S(1)} %dynamic-slice_bitcast_fusion.4), channel_id=1, source_target_pairs={{0,4},{4,0},{8,12},{12,8},{16,20},{20,16},{24,28},{28,24},{1,5},{5... | collective-permute-start | bytes 1867784 | tf_op jit(solution)/shard_map/ppermute | solution.py:580
  610.0 65.2 %collective-permute-start.37 = (bf16[2,2,2,152,256]{4,3,0,1,2:T(8,128)(2,1)S(1)}, bf16[2,2,2,152,256]{4,3,0,1,2:T(8,128)(2,1)S(1)}, u32[]{:S(2)}, u32[]{:S(2)}) collective-permute-start(bf16[2,2,2,152,256]{4,3,0,1,2:T(8,128)(2,1)S(1)} %dynamic-slice_bitcast_fusion.7), channel_id=1, source_target_pairs={{0,2},{1,3},{2,0},{3,1},{4,6},{5,7},{6,4},{7,5},{8,10},{9,11},{10,... | collective-permute-start | bytes 1867784 | tf_op jit(solution)/shard_map/ppermute | solution.py:580
  662.3 44.6 %collective-permute-start.62 = (bf16[2,2,2,128,512]{4,3,1,2,0:T(8,128)(2,1)S(1)}, bf16[2,2,2,128,512]{4,3,1,2,0:T(8,128)(2,1)S(1)}, u32[]{:S(2)}, u32[]{:S(2)}) collective-permute-start(bf16[2,2,2,128,512]{4,3,1,2,0:T(8,128)(2,1)S(1)} %dynamic-slice_bitcast_fusion), channel_id=1, source_target_pairs={{0,4},{4,0},{8,12},{12,8},{16,20},{20,16},{24,28},{28,24},{1,5},{5... | collective-permute-start | bytes 3145736 | tf_op jit(solution)/shard_map/ppermute | solution.py:580
  675.2 26.5 %collective-permute-start.42 = (bf16[2,2,2,152,256]{4,3,1,2,0:T(8,128)(2,1)S(1)}, bf16[2,2,2,152,256]{4,3,1,2,0:T(8,128)(2,1)S(1)}, u32[]{:S(2)}, u32[]{:S(2)}) collective-permute-start(bf16[2,2,2,152,256]{4,3,1,2,0:T(8,128)(2,1)S(1)} %dynamic-slice_bitcast_fusion.6), channel_id=1, source_target_pairs={{0,4},{4,0},{8,12},{12,8},{16,20},{20,16},{24,28},{28,24},{1,5},{5... | collective-permute-start | bytes 1867784 | tf_op jit(solution)/shard_map/ppermute | solution.py:580
  675.8 48.4 %collective-permute-start.57 = (bf16[2,2,2,128,512]{4,3,1,2,0:T(8,128)(2,1)S(1)}, bf16[2,2,2,128,512]{4,3,1,2,0:T(8,128)(2,1)S(1)}, u32[]{:S(2)}, u32[]{:S(2)}) collective-permute-start(bf16[2,2,2,128,512]{4,3,1,2,0:T(8,128)(2,1)S(1)} %dynamic-slice_bitcast_fusion.1), channel_id=1, source_target_pairs={{0,4},{4,0},{8,12},{12,8},{16,20},{20,16},{24,28},{28,24},{1,5},{5... | collective-permute-start | bytes 3145736 | tf_op jit(solution)/shard_map/ppermute | solution.py:580
  701.8 29.1 %collective-permute-start.48 = (bf16[2,2,152,256]{3,2,0,1:T(8,128)(2,1)S(1)}, bf16[2,2,152,256]{3,2,0,1:T(8,128)(2,1)S(1)}, u32[]{:S(2)}, u32[]{:S(2)}) collective-permute-start(bf16[2,2,152,256]{3,2,0,1:T(8,128)(2,1)S(1)} %dynamic-slice_bitcast_fusion.13), channel_id=1, source_target_pairs={{0,4},{4,0},{8,12},{12,8},{16,20},{20,16},{24,28},{28,24},{1,5},{5... | collective-permute-start | bytes 933896 | tf_op jit(solution)/shard_map/ppermute | solution.py:580
  702.2 29.0 %collective-permute-start.53 = (bf16[2,2,152,256]{3,2,0,1:T(8,128)(2,1)S(1)}, bf16[2,2,152,256]{3,2,0,1:T(8,128)(2,1)S(1)}, u32[]{:S(2)}, u32[]{:S(2)}) collective-permute-start(bf16[2,2,152,256]{3,2,0,1:T(8,128)(2,1)S(1)} %dynamic-slice_bitcast_fusion.12), channel_id=1, source_target_pairs={{0,2},{1,3},{2,0},{3,1},{4,6},{5,7},{6,4},{7,5},{8,10},{9,11},{10,... | collective-permute-start | bytes 933896 | tf_op jit(solution)/shard_map/ppermute | solution.py:580
  705.4 32.2 %collective-permute-start.38 = (bf16[2,2,152,256]{3,2,0,1:T(8,128)(2,1)S(1)}, bf16[2,2,152,256]{3,2,0,1:T(8,128)(2,1)S(1)}, u32[]{:S(2)}, u32[]{:S(2)}) collective-permute-start(bf16[2,2,152,256]{3,2,0,1:T(8,128)(2,1)S(1)} %dynamic-slice_bitcast_fusion.15), channel_id=1, source_target_pairs={{0,4},{4,0},{8,12},{12,8},{16,20},{20,16},{24,28},{28,24},{1,5},{5... | collective-permute-start | bytes 933896 | tf_op jit(solution)/shard_map/ppermute | solution.py:580
  707.0 32.1 %collective-permute-start.43 = (bf16[2,2,152,256]{3,2,0,1:T(8,128)(2,1)S(1)}, bf16[2,2,152,256]{3,2,0,1:T(8,128)(2,1)S(1)}, u32[]{:S(2)}, u32[]{:S(2)}) collective-permute-start(bf16[2,2,152,256]{3,2,0,1:T(8,128)(2,1)S(1)} %dynamic-slice_bitcast_fusion.14), channel_id=1, source_target_pairs={{0,2},{1,3},{2,0},{3,1},{4,6},{5,7},{6,4},{7,5},{8,10},{9,11},{10,... | collective-permute-start | bytes 933896 | tf_op jit(solution)/shard_map/ppermute | solution.py:580
  724.2 63.1 %collective-permute-start.33 = (bf16[2,2,128,512]{3,2,0,1:T(8,128)(2,1)}, bf16[2,2,128,512]{3,2,0,1:T(8,128)(2,1)}, u32[]{:S(2)}, u32[]{:S(2)}) collective-permute-start(bf16[2,2,128,512]{3,2,0,1:T(8,128)(2,1)} %dynamic-slice_bitcast_fusion.10), channel_id=1, source_target_pairs={{0,4},{4,0},{8,12},{12,8},{16,20},{20,16},{24,28},{28,24},{1,5},{5... | collective-permute-start | bytes 1572872 | tf_op jit(solution)/shard_map/ppermute | solution.py:580
  730.9 61.3 %collective-permute-start.28 = (bf16[2,2,128,512]{3,2,0,1:T(8,128)(2,1)}, bf16[2,2,128,512]{3,2,0,1:T(8,128)(2,1)}, u32[]{:S(2)}, u32[]{:S(2)}) collective-permute-start(bf16[2,2,128,512]{3,2,0,1:T(8,128)(2,1)} %dynamic-slice_bitcast_fusion.11), channel_id=1, source_target_pairs={{0,4},{4,0},{8,12},{12,8},{16,20},{20,16},{24,28},{28,24},{1,5},{5... | collective-permute-start | bytes 1572872 | tf_op jit(solution)/shard_map/ppermute | solution.py:580
  731.2 62.3 %collective-permute-start.63 = (bf16[2,2,128,512]{3,2,0,1:T(8,128)(2,1)}, bf16[2,2,128,512]{3,2,0,1:T(8,128)(2,1)}, u32[]{:S(2)}, u32[]{:S(2)}) collective-permute-start(bf16[2,2,128,512]{3,2,0,1:T(8,128)(2,1)} %dynamic-slice_bitcast_fusion.8), channel_id=1, source_target_pairs={{0,2},{1,3},{2,0},{3,1},{4,6},{5,7},{6,4},{7,5},{8,10},{9,11},{10,... | collective-permute-start | bytes 1572872 | tf_op jit(solution)/shard_map/ppermute | solution.py:580
  737.6 59.2 %collective-permute-start.58 = (bf16[2,2,128,512]{3,2,0,1:T(8,128)(2,1)}, bf16[2,2,128,512]{3,2,0,1:T(8,128)(2,1)}, u32[]{:S(2)}, u32[]{:S(2)}) collective-permute-start(bf16[2,2,128,512]{3,2,0,1:T(8,128)(2,1)} %dynamic-slice_bitcast_fusion.9), channel_id=1, source_target_pairs={{0,2},{1,3},{2,0},{3,1},{4,6},{5,7},{6,4},{7,5},{8,10},{9,11},{10,... | collective-permute-start | bytes 1572872 | tf_op jit(solution)/shard_map/ppermute | solution.py:580
  (98 other events, 939.3 us)
Sparse Core Ops, SparseCore 0:
  11.5 103.2 all-gather.7
  117.7 102.1 all-gather.9

commit v2 on v1

--- a/solution.py
+++ b/solution.py
@@ -111,37 +111,34 @@
     return ((row >= col) if lower else (row <= col)).astype(f32)
 
 
-def scan_in_kernel(
-    heads,
-    own,
-    taps_n,
-    nrm,
-    w,
-    wb,
-    prm,
-    cbc,
-    hp,
-    segc,
-    segr,
-    y,
-    xin,
-    state,
-    ftot,
-    shared,
-    b_out,
-    c_out,
-    bt_out,
-    ct_out,
-    dtp_out,
-    cumt_out,
-    dts_out,
-    es_out,
-    fs_out,
-    fd_out,
-    cums_out,
-    g_scr,
-    m_scr,
-):
+def scan_in_kernel(heads, own, taps_n, pieces, nrm, *refs):
+    w, refs = refs[:pieces], refs[pieces:]
+    (
+        wb,
+        prm,
+        cbc,
+        hp,
+        segc,
+        segr,
+        y,
+        xin,
+        state,
+        ftot,
+        shared,
+        b_out,
+        c_out,
+        bt_out,
+        ct_out,
+        dtp_out,
+        cumt_out,
+        dts_out,
+        es_out,
+        fs_out,
+        fd_out,
+        cums_out,
+        g_scr,
+        m_scr,
+    ) = refs
     group = pl.program_id(0)
     rows = y.shape[0]
     width = y.shape[1]
@@ -190,8 +187,9 @@
             )
             m_scr[c] = jnp.where(ok, 0.0, NEG)
 
-    weight = w[...].reshape(-1, width)
-    ext = mm(nrm[...], weight)
+    ext = jnp.concatenate(
+        [mm(nrm[...], part[...].reshape(nrm.shape[1], -1)) for part in w], axis=1
+    )
     xin[...] = ext
     u = conv(ext, prm[0], keep, rows, taps_n)
     xc = u * jax.nn.sigmoid(u)
@@ -225,8 +223,9 @@
             now = fx[hi - 1 : hi] * now + local
         else:
             now = local
-    state[...] = low(now)
-    ftot[...] = jnp.broadcast_to(mm(fd_out[...], grow)[rows - 1 : rows], ftot.shape)
+    whole_factor = mm(fd_out[...], grow)[rows - 1 : rows]
+    ftot[...] = jnp.broadcast_to(whole_factor, ftot.shape)
+    put_state(state, now, whole_factor)
 
 
 def gate_kernel(
@@ -248,6 +247,7 @@
     grms,
     nxt,
     ss,
+    gated_scr,
 ):
     group = pl.program_id(0)
     width = y_loc.shape[1]
@@ -259,23 +259,25 @@
     y_out[...] = y
     gated = y * (z * jax.nn.sigmoid(z))
     squares = jnp.sum(gated * gated, axis=1, keepdims=True)
-    part = mmt(low(gated * prm[0, 5:6]), wo[...].reshape(-1, width))
+    gated_scr[group] = gated
 
     @pl.when(group == 0)
     def _():
         ss[...] = jnp.broadcast_to(squares, ss.shape)
-        branch[...] = part
 
     @pl.when(group > 0)
     def _():
         ss[...] += jnp.broadcast_to(squares, ss.shape)
-        branch[...] += part
 
     @pl.when(group == pl.num_programs(0) - 1)
     def _():
         scale = lax.rsqrt(ss[...] / full + epsilon)
         grms[...] = scale
-        total = branch[...] * scale[:, 0:1]
+        total = None
+        for g in range(prm.shape[0]):
+            mixed = low(gated_scr[g] * scale[:, 0:1] * prm[g, 5:6])
+            part = mmt(mixed, wo[g].reshape(-1, width))
+            total = part if total is None else total + part
         branch[...] = total
         nxt[...] = hid[...] + total
 
@@ -296,8 +298,7 @@
     ct,
     fd,
     prm,
-    g_out,
-    g_z,
+    g_zo,
     dy_out,
     dn,
     dstate,
@@ -306,6 +307,8 @@
 ):
     group = pl.program_id(0)
     rows, width = z_in.shape
+    depth = wz.shape[1]
+    block = wz.shape
 
     @pl.when(group == 0)
     def _():
@@ -320,13 +323,13 @@
     gated = y * sz
     scaled = gated * rms
     gain = prm[0, 5:6]
-    g_out[...] = low(mm(dbrt[...], low(scaled * gain))).reshape(g_out.shape)
+    g_zo[:, depth:] = low(mm(dbrt[...], low(scaled * gain))).reshape(block)
     g_gain[...] = jnp.broadcast_to(jnp.sum(dm * scaled, axis=0, keepdims=True), g_gain.shape)
     dg = rms * (dm * gain) - gated * q_scr[:, 0:1]
     dy = dg * sz
     dy_out[...] = dy
     dz = low(dg * y * (sg + sz * (1.0 - sg)))
-    g_z[...] = low(mm(nrmt[:, :rows], dz)).reshape(g_z.shape)
+    g_zo[:, :depth] = low(mm(nrmt[:, :rows], dz)).reshape(block)
     part = mmt(dz, wz[...].reshape(-1, width))
 
     @pl.when(group == 0)
@@ -337,7 +340,16 @@
     def _():
         dn[...] += part
 
-    dstate[...] = low(mm3(ct[...], mm(fd[...], spread(group, heads, own, width)) * dy))
+    fx = mm(fd[...], spread(group, heads, own, width))
+    put_state(dstate, mm3(ct[...], fx * dy), fx[rows - 1 : rows])
+
+
+def put_state(state, now, factor):
+    high, rest = two(factor)
+    count = state.shape[0] - now.shape[0]
+    row = iota((count, factor.shape[1]), 0)
+    tail = jnp.where(row == 0, high.astype(f32), jnp.where(row == 1, rest.astype(f32), 0.0))
+    state[...] = low(jnp.concatenate([now, tail], axis=0))
 
 
 def conv_back(du, ext, taps, keep, rows, count, dest):
@@ -353,51 +365,44 @@
     return sums, jnp.sum(du, axis=0, keepdims=True)
 
 
-def scan_back_kernel(
-    heads,
-    own,
-    taps_n,
-    xin,
-    dy_in,
-    y_in,
-    s_in,
-    ds_in,
-    w,
-    wb,
-    prm,
-    cbc,
-    hp,
-    segc,
-    segr,
-    nrmt,
-    shared,
-    b_in,
-    c_in,
-    bt,
-    ct,
-    dtp,
-    cumt,
-    dts,
-    es,
-    fs,
-    cums,
-    g_x,
-    g_b,
-    dn,
-    g_prm,
-    g_cbc,
-    g_hp,
-    gt_scr,
-    mt_scr,
-    dgt_scr,
-    db_scr,
-    dc_scr,
-    dcum_scr,
-    ddt_scr,
-    dx_scr,
-    dbc_scr,
-    dxc_scr,
-):
+def scan_back_kernel(heads, own, taps_n, pieces, xin, dy_in, y_in, s_in, ds_in, *refs):
+    w, refs = refs[:pieces], refs[pieces:]
+    (
+        wb,
+        prm,
+        cbc,
+        hp,
+        segc,
+        segr,
+        nrmt,
+        shared,
+        b_in,
+        c_in,
+        bt,
+        ct,
+        dtp,
+        cumt,
+        dts,
+        es,
+        fs,
+        cums,
+        g_x,
+        g_b,
+        dn,
+        g_prm,
+        g_cbc,
+        g_hp,
+        gt_scr,
+        mt_scr,
+        dgt_scr,
+        db_scr,
+        dc_scr,
+        dcum_scr,
+        ddt_scr,
+        dx_scr,
+        dbc_scr,
+        dxc_scr,
+    ) = refs
     group = pl.program_id(0)
     rows, width = dy_in.shape
     chunks = rows // SPAN
@@ -489,7 +494,13 @@
     g_prm[0, 7:8] = jnp.zeros_like(bias)
     dxb = low(dx_scr[...])
     g_x[...] = low(mm(nrmt[...], dxb)).reshape(g_x.shape)
-    part = mmt(dxb[: rows + HALO], w[...].reshape(-1, width))
+    part, step = None, width // pieces
+    for n, weight in enumerate(w):
+        term = mmt(
+            dxb[: rows + HALO, n * step : (n + 1) * step],
+            weight[...].reshape(-1, step),
+        )
+        part = term if part is None else part + term
 
     @pl.when(group == 0)
     def _():
@@ -549,9 +560,10 @@
     return pl.BlockSpec((rows, width), lambda g: (0, g))
 
 
-def kind_block(weights, kind):
+def kind_block(depth, pair):
+    weights, kind = pair
     shape = weights.shape
-    return pl.BlockSpec((None, shape[1], None, shape[3], shape[4]), lambda g: (g, 0, kind, 0, 0))
+    return pl.BlockSpec((None, shape[1], depth, shape[3]), lambda g: (g, 0, kind, 0))
 
 
 def params(flops, moved):
@@ -586,48 +598,62 @@
     return x
 
 
-def scatter_sum(x, axes, order, kind):
+def scatter_start(x, axes):
     names = [pair for axis in axes for pair in reversed(bits_of(axis))]
-    x = x.reshape((2,) * len(names) + x.shape[len(axes) :])
-    for n, (axis, bit) in enumerate(order):
-        dim = names.index((axis, bit))
-        mine = (lax.axis_index(axis) >> bit) & 1
-        got = exchange(lax.dynamic_index_in_dim(x, 1 - mine, dim, False), axis, bit)
-        x = lax.dynamic_index_in_dim(x, mine, dim, False).astype(f32) + got.astype(f32)
-        if n + 1 < len(order):
-            x = x.astype(kind)
-        names.pop(dim)
+    return x.reshape((2,) * len(names) + x.shape[len(axes) :]), names
+
+
+def outgoing(x, names, pair):
+    axis, bit = pair
+    mine = (lax.axis_index(axis) >> bit) & 1
+    return lax.dynamic_index_in_dim(x, 1 - mine, names.index(pair), False)
+
+
+def scatter_step(x, names, pair, got=None, kind=bf16):
+    axis, bit = pair
+    mine = (lax.axis_index(axis) >> bit) & 1
+    if got is None:
+        got = exchange(outgoing(x, names, pair), axis, bit)
+    x = lax.dynamic_index_in_dim(x, mine, names.index(pair), False)
+    x = (x.astype(f32) + got.astype(f32)).astype(kind)
+    return x, [name for name in names if name != pair]
+
+
+def scatter_rest(x, names, order, kind=bf16):
+    for n, pair in enumerate(order):
+        x, names = scatter_step(x, names, pair, None, f32 if n + 1 == len(order) else kind)
     return x
 
 
-def carry_states(state, factor, axis, backward):
+def carry_states(packed, axis, backward):
     size, at = lax.axis_size(axis), lax.axis_index(axis)
-    total = state.astype(f32)
+    count = packed.shape[0] - HALO
+
+    def unpack(x):
+        x = x.astype(f32)
+        return x[:count], x[count : count + 1] + x[count + 1 : count + 2]
+
+    total, factor = unpack(packed)
     prefix = jnp.zeros_like(total)
     prefix_factor = jnp.ones_like(factor)
     step = 1
     while step < size:
-        first = low(factor)
-        second = low(factor - first.astype(f32))
-        packed = jnp.concatenate(
-            [low(total), first, second, jnp.zeros((14, factor.shape[1]), bf16)], axis=0
-        )
         upper = ((at // step) % 2) == 1
         follows = jnp.logical_not(upper) if backward else upper
         pairs = [(i, i ^ step) for i in range(size)]
         final = 2 * step >= size
         if final:
             pairs = [p for p in pairs if (p[0] > p[1]) == backward]
-        got = lax.ppermute(packed, axis, pairs)
-        other = got[: state.shape[0]].astype(f32)
-        other_factor = got[state.shape[0] : state.shape[0] + 1].astype(f32) + got[
-            state.shape[0] + 1 : state.shape[0] + 2
-        ].astype(f32)
+        other, other_factor = unpack(lax.ppermute(packed, axis, pairs))
         prefix = jnp.where(follows, prefix_factor * other + prefix, prefix)
         if not final:
             prefix_factor = jnp.where(follows, prefix_factor * other_factor, prefix_factor)
             total = jnp.where(follows, factor * other + total, other_factor * total + other)
             factor = factor * other_factor
+            high, rest = two(factor)
+            packed = jnp.concatenate(
+                [low(total), high, rest, jnp.zeros((HALO - 2, factor.shape[1]), bf16)], axis=0
+            )
         step *= 2
     return low(prefix)
 
@@ -651,6 +677,10 @@
 ):
     layers, taps_n = conv_x.shape[0], conv_x.shape[1]
     groups, shards = lax.axis_size("tensor"), lax.axis_size("dp")
+    tb, db = bits_of("tensor"), bits_of("dp")
+    axes = ("tensor", "dp")
+    order_x = tb + db
+    order_y = tb[:1] + db[:1] + tb[1:] + db[1:]
     at_t = lax.axis_index("tensor")
     at_d = lax.axis_index("dp")
     own = dt_bias.shape[1]
@@ -703,16 +733,60 @@
         [conv_bc, conv_bc_bias[:, None], jnp.zeros((layers, 3, bc), f32)], axis=1
     )
 
-    gains = lax.all_gather(in_gain, "dp", axis=1, tiled=True).astype(f32)
-    weights, wbs = [], []
+    rows_b = depth // groups
+
+    def shared_rows(i):
+        both = jnp.concatenate([w_bcdt[i], in_gain[i][:, None]], axis=1)
+        own_rows = lax.dynamic_slice_in_dim(both, at_t * rows_b, rows_b, 0)
+        return jnp.pad(own_rows, ((0, 0), (0, width - both.shape[1])))
+
+    def gather(pieces):
+        local = jnp.concatenate(pieces, axis=0)
+        got = lax.all_gather(local, ("tensor", "dp"), axis=0, tiled=False)
+        return got.reshape((groups, shards) + local.shape)
+
+    def spread_out(x, order):
+        target = [pair for axis in axes for pair in reversed(bits_of(axis))]
+        names = []
+        for axis, bit in order:
+            got = exchange(x, axis, bit)
+            mine = (lax.axis_index(axis) >> bit) & 1
+            dim = sum(target.index(name) < target.index((axis, bit)) for name in names)
+            x = jnp.stack([jnp.where(mine == 0, x, got), jnp.where(mine == 0, got, x)], axis=dim)
+            names.insert(dim, (axis, bit))
+        return x.reshape((groups, shards) + x.shape[len(names) :])
+
+    first = jnp.concatenate([w_zx[0, :, 1], shared_rows(0)], axis=0)
+    half = width // 2
+    ring = db[1:] + db[:1]
+    first = [
+        spread_out(first[:, :half], ring + tb[1:] + tb[:1]),
+        spread_out(first[:, half:], ring[:-1] + tb[1:] + ring[-1:] + tb[:1]),
+    ]
+    head = gather(
+        [w_zx[0, :, 0], w_out[0]]
+        + [w_zx[i, :, 1] for i in range(1, layers)]
+        + [shared_rows(i) for i in range(1, layers)]
+    )
+    w_x = [[(part, 0) for part in first]] + [[(head, 1 + i)] for i in range(1, layers)]
+    w_z, w_o = [(head, 0)], [(head, 1)]
+    for i in range(1, layers):
+        later = gather([w_zx[i, :, 0], w_out[i]])
+        w_z.append((later, 0))
+        w_o.append((later, 1))
+    wbs, gains = [], []
     for i in range(layers):
-        local = jnp.concatenate(
-            [jnp.moveaxis(w_zx[i], 1, 0), w_out[i][None]], axis=0
+        at = (1 + layers) * depth + (i - 1) * rows_b
+        held = [part[:, :, depth:] for part in first] if i == 0 else [head[:, :, at : at + rows_b]]
+        got = jnp.concatenate(
+            [jnp.moveaxis(part, 0, 1).reshape(model, -1)[:, : 2 * half] for part in held], axis=1
         )
-        got = lax.all_gather(local, ("tensor", "dp"), axis=0, tiled=False)
-        weights.append(got.reshape(groups, shards, 3, depth, width))
-        wb = lax.all_gather(w_bcdt[i], "dp", axis=0, tiled=True)
-        wbs.append(jnp.concatenate([wb[:, :bc], jnp.tile(wb[:, bc:], (1, copies))], axis=1))
+        wbs.append(
+            jnp.concatenate(
+                [got[:, :bc], jnp.tile(got[:, bc : bc + heads], (1, copies))], axis=1
+            )
+        )
+        gains.append(got[:, bc + heads].astype(f32))
 
     small = [
         ((ext, wide), f32),
@@ -739,14 +813,14 @@
         nrmt = jnp.concatenate(
             [normed, before, jnp.zeros((LANES - HALO, model), bf16)], axis=0
         ).T
-        w, wb, pr = weights[i], wbs[i], prm[:, i]
+        wb, pr = wbs[i], prm[:, i]
         flops = 2 * ext * model * (full + wide)
         outs = pl.pallas_call(
-            partial(scan_in_kernel, heads, own, taps_n),
+            partial(scan_in_kernel, heads, own, taps_n, len(w_x[i])),
             grid=(groups,),
             in_specs=[
                 whole((ext, model)),
-                kind_block(w, 1),
+                *[kind_block(depth, part) for part in w_x[i]],
                 whole((model, wide)),
                 prm_spec,
                 whole((8, bc)),
@@ -757,14 +831,14 @@
             out_specs=[
                 by_column(rows, width),
                 by_column(ext, width),
-                by_column(state_n, width),
+                by_column(state_n + HALO, width),
                 by_column(8, width),
             ]
             + [whole(s) for s, _ in small],
             out_shape=[
                 struct(rows, full),
                 struct(ext, full),
-                struct(state_n, full, dtype=bf16),
+                struct(state_n + HALO, full, dtype=bf16),
                 struct(8, full),
             ]
             + [struct(*s, dtype=d) for s, d in small],
@@ -774,23 +848,23 @@
             ],
             name="scan_in",
             **params(3 * flops, 4 * rows * full * 3),
-        )(nrm, w, wb, pr, cbc[i], hp[i], segc, segr)
+        )(nrm, *[part for part, _ in w_x[i]], wb, pr, cbc[i], hp[i], segc, segr)
         y_loc, xin, state, ftot = outs[:4]
         rest = outs[4:]
         shared, b_m, c_m, b_t, c_t, dtp, cumt, dts, es, fs, fd, cums = rest
-        s_in = carry_states(state, ftot[0:1], "tensor", False)
+        s_in = carry_states(state, "tensor", False)
         z, y, branch, grms, nxt = pl.pallas_call(
             partial(gate_kernel, heads, own, full),
             grid=(groups,),
             in_specs=[
                 whole((ext, model)),
-                kind_block(w, 0),
-                kind_block(w, 2),
+                kind_block(depth, w_z[i]),
+                pl.BlockSpec((groups, shards, depth, width), lambda g, k=w_o[i][1]: (0, 0, k, 0)),
                 by_column(rows, width),
                 whole((rows, state_n)),
                 whole((rows, LANES)),
                 by_column(state_n, width),
-                prm_spec,
+                whole((groups, 8, width)),
                 whole((rows, model)),
             ],
             out_specs=[
@@ -807,35 +881,40 @@
                 struct(rows, LANES),
                 struct(rows, model),
             ],
-            scratch_shapes=[pltpu.VMEM((rows, LANES), f32)],
+            scratch_shapes=[
+                pltpu.VMEM((rows, LANES), f32),
+                pltpu.VMEM((groups, rows, width), f32),
+            ],
             name="gate",
             **params(4 * rows * model * full, 4 * rows * full * 5),
-        )(nrm, w, w, y_loc, c_m, fd, s_in, pr, stream)
+        )(nrm, w_z[i][0], w_o[i][0], y_loc, c_m, fd, s_in, pr, stream)
         saved.append((stream, rinv, nrmt, xin, ftot, rest, s_in, z, y, branch, grms))
         stream = nxt
 
+    def grad_block(count):
+        return pl.BlockSpec((None, shards, count, width), lambda g: (g, 0, 0, 0))
+
     grad = cotangent
-    big, shared_grads, gain_grads, prm_grads, cbc_grads, hp_grads = [], [], [], [], [], []
-    in_gain_grads = []
-    tb, db = bits_of("tensor"), bits_of("dp")
-    order_x = tb + db
-    order_y = tb[:1] + db[:1] + tb[1:] + db[1:]
+    x_part = None
+    gain_grads, prm_grads, cbc_grads, hp_grads = [], [], [], []
+
     for i in reversed(range(layers)):
         stream_in, rinv, nrmt, xin, ftot, rest, s_in, z, y, branch, grms = saved[i]
         shared, b_m, c_m, b_t, c_t, dtp, cumt, dts, es, fs, fd, cums = rest
-        w, wb, pr = weights[i], wbs[i], prm[:, i]
+        wb, pr = wbs[i], prm[:, i]
         dbr = grad.astype(bf16)
-        grad_block = pl.BlockSpec((None, shards, depth, width), lambda g: (g, 0, 0, 0))
-        grad_shape = struct(groups, shards, depth, width, dtype=bf16)
-        g_out, g_z, dy, dnz, dstate, g_gain = pl.pallas_call(
+        if x_part is not None:
+            dbr, x_part, x_send = lax.optimization_barrier((dbr, x_part, x_send))
+            x_got = exchange(x_send, *tb[1])
+        g_zo, dy, dnz, dstate, g_gain = pl.pallas_call(
             partial(gate_back_kernel, heads, own, full),
             grid=(groups,),
             in_specs=[
                 whole((rows, model)),
                 whole((model, rows)),
                 whole((rows, model)),
-                kind_block(w, 2),
-                kind_block(w, 0),
+                kind_block(depth, w_o[i]),
+                kind_block(depth, w_z[i]),
                 by_column(rows, width),
                 by_column(rows, width),
                 whole((rows, LANES)),
@@ -845,28 +924,53 @@
                 prm_spec,
             ],
             out_specs=[
-                grad_block,
-                grad_block,
+                grad_block(2 * depth),
                 by_column(rows, width),
                 whole((rows, model)),
-                by_column(state_n, width),
+                by_column(state_n + HALO, width),
                 by_column(8, width),
             ],
             out_shape=[
-                grad_shape,
-                grad_shape,
+                struct(groups, shards, 2 * depth, width, dtype=bf16),
                 struct(rows, full),
                 struct(rows, model),
-                struct(state_n, full, dtype=bf16),
+                struct(state_n + HALO, full, dtype=bf16),
                 struct(8, full),
             ],
             scratch_shapes=[pltpu.VMEM((rows, LANES), f32)],
             name="gate_back",
             **params(8 * rows * model * full, 4 * rows * full * 6),
-        )(dbr, dbr.T, branch, w, w, z, y, grms, nrmt, c_t, fd, pr)
-        ds_in = carry_states(dstate, ftot[0:1], "tensor", True)
+        )(dbr, dbr.T, branch, w_o[i][0], w_z[i][0], z, y, grms, nrmt, c_t, fd, pr)
+        if x_part is not None:
+            g_zo, dy, dnz, dstate, g_gain, x_got = lax.optimization_barrier(
+                (g_zo, dy, dnz, dstate, g_gain, x_got)
+            )
+        ds_in = carry_states(dstate, "tensor", True)
+        if x_part is not None:
+            x_part, _ = scatter_step(x_part, x_names, tb[1], x_got)
+            later_sum = jnp.concatenate([z_part, o_part, x_part], axis=len(db))
+            ds_in, later_sum = lax.optimization_barrier((ds_in, later_sum))
+            later_sum = lax.psum_scatter(
+                later_sum.reshape((shards,) + later_sum.shape[len(db) :]),
+                "dp",
+                scatter_dimension=0,
+                tiled=False,
+            )
+        chains = []
+        for part, order in (
+            (g_zo[:, :, :depth], order_x),
+            (g_zo[:, :, depth:], order_y if i == 0 else order_x),
+        ):
+            part, names = scatter_step(*scatter_start(part, axes), order[0])
+            chains.append((part, names, order[1], outgoing(part, names, order[1])))
+        (z_part, z_names, z_pair, z_send), (o_part, o_names, o_pair, o_send) = chains
+        ds_in, z_part, o_part, z_send, o_send = lax.optimization_barrier(
+            (ds_in, z_part, o_part, z_send, o_send)
+        )
+        z_got = exchange(z_send, *z_pair)
+        o_got = exchange(o_send, *o_pair)
         g_x, g_b, dn, g_prm, g_cbc, g_hp = pl.pallas_call(
-            partial(scan_back_kernel, heads, own, taps_n),
+            partial(scan_back_kernel, heads, own, taps_n, len(w_x[i])),
             grid=(groups,),
             in_specs=[
                 by_column(ext, width),
@@ -874,7 +978,7 @@
                 by_column(rows, width),
                 by_column(state_n, width),
                 by_column(state_n, width),
-                kind_block(w, 1),
+                *[kind_block(depth, part) for part in w_x[i]],
                 whole((model, wide)),
                 prm_spec,
                 whole((8, bc)),
@@ -885,7 +989,7 @@
             ]
             + [whole(s) for n, (s, _) in enumerate(small) if n != 10],
             out_specs=[
-                grad_block,
+                grad_block(depth),
                 whole((model, wide)),
                 whole((ext, model)),
                 pl.BlockSpec((1, 8, width), lambda g: (g, 0, 0)),
@@ -893,7 +997,7 @@
                 whole((8, LANES)),
             ],
             out_shape=[
-                grad_shape,
+                struct(groups, shards, depth + rows_b, width, dtype=bf16),
                 struct(model, wide),
                 struct(ext, model),
                 struct(groups, 8, width),
@@ -915,9 +1019,50 @@
             name="scan_back",
             **params(8 * rows * model * full, 4 * rows * full * 6),
         )(
-            xin, dy, y, s_in, ds_in, w, wb, pr, cbc[i], hp[i], segc, segr, nrmt,
+            xin, dy, y, s_in, ds_in, *[part for part, _ in w_x[i]], wb, pr, cbc[i], hp[i], segc, segr, nrmt,
             shared, b_m, c_m, b_t, c_t, dtp, cumt, dts, es, fs, cums,
         )
+        g_x, g_b, dn, g_prm, g_cbc, g_hp, z_got, o_got = lax.optimization_barrier(
+            (g_x, g_b, dn, g_prm, g_cbc, g_hp, z_got, o_got)
+        )
+        z_part, z_names = scatter_step(z_part, z_names, z_pair, z_got)
+        o_part, o_names = scatter_step(o_part, o_names, o_pair, o_got)
+        parts_b = low(jnp.pad(g_b[:, : bc + heads], ((0, 0), (0, width - bc - heads))))
+        parts_b = jnp.moveaxis(parts_b.reshape(shards, groups, rows_b, width), 1, 0)
+        g_x = lax.dynamic_update_slice(g_x, parts_b, (0, 0, depth, 0))
+        if i > 0:
+            x_part, x_names = scatter_step(*scatter_start(g_x, axes), tb[0])
+            x_send = outgoing(x_part, x_names, tb[1])
+        else:
+            x_full, x_names = scatter_start(g_x, axes)
+            x_got = exchange(outgoing(x_full, x_names, tb[0]), *tb[0])
+            chains = []
+            for cut, order in ((slice(None, half), order_x), (slice(half, None), order_y)):
+                part, names = scatter_step(x_full[..., cut], x_names, tb[0], x_got[..., cut])
+                chains.append([part, names, list(order[1:])])
+            chains.append([z_part, z_names, list(order_x[2:])])
+            chains.append([o_part, o_names, [p for p in order_y if p in o_names]])
+            later = (dn, g_prm, g_cbc, g_hp, g_gain)
+            while any(order for _, _, order in chains):
+                sends = [
+                    outgoing(part, names, order[0]) if order else part for part, names, order in chains
+                ]
+                if later is None:
+                    sends = lax.optimization_barrier(sends)
+                else:
+                    sends, later = lax.optimization_barrier((sends, later))
+                    dn, g_prm, g_cbc, g_hp, g_gain = later
+                    later = None
+                gots = [
+                    exchange(send, *order[0]) if order else send
+                    for send, (_, _, order) in zip(sends, chains)
+                ]
+                for chain, got in zip(chains, gots):
+                    part, names, order = chain
+                    if order:
+                        kind = bf16 if len(order) > 1 else f32
+                        chain[0], chain[1] = scatter_step(part, names, order[0], got, kind)
+                        chain[2] = order[1:]
         after = shift(dn[rows:], "tensor", -1)
         dnormed = dnz + dn[:rows]
         dnormed = jnp.concatenate(
@@ -930,49 +1075,43 @@
             scaled - scaled_in * jnp.mean(scaled * scaled_in, axis=-1, keepdims=True)
         )
 
-        rows_b = depth // groups
-        parts_b = jnp.pad(
-            low(g_b[:, : bc + heads]), ((0, 0), (0, wide - bc - heads))
-        ).reshape(shards, groups, rows_b * wide // width, width)
-        with_b = jnp.concatenate([g_x, jnp.moveaxis(parts_b, 1, 0)], axis=2)
-        half = width // 2
-        left = scatter_sum(with_b[..., :half], ("tensor", "dp"), order_x, bf16)
-        right = scatter_sum(with_b[..., half:], ("tensor", "dp"), order_y, bf16)
-        with_b = jnp.concatenate([left, right], axis=1)
-        big.append(
-            (
-                scatter_sum(g_z, ("tensor", "dp"), order_x, bf16),
-                with_b[:depth],
-                scatter_sum(g_out, ("tensor", "dp"), order_y, bf16),
-            )
-        )
-        shared_grads.append(with_b[depth:].reshape(rows_b, wide)[:, : bc + heads])
         g_prm = g_prm.at[:, 5].set(g_gain[0].reshape(groups, width))
-        g_prm = scatter_sum(g_prm, ("tensor",), bits_of("tensor"), f32)
-        rest_sum = jnp.concatenate([gain_grads[-1], g_cbc.reshape(-1), g_hp.reshape(-1)])
-        rest_sum = all_sum(rest_sum.reshape(-1, width), bits_of("tensor"))
-        rest_sum = all_sum(jnp.concatenate([g_prm, rest_sum], axis=0), bits_of("dp"))
-        prm_grads.append(rest_sum[:8])
-        rest_sum = rest_sum[8:].reshape(-1)
-        gain_all = rest_sum[:model]
-        cbc_grads.append(rest_sum[model : model + 8 * bc].reshape(8, bc))
-        hp_grads.append(rest_sum[model + 8 * bc :].reshape(8, LANES))
-        per = model // (groups * shards)
-        in_gain_grads.append(
-            lax.dynamic_slice_in_dim(gain_all, (at_d * groups + at_t) * per, per, 0)
-        )
+        prm_grads.append(g_prm)
+        cbc_grads.append(g_cbc)
+        hp_grads.append(g_hp)
 
     def stacked(items):
         return jnp.stack(items[::-1], axis=0)
 
-    grad_w_zx = jnp.stack([stacked([b[0] for b in big]), stacked([b[1] for b in big])], axis=2)
-    grad_w_out = stacked([b[2] for b in big])
-    grad_w_bcdt = stacked(shared_grads)
-    grad_in_gain = stacked(in_gain_grads)
-    mine = stacked(prm_grads)
-    cbc_all = stacked(cbc_grads)
-    hp_all = stacked(hp_grads)
+    x_done = jnp.concatenate([chains[0][0], chains[1][0]], axis=1)
+    z_done, o_done = chains[2][0], chains[3][0]
+    done = [jnp.concatenate([z_done, o_done, x_done], axis=0), later_sum.astype(f32)]
+
+    g_prm = stacked(prm_grads).swapaxes(0, 1)
+    g_prm = scatter_rest(*scatter_start(g_prm, ("tensor",)), tb, f32)
+    rest_sum = jnp.concatenate(
+        [
+            stacked(gain_grads).reshape(-1),
+            stacked(cbc_grads).reshape(-1),
+            stacked(hp_grads).reshape(-1),
+        ]
+    )
+    rest_sum = all_sum(rest_sum.reshape(-1, width), tb)
+    rest_sum = all_sum(jnp.concatenate([g_prm.reshape(-1, width), rest_sum], axis=0), db)
+    mine = rest_sum[: 8 * layers].reshape(layers, 8, width)
+    flat = rest_sum[8 * layers :].reshape(-1)
+    gain_all = flat[: layers * model].reshape(layers, model)
+    flat = flat[layers * model :]
+    cbc_all = flat[: layers * 8 * bc].reshape(layers, 8, bc)
+    hp_all = flat[layers * 8 * bc :].reshape(layers, 8, LANES)
+    per = model // (groups * shards)
+    grad_in_gain = lax.dynamic_slice_in_dim(gain_all, (at_d * groups + at_t) * per, per, 1)
     heads_mine = lax.dynamic_slice_in_dim(hp_all, at_t * own, own, 2)
+    grad_w_zx = jnp.stack(
+        [jnp.stack([d[:depth], d[2 * depth : 3 * depth]], axis=1) for d in done], axis=0
+    )
+    grad_w_out = jnp.stack([d[depth : 2 * depth] for d in done], axis=0)
+    grad_w_bcdt = jnp.stack([d[3 * depth :, : bc + heads] for d in done], axis=0)
     return (
         stream,
         grad,

time: 841 us -> 693 us (0.82)
  blocking collectives: 97.3 us -> 5.43 us
  waiting for transfers between devices: 212 us -> 164 us
  local copies, waits for them, and re-layouts: 120 us -> 108 us
  starting transfers between devices: 74.5 us -> 83.9 us
    all_gather x3 -> x0, blocking collectives: 90.8 us -> none  [the longest x2 68.6 us: body(): wb = lax.all_gather(w_bcdt[i], 'dp', axis=0, tiled=True)]
    ppermute x54 -> x42, waiting for transfers between devices: 168 us -> 113 us  [exchange(): lax.ppermute(x, axis, [(i, i ^ 1 << bit) for i in range(lax.axis_size(axi...]
    dynamic_slice x12 -> x5, local copies, waits for them, and re-layouts: 28.6 us -> 1.83 us  [the longest x2 0.86 us: scatter_step(): x = lax.dynamic_index_in_dim(x, mine, names.index(pair), False)]
    ppermute x8, starting transfers between devices: 12.5 us -> 26.4 us  [carry_states(): other, other_factor = unpack(lax.ppermute(packed, axis, pairs))]
    ppermute x8, waiting for transfers between devices: 37.8 us -> 51.4 us  [carry_states(): other, other_factor = unpack(lax.ppermute(packed, axis, pairs))]
    slice x18 -> x21, local copies, waits for them, and re-layouts: 9.99 us -> 22.8 us  [the longest x2 7.71 us: body(): g_zo[:, :, depth:]]
    convert_element_type x32, other arithmetic: 20.2 us -> 33 us  [the longest x21 26.1 us: scatter_step(): x = (x.astype(f32) + got.astype(f32)).astype(kind)]
    optimization_barrier x0 -> x4, local copies, waits for them, and re-layouts: none -> 11.7 us  [the longest x1 3.22 us: body(): sends, later = lax.optimization_barrier((sends, later))]
  transfers between devices with their start and end apart: 68 -> 57, of which waited for: 32 -> 24; matrix products, arithmetic and copies ran while one was open for 22% -> 22% of each run, Pallas kernels for 13% -> 26%
where the time goes in v2:
time: 693 us; the launch traced here: 685 us
  Pallas kernels  213 us (31%)
  waiting for transfers between devices  164 us (24%)
  local copies, waits for them, and re-layouts  108 us (16%)
  other arithmetic  93.5 us (13%)
  starting transfers between devices  83.9 us (12%)
  between operations  16 us (2%)
    ppermute x42, waiting for transfers between devices, exchange(): lax.ppermute(x, axis, [(i, i ^ 1 << bit) for i in range(lax.axis_size(axi...  113 us
    pallas_call x2, Pallas kernels, body(): pl.pallas_call(partial(scan_back_kernel, heads, own, taps_n, len(w_x[i]))...  94.4 us
    ppermute x8, waiting for transfers between devices, carry_states(): other, other_factor = unpack(lax.ppermute(packed, axis, pairs))  51.4 us
    ppermute x42, starting transfers between devices, exchange(): lax.ppermute(x, axis, [(i, i ^ 1 << bit) for i in range(lax.axis_size(axi...  50.4 us
    pallas_call x2, Pallas kernels, body(): pl.pallas_call(partial(scan_in_kernel, heads, own, taps_n, len(w_x[i])),...  45.7 us
    pallas_call x2, Pallas kernels, body(): pl.pallas_call(partial(gate_back_kernel, heads, own, full), grid=(groups,...  41.8 us
    pallas_call x2, Pallas kernels, body(): pl.pallas_call(partial(gate_kernel, heads, own, full), grid=(groups,), in...  31.4 us
    ppermute x8, starting transfers between devices, carry_states(): other, other_factor = unpack(lax.ppermute(packed, axis, pairs))  26.4 us
  transfers between devices with their start and end apart: 57, of which 24 were waited for; matrix products, arithmetic and copies ran while one was open for 22% of the time, Pallas kernels for 26%

profile of v2, /device:TPU:0, one launch (start us, length us, event | category | flops | bytes accessed | tf_op | source)
XLA Modules:
  0.0 684.7 jit_solution(10483942109031220419)
XLA Ops:
  17.1 5.4 all-gather.1
  28.2 7.6 %collective-permute-done = bf16[160,256]{1,0:T(8,128)(2,1)S(1)} collective-permute-done((bf16[160,256]{1,0:T(8,128)(2,1)S(1)}, bf16[160,256]{1,0:T(8,128)(2,1)S(1)}, u32[]{:S(2)}, u32[]{:S(2)}) %collective-permute-start) | collective-permute-done | bytes 81952 | tf_op jit(solution)/shard_map/ppermute | solution.py:592
  35.9 11.3 %collective-permute-done.7 = bf16[2,160,256]{2,1,0:T(8,128)(2,1)S(1)} collective-permute-done((bf16[2,160,256]{2,1,0:T(8,128)(2,1)S(1)}, bf16[2,160,256]{2,1,0:T(8,128)(2,1)S(1)}, u32[]{:S(2)}, u32[]{:S(2)}) %collective-permute-start.7) | collective-permute-done | bytes 163872 | tf_op jit(solution)/shard_map/ppermute | solution.py:592
  52.8 6.5 collective-permute-done.8
  61.8 6.7 collective-permute-done.2
  71.0 16.1 %collective-permute-done.9 = bf16[2,2,2,160,256]{4,3,1,0,2:T(8,128)(2,1)} collective-permute-done((bf16[2,2,2,160,256]{4,3,1,0,2:T(8,128)(2,1)S(1)}, bf16[2,2,2,160,256]{4,3,1,0,2:T(8,128)(2,1)}, u32[]{:S(2)}, u32[]{:S(2)}) %collective-permute-start.9) | collective-permute-done | bytes 655392 | tf_op jit(solution)/shard_map/ppermute | solution.py:592
  118.0 23.0 %scan_in.2 = (f32[512,2048]{1,0:T(8,128)}, f32[528,2048]{1,0:T(8,128)}, bf16[144,2048]{1,0:T(8,128)(2,1)}, f32[8,2048]{1,0:T(8,128)}, f32[528,384]{1,0:T(8,128)}...) custom-call(bf16[528,1024]{1,0:T(8,128)(2,1)} %copy.151.nrm, ...), custom_call_target="tpu_custom_call" | custom-call | flops 7889485824 | bytes 12582912 | tf_op jit(solution)/shard_map/scan_in/pallas_call | solution.py:818
  141.1 5.6 collective-permute-start.11
  154.6 13.1 %collective-permute-done.12 = bf16[144,2048]{1,0:T(8,128)(2,1)S(1)} collective-permute-done((bf16[144,2048]{1,0:T(8,128)(2,1)}, bf16[144,2048]{1,0:T(8,128)(2,1)S(1)}, u32[]{:S(2)}, u32[]{:S(2)}) %collective-permute-start.12) | collective-permute-done | bytes 589856 | tf_op jit(solution)/shard_map/ppermute | solution.py:647
  172.0 15.8 %gate.2 = (f32[512,2048]{1,0:T(8,128)}, f32[512,2048]{1,0:T(8,128)}, f32[512,1024]{1,0:T(8,128)}, f32[512,128]{1,0:T(8,128)}, f32[512,1024]{1,0:T(8,128)}) custom-call(bf16[528,1024]{1,0:T(8,128)(2,1)} %copy.151.nrm, bf16[4,8,416,512]{3,2,1,0:T(8,128)(2,1)} %bitcast.345, bf16[4,8,416,512]{3,2,1,0:T(8,128)(2,1)} %bitcast.346, ...), custom_call_target="tpu_custom_call" | custom-call | flops 4294967296 | bytes 20971520 | tf_op jit(solution)/shard_map/gate/pallas_call | solution.py:856
  203.8 22.7 %scan_in.3 = (f32[512,2048]{1,0:T(8,128)}, f32[528,2048]{1,0:T(8,128)}, bf16[144,2048]{1,0:T(8,128)(2,1)}, f32[8,2048]{1,0:T(8,128)}, f32[528,384]{1,0:T(8,128)}...) custom-call(bf16[528,1024]{1,0:T(8,128)(2,1)} %copy.159.nrm, ...), custom_call_target="tpu_custom_call" | custom-call | flops 7889485824 | bytes 12582912 | tf_op jit(solution)/shard_map/scan_in/pallas_call | solution.py:818
  226.5 8.2 %collective-permute-start.14 = (bf16[144,2048]{1,0:T(8,128)(2,1)}, bf16[144,2048]{1,0:T(8,128)(2,1)}, u32[]{:S(2)}, u32[]{:S(2)}) collective-permute-start(bf16[144,2048]{1,0:T(8,128)(2,1)} %get-tuple-element.164), channel_id=1, source_target_pairs={{0,1},{1,0},{2,3},{3,2},{4,5},{5,4},{6,7},{7,6},{8,9},{9,8},{10,11... | collective-permute-start | bytes 1769480 | tf_op jit(solution)/shard_map/ppermute | solution.py:647
  250.8 9.7 %collective-permute-done.15 = bf16[144,2048]{1,0:T(8,128)(2,1)S(1)} collective-permute-done((bf16[144,2048]{1,0:T(8,128)(2,1)S(1)}, bf16[144,2048]{1,0:T(8,128)(2,1)S(1)}, u32[]{:S(2)}, u32[]{:S(2)}) %collective-permute-start.15) | collective-permute-done | bytes 589856 | tf_op jit(solution)/shard_map/ppermute | solution.py:647
  261.5 15.6 %gate.3 = (f32[512,2048]{1,0:T(8,128)}, f32[512,2048]{1,0:T(8,128)}, f32[512,1024]{1,0:T(8,128)}, f32[512,128]{1,0:T(8,128)}, f32[512,1024]{1,0:T(8,128)}) custom-call(bf16[528,1024]{1,0:T(8,128)(2,1)} %copy.159.nrm, bf16[4,8,256,512]{3,2,1,0:T(8,128)(2,1)} %bitcast.351, bf16[4,8,256,512]{3,2,1,0:T(8,128)(2,1)} %bitcast.352, ...), custom_call_target="tpu_custom_call" | custom-call | flops 4294967296 | bytes 20971520 | tf_op jit(solution)/shard_map/gate/pallas_call | solution.py:856
  277.1 20.9 %gate_back.2 = (bf16[4,8,256,512]{3,2,1,0:T(8,128)(2,1)}, f32[512,2048]{1,0:T(8,128)}, f32[512,1024]{1,0:T(8,128)}, bf16[144,2048]{1,0:T(8,128)(2,1)}, f32[8,2048]{1,0:T(8,128)}) custom-call(bf16[512,1024]{1,0:T(8,128)(2,1)} %copy.161.dbr, bf16[1024,512]{1,0:T(8,128)(2,1)} %convert_bitcast_fusion.1.dbrt, f32[512,1024]{1,0:T(8,128)} %get-tuple-element.166.branch, ...), custom_call_target="tpu_custom_call" | custom-call | flops 8589934592 | bytes 25165824 | tf_op jit(solution)/shard_map/gate_back/pallas_call | solution.py:909
  309.8 16.3 %collective-permute-done.17 = bf16[144,2048]{1,0:T(8,128)(2,1)} collective-permute-done((bf16[144,2048]{1,0:T(8,128)(2,1)}, bf16[144,2048]{1,0:T(8,128)(2,1)}, u32[]{:S(2)}, u32[]{:S(2)}) %collective-permute-start.17) | collective-permute-done | bytes 589856 | tf_op jit(solution)/shard_map/ppermute | solution.py:647
  337.7 47.2 %scan_back.2 = (bf16[4,8,160,512]{3,2,1,0:T(8,128)(2,1)}, f32[1024,384]{1,0:T(8,128)}, f32[528,1024]{1,0:T(8,128)}, f32[4,8,512]{2,1,0:T(8,128)}, f32[8,256]{1,0:T(8,128)}, /*index=5*/f32[8,128]{1,0:T(8,128)}) custom-call(f32[528,2048]{1,0:T(8,128)} %get-tuple-element.172.xin, f32[512,2048]{1,0:T(8,128)} %get-tuple-element.173.dy_in, ...), custom_call_target="tpu_custom_call" | custom-call | flops 8589934592 | bytes 25165824 | tf_op jit(solution)/shard_map/scan_back/pallas_call | solution.py:972
  410.6 6.6 collective-permute-start.24
  422.3 20.9 %gate_back.3 = (bf16[4,8,256,512]{3,2,1,0:T(8,128)(2,1)}, f32[512,2048]{1,0:T(8,128)}, f32[512,1024]{1,0:T(8,128)}, bf16[144,2048]{1,0:T(8,128)(2,1)}, f32[8,2048]{1,0:T(8,128)}) custom-call(bf16[512,1024]{1,0:T(8,128)(2,1)} %copy.170.dbr, bf16[1024,512]{1,0:T(8,128)(2,1)} %bitcast.370, f32[512,1024]{1,0:T(8,128)} %get-tuple-element.198.branch, ...), custom_call_target="tpu_custom_call" | custom-call | flops 8589934592 | bytes 25165824 | tf_op jit(solution)/shard_map/gate_back/pallas_call | solution.py:909
  458.9 11.8 %collective-permute-done.26 = bf16[144,2048]{1,0:T(8,128)(2,1)S(1)} collective-permute-done((bf16[144,2048]{1,0:T(8,128)(2,1)S(1)}, bf16[144,2048]{1,0:T(8,128)(2,1)S(1)}, u32[]{:S(2)}, u32[]{:S(2)}) %collective-permute-start.26) | collective-permute-done | bytes 589856 | tf_op jit(solution)/shard_map/ppermute | solution.py:647
  476.4 47.2 %scan_back.3 = (bf16[4,8,160,512]{3,2,1,0:T(8,128)(2,1)}, f32[1024,384]{1,0:T(8,128)}, f32[528,1024]{1,0:T(8,128)}, f32[4,8,512]{2,1,0:T(8,128)}, f32[8,256]{1,0:T(8,128)}, /*index=5*/f32[8,128]{1,0:T(8,128)}) custom-call(f32[528,2048]{1,0:T(8,128)} %get-tuple-element.210.xin, f32[512,2048]{1,0:T(8,128)} %get-tuple-element.211.dy_in, ...), custom_call_target="tpu_custom_call" | custom-call | flops 8589934592 | bytes 25165824 | tf_op jit(solution)/shard_map/scan_back/pallas_call | solution.py:972
  598.5 18.6 %collective-permute-done.40 = bf16[2,2,128,512]{3,2,0,1:T(8,128)(2,1)} collective-permute-done((bf16[2,2,128,512]{3,2,0,1:T(8,128)(2,1)}, bf16[2,2,128,512]{3,2,0,1:T(8,128)(2,1)}, u32[]{:S(2)}, u32[]{:S(2)}) %collective-permute-start.40) | collective-permute-done | bytes 524320 | tf_op jit(solution)/shard_map/ppermute | solution.py:592
  644.6 16.9 %collective-permute-done.51 = bf16[128,512]{1,0:T(8,128)(2,1)S(1)} collective-permute-done((bf16[128,512]{1,0:T(8,128)(2,1)S(1)}, bf16[128,512]{1,0:T(8,128)(2,1)S(1)}, u32[]{:S(2)}, u32[]{:S(2)}) %collective-permute-start.51) | collective-permute-done | bytes 131104 | tf_op jit(solution)/shard_map/ppermute | solution.py:592
  661.6 5.2 collective-permute-done.50
  (531 shorter events, 289.7 us)
Async XLA Ops:
  7.2 161.5 %all-gather.6.cloned.1.call-start = ((), (), s32[]{:S(2)}) async-start(), calls=%async_computation.2 | async-start | bytes 14057472 | tf_op jit(solution)/shard_map/all_gather | solution.py:745
  12.5 249.0 %all-gather.8.cloned.1.call-start = ((), (), s32[]{:S(2)}) async-start(), calls=%async_computation.3 | async-start | bytes 8650752 | tf_op jit(solution)/shard_map/all_gather | solution.py:745
  16.8 656.5 %reduce-scatter.2.cloned.1.call-start = ((), (), s32[]{:S(2)}) async-start(), calls=%async_computation.1 | async-start | bytes 3833856 | tf_op jit(solution)/shard_map/reduce_scatter | solution.py:953
  25.1 22.1 %collective-permute-start.7 = (bf16[2,160,256]{2,1,0:T(8,128)(2,1)S(1)}, bf16[2,160,256]{2,1,0:T(8,128)(2,1)S(1)}, u32[]{:S(2)}, u32[]{:S(2)}) collective-permute-start(bf16[2,160,256]{2,1,0:T(8,128)(2,1)S(1)} %pad_maximum_fusion.19), channel_id=1, source_target_pairs={{0,16},{4,20},{8,24},{12,28},{16,0},{20,4},{24,8},{28,12},{1,17},{... | collective-permute-start | bytes 491528 | tf_op jit(solution)/shard_map/ppermute | solution.py:592
  59.4 27.7 %collective-permute-start.9 = (bf16[2,2,2,160,256]{4,3,1,0,2:T(8,128)(2,1)S(1)}, bf16[2,2,2,160,256]{4,3,1,0,2:T(8,128)(2,1)}, u32[]{:S(2)}, u32[]{:S(2)}) collective-permute-start(bf16[2,2,2,160,256]{4,3,1,0,2:T(8,128)(2,1)S(1)} %pad_maximum_fusion.13), channel_id=1, source_target_pairs={{0,2},{1,3},{2,0},{3,1},{4,6},{5,7},{6,4},{7,5},{8,10},{9,11},{10,... | collective-permute-start | bytes 1966088 | tf_op jit(solution)/shard_map/ppermute | solution.py:592
  69.5 23.2 %collective-permute-start.3 = (bf16[2,2,2,160,256]{4,3,2,1,0:T(8,128)(2,1)}, bf16[2,2,2,160,256]{4,3,2,1,0:T(8,128)(2,1)}, u32[]{:S(2)}, u32[]{:S(2)}) collective-permute-start(bf16[2,2,2,160,256]{4,3,2,1,0:T(8,128)(2,1)} %pad_maximum_fusion.12), channel_id=1, source_target_pairs={{0,4},{4,0},{8,12},{12,8},{16,20},{20,16},{24,28},{28,24},{1,5},{5... | collective-permute-start | bytes 1966088 | tf_op jit(solution)/shard_map/ppermute | solution.py:592
  149.9 17.8 %collective-permute-start.12 = (bf16[144,2048]{1,0:T(8,128)(2,1)}, bf16[144,2048]{1,0:T(8,128)(2,1)S(1)}, u32[]{:S(2)}, u32[]{:S(2)}) collective-permute-start(bf16[144,2048]{1,0:T(8,128)(2,1)} %maximum_maximum_fusion), channel_id=1, source_target_pairs={{0,2},{1,3},{4,6},{5,7},{8,10},{9,11},{12,14},{13,15},{16,18},{17,... | collective-permute-start | bytes 1769480 | tf_op jit(solution)/shard_map/ppermute | solution.py:647
  243.0 17.5 %collective-permute-start.15 = (bf16[144,2048]{1,0:T(8,128)(2,1)S(1)}, bf16[144,2048]{1,0:T(8,128)(2,1)S(1)}, u32[]{:S(2)}, u32[]{:S(2)}) collective-permute-start(bf16[144,2048]{1,0:T(8,128)(2,1)S(1)} %maximum_maximum_fusion.1), channel_id=1, source_target_pairs={{0,2},{1,3},{4,6},{5,7},{8,10},{9,11},{12,14},{13,15},{16,18},{17,... | collective-permute-start | bytes 1769480 | tf_op jit(solution)/shard_map/ppermute | solution.py:647
  303.8 24.3 %collective-permute-start.18 = (bf16[2,2,2,2,128,512]{5,4,3,2,1,0:T(8,128)(2,1)}, bf16[2,2,2,2,128,512]{5,4,3,2,1,0:T(8,128)(2,1)}, u32[]{:S(2)}, u32[]{:S(2)}) collective-permute-start(bf16[2,2,2,2,128,512]{5,4,3,2,1,0:T(8,128)(2,1)} %dynamic-slice_bitcast_fusion.2), channel_id=1, source_target_pairs={{0,1},{1,0},{2,3},{3,2},{4,5},{5,4},{6,7},{7,6},{8,9},{9,8},{10,11... | collective-permute-start | bytes 6291464 | tf_op jit(solution)/shard_map/ppermute | solution.py:592
  306.6 24.7 %collective-permute-start.19 = (bf16[2,2,2,2,128,512]{5,4,3,2,1,0:T(8,128)(2,1)}, bf16[2,2,2,2,128,512]{5,4,3,2,1,0:T(8,128)(2,1)}, u32[]{:S(2)}, u32[]{:S(2)}) collective-permute-start(bf16[2,2,2,2,128,512]{5,4,3,2,1,0:T(8,128)(2,1)} %dynamic-slice_bitcast_fusion.1), channel_id=1, source_target_pairs={{0,1},{1,0},{2,3},{3,2},{4,5},{5,4},{6,7},{7,6},{8,9},{9,8},{10,11... | collective-permute-start | bytes 6291464 | tf_op jit(solution)/shard_map/ppermute | solution.py:592
  308.5 17.6 %collective-permute-start.17 = (bf16[144,2048]{1,0:T(8,128)(2,1)}, bf16[144,2048]{1,0:T(8,128)(2,1)}, u32[]{:S(2)}, u32[]{:S(2)}) collective-permute-start(bf16[144,2048]{1,0:T(8,128)(2,1)} %maximum_maximum_fusion.2), channel_id=1, source_target_pairs={{2,0},{3,1},{6,4},{7,5},{10,8},{11,9},{14,12},{15,13},{18,16},{19,... | collective-permute-start | bytes 1769480 | tf_op jit(solution)/shard_map/ppermute | solution.py:647
  335.6 49.3 %collective-permute-start.20 = (bf16[2,2,2,128,512]{4,3,2,1,0:T(8,128)(2,1)S(1)}, bf16[2,2,2,128,512]{4,3,2,1,0:T(8,128)(2,1)S(1)}, u32[]{:S(2)}, u32[]{:S(2)}) collective-permute-start(bf16[2,2,2,128,512]{4,3,2,1,0:T(8,128)(2,1)S(1)} %dynamic-slice_bitcast_fusion.7), channel_id=1, source_target_pairs={{0,2},{1,3},{2,0},{3,1},{4,6},{5,7},{6,4},{7,5},{8,10},{9,11},{10,... | collective-permute-start | bytes 3145736 | tf_op jit(solution)/shard_map/ppermute | solution.py:592
  335.6 49.3 %collective-permute-start.21 = (bf16[2,2,2,128,512]{4,3,2,1,0:T(8,128)(2,1)S(1)}, bf16[2,2,2,128,512]{4,3,2,1,0:T(8,128)(2,1)S(1)}, u32[]{:S(2)}, u32[]{:S(2)}) collective-permute-start(bf16[2,2,2,128,512]{4,3,2,1,0:T(8,128)(2,1)S(1)} %dynamic-slice_bitcast_fusion.6), channel_id=1, source_target_pairs={{0,2},{1,3},{2,0},{3,1},{4,6},{5,7},{6,4},{7,5},{8,10},{9,11},{10,... | collective-permute-start | bytes 3145736 | tf_op jit(solution)/shard_map/ppermute | solution.py:592
  410.6 35.6 %collective-permute-start.24 = (bf16[2,2,2,160,512]{4,3,2,1,0:T(8,128)(2,1)}, bf16[2,2,2,160,512]{4,3,2,1,0:T(8,128)(2,1)}, u32[]{:S(2)}, u32[]{:S(2)}) collective-permute-start(bf16[2,2,2,160,512]{4,3,2,1,0:T(8,128)(2,1)} %dynamic-slice_bitcast_fusion.3), channel_id=1, source_target_pairs={{0,2},{1,3},{2,0},{3,1},{4,6},{5,7},{6,4},{7,5},{8,10},{9,11},{10,... | collective-permute-start | bytes 3932168 | tf_op jit(solution)/shard_map/ppermute | solution.py:592
  451.5 20.2 %collective-permute-start.27 = (bf16[2,2,2,2,128,512]{5,4,1,2,3,0:T(8,128)(2,1)S(1)}, bf16[2,2,2,2,128,512]{5,4,1,2,3,0:T(8,128)(2,1)S(1)}, u32[]{:S(2)}, u32[]{:S(2)}) collective-permute-start(bf16[2,2,2,2,128,512]{5,4,1,2,3,0:T(8,128)(2,1)S(1)} %bitcast.387), channel_id=1, source_target_pairs={{0,1},{1,0},{2,3},{3,2},{4,5},{5,4},{6,7},{7,6},{8,9},{9,8},{10,11... | collective-permute-start | bytes 6291464 | tf_op jit(solution)/shard_map/ppermute | solution.py:592
  452.2 20.3 %collective-permute-start.28 = (bf16[2,2,2,2,128,512]{5,4,1,2,0,3:T(8,128)(2,1)S(1)}, bf16[2,2,2,2,128,512]{5,4,1,2,0,3:T(8,128)(2,1)S(1)}, u32[]{:S(2)}, u32[]{:S(2)}) collective-permute-start(bf16[2,2,2,2,128,512]{5,4,1,2,0,3:T(8,128)(2,1)S(1)} %bitcast.388), channel_id=1, source_target_pairs={{0,1},{1,0},{2,3},{3,2},{4,5},{5,4},{6,7},{7,6},{8,9},{9,8},{10,11... | collective-permute-start | bytes 6291464 | tf_op jit(solution)/shard_map/ppermute | solution.py:592
  474.6 49.0 %collective-permute-start.29 = (bf16[2,2,2,128,512]{4,3,0,1,2:T(8,128)(2,1)S(1)}, bf16[2,2,2,128,512]{4,3,0,1,2:T(8,128)(2,1)S(1)}, u32[]{:S(2)}, u32[]{:S(2)}) collective-permute-start(bf16[2,2,2,128,512]{4,3,0,1,2:T(8,128)(2,1)S(1)} %dynamic-slice_bitcast_fusion.5), channel_id=1, source_target_pairs={{0,2},{1,3},{2,0},{3,1},{4,6},{5,7},{6,4},{7,5},{8,10},{9,11},{10,... | collective-permute-start | bytes 3145736 | tf_op jit(solution)/shard_map/ppermute | solution.py:592
  474.7 48.9 %collective-permute-start.30 = (bf16[2,2,2,128,512]{4,3,1,2,0:T(8,128)(2,1)S(1)}, bf16[2,2,2,128,512]{4,3,1,2,0:T(8,128)(2,1)S(1)}, u32[]{:S(2)}, u32[]{:S(2)}) collective-permute-start(bf16[2,2,2,128,512]{4,3,1,2,0:T(8,128)(2,1)S(1)} %dynamic-slice_bitcast_fusion.4), channel_id=1, source_target_pairs={{0,4},{4,0},{8,12},{12,8},{16,20},{20,16},{24,28},{28,24},{1,5},{5... | collective-permute-start | bytes 3145736 | tf_op jit(solution)/shard_map/ppermute | solution.py:592
  578.1 41.4 %collective-permute-start.41 = (bf16[2,2,2,160,256]{4,3,0,1,2:T(8,128)(2,1)}, bf16[2,2,2,160,256]{4,3,0,1,2:T(8,128)(2,1)}, u32[]{:S(2)}, u32[]{:S(2)}) collective-permute-start(bf16[2,2,2,160,256]{4,3,0,1,2:T(8,128)(2,1)} %dynamic-slice_bitcast_fusion.9), channel_id=1, source_target_pairs={{0,2},{1,3},{2,0},{3,1},{4,6},{5,7},{6,4},{7,5},{8,10},{9,11},{10,... | collective-permute-start | bytes 1966088 | tf_op jit(solution)/shard_map/ppermute | solution.py:592
  579.9 41.0 %collective-permute-start.42 = (bf16[2,2,2,160,256]{4,3,1,2,0:T(8,128)(2,1)}, bf16[2,2,2,160,256]{4,3,1,2,0:T(8,128)(2,1)}, u32[]{:S(2)}, u32[]{:S(2)}) collective-permute-start(bf16[2,2,2,160,256]{4,3,1,2,0:T(8,128)(2,1)} %dynamic-slice_bitcast_fusion.8), channel_id=1, source_target_pairs={{0,4},{4,0},{8,12},{12,8},{16,20},{20,16},{24,28},{28,24},{1,5},{5... | collective-permute-start | bytes 1966088 | tf_op jit(solution)/shard_map/ppermute | solution.py:592
  581.5 35.6 %collective-permute-start.40 = (bf16[2,2,128,512]{3,2,0,1:T(8,128)(2,1)}, bf16[2,2,128,512]{3,2,0,1:T(8,128)(2,1)}, u32[]{:S(2)}, u32[]{:S(2)}) collective-permute-start(bf16[2,2,128,512]{3,2,0,1:T(8,128)(2,1)} %dynamic-slice_bitcast_fusion.11), channel_id=1, source_target_pairs={{0,4},{4,0},{8,12},{12,8},{16,20},{20,16},{24,28},{28,24},{1,5},{5... | collective-permute-start | bytes 1572872 | tf_op jit(solution)/shard_map/ppermute | solution.py:592
  581.9 36.4 %collective-permute-start.43 = (bf16[2,2,128,512]{3,2,0,1:T(8,128)(2,1)}, bf16[2,2,128,512]{3,2,0,1:T(8,128)(2,1)}, u32[]{:S(2)}, u32[]{:S(2)}) collective-permute-start(bf16[2,2,128,512]{3,2,0,1:T(8,128)(2,1)} %dynamic-slice_bitcast_fusion.10), channel_id=1, source_target_pairs={{0,2},{1,3},{2,0},{3,1},{4,6},{5,7},{6,4},{7,5},{8,10},{9,11},{10,... | collective-permute-start | bytes 1572872 | tf_op jit(solution)/shard_map/ppermute | solution.py:592
  642.5 19.0 %collective-permute-start.49 = (bf16[2,160,256]{2,1,0:T(8,128)(2,1)S(1)}, bf16[2,160,256]{2,1,0:T(8,128)(2,1)S(1)}, u32[]{:S(2)}, u32[]{:S(2)}) collective-permute-start(bf16[2,160,256]{2,1,0:T(8,128)(2,1)S(1)} %dynamic-slice_bitcast_fusion.17), channel_id=1, source_target_pairs={{0,8},{4,12},{8,0},{12,4},{16,24},{20,28},{24,16},{28,20},{1,9},{5... | collective-permute-start | bytes 491528 | tf_op jit(solution)/shard_map/ppermute | solution.py:592
  642.8 24.0 %collective-permute-start.50 = (bf16[2,160,256]{2,1,0:T(8,128)(2,1)S(1)}, bf16[2,160,256]{2,1,0:T(8,128)(2,1)S(1)}, u32[]{:S(2)}, u32[]{:S(2)}) collective-permute-start(bf16[2,160,256]{2,1,0:T(8,128)(2,1)S(1)} %dynamic-slice_bitcast_fusion.16), channel_id=1, source_target_pairs={{0,8},{4,12},{8,0},{12,4},{16,24},{20,28},{24,16},{28,20},{1,9},{5... | collective-permute-start | bytes 491528 | tf_op jit(solution)/shard_map/ppermute | solution.py:592
  (106 other events, 674.9 us)
Sparse Core Ops, SparseCore 0:
  12.6 125.7 all-gather.5
  141.4 78.4 all-gather.7
  572.5 96.1 reduce-scatter.1

commit v3 on v2

--- a/solution.py
+++ b/solution.py
@@ -111,7 +111,7 @@
     return ((row >= col) if lower else (row <= col)).astype(f32)
 
 
-def scan_in_kernel(heads, own, taps_n, pieces, nrm, *refs):
+def scan_in_kernel(heads, own, taps_n, pieces, halo, nrm, *refs):
     w, refs = refs[:pieces], refs[pieces:]
     (
         wb,
@@ -147,7 +147,7 @@
 
     @pl.when(group == 0)
     def _():
-        sh = mm(nrm[...], wb[...])
+        sh = jnp.concatenate([mm(halo[...], wb[...]), mm(nrm[...], wb[...])], axis=0)
         shared[...] = sh
         half = cbc.shape[1] // 2
         act = conv(sh[:, : 2 * half], cbc[...], keep, rows, taps_n)
@@ -187,8 +187,13 @@
             )
             m_scr[c] = jnp.where(ok, 0.0, NEG)
 
+    weight = [part[...].reshape(nrm.shape[1], -1) for part in w]
     ext = jnp.concatenate(
-        [mm(nrm[...], part[...].reshape(nrm.shape[1], -1)) for part in w], axis=1
+        [
+            jnp.concatenate([mm(source[...], part) for part in weight], axis=1)
+            for source in (halo, nrm)
+        ],
+        axis=0,
     )
     xin[...] = ext
     u = conv(ext, prm[0], keep, rows, taps_n)
@@ -251,7 +256,7 @@
 ):
     group = pl.program_id(0)
     width = y_loc.shape[1]
-    z = mm(nrm[HALO:], wz[...].reshape(-1, width))
+    z = mm(nrm[...], wz[...].reshape(-1, width))
     y = y_loc[...] + mm(fd[...], spread(group, heads, own, width)) * (
         lambda parts: mm(parts[0], s_in[...]) + mm(parts[1], s_in[...])
     )(two(c_in[...]))
@@ -365,7 +370,7 @@
     return sums, jnp.sum(du, axis=0, keepdims=True)
 
 
-def scan_back_kernel(heads, own, taps_n, pieces, xin, dy_in, y_in, s_in, ds_in, *refs):
+def scan_back_kernel(heads, own, taps_n, pieces, xin, dy_in, y_in, s_in, ds_in, dnz, *refs):
     w, refs = refs[:pieces], refs[pieces:]
     (
         wb,
@@ -504,7 +509,8 @@
 
     @pl.when(group == 0)
     def _():
-        dn[...] = part
+        dn[0:rows] = dnz[...] + part[:rows]
+        dn[rows:] = part[rows:]
 
     @pl.when(group > 0)
     def _():
@@ -548,7 +554,8 @@
                 axis=1,
             )
         )
-        g_b[...] = mm(nrmt[...], dsh)
+        g_b[...] = jnp.zeros_like(g_b)
+        g_b[:, : dsh.shape[1]] = low(mm(nrmt[...], dsh))
         dn[...] += mmt(dsh[: rows + HALO], wb[...])
 
 
@@ -625,7 +632,7 @@
     return x
 
 
-def carry_states(packed, axis, backward):
+def carry_states(packed, axis, backward, beside=lambda got: (got, None)):
     size, at = lax.axis_size(axis), lax.axis_index(axis)
     count = packed.shape[0] - HALO
 
@@ -644,7 +651,10 @@
         final = 2 * step >= size
         if final:
             pairs = [p for p in pairs if (p[0] > p[1]) == backward]
-        other, other_factor = unpack(lax.ppermute(packed, axis, pairs))
+        got = lax.ppermute(packed, axis, pairs)
+        if final:
+            got, beside = beside(got)
+        other, other_factor = unpack(got)
         prefix = jnp.where(follows, prefix_factor * other + prefix, prefix)
         if not final:
             prefix_factor = jnp.where(follows, prefix_factor * other_factor, prefix_factor)
@@ -655,7 +665,7 @@
                 [low(total), high, rest, jnp.zeros((HALO - 2, factor.shape[1]), bf16)], axis=0
             )
         step *= 2
-    return low(prefix)
+    return low(prefix), beside
 
 
 def body(
@@ -740,8 +750,10 @@
         own_rows = lax.dynamic_slice_in_dim(both, at_t * rows_b, rows_b, 0)
         return jnp.pad(own_rows, ((0, 0), (0, width - both.shape[1])))
 
-    def gather(pieces):
+    def gather(pieces, after=None):
         local = jnp.concatenate(pieces, axis=0)
+        if after is not None:
+            local, _ = lax.optimization_barrier((local, after))
         got = lax.all_gather(local, ("tensor", "dp"), axis=0, tiled=False)
         return got.reshape((groups, shards) + local.shape)
 
@@ -759,14 +771,12 @@
     first = jnp.concatenate([w_zx[0, :, 1], shared_rows(0)], axis=0)
     half = width // 2
     ring = db[1:] + db[:1]
-    first = [
-        spread_out(first[:, :half], ring + tb[1:] + tb[:1]),
-        spread_out(first[:, half:], ring[:-1] + tb[1:] + ring[-1:] + tb[:1]),
-    ]
+    right = spread_out(first[:, half:], ring[:-1] + tb[1:] + ring[-1:] + tb[:1])
+    first = [spread_out(first[:, :half], ring + tb[1:] + tb[:1]), right]
     head = gather(
         [w_zx[0, :, 0], w_out[0]]
         + [w_zx[i, :, 1] for i in range(1, layers)]
-        + [shared_rows(i) for i in range(1, layers)]
+        + [shared_rows(i) for i in range(1, layers)],
     )
     w_x = [[(part, 0) for part in first]] + [[(head, 1 + i)] for i in range(1, layers)]
     w_z, w_o = [(head, 0)], [(head, 1)]
@@ -809,7 +819,6 @@
         rinv = lax.rsqrt(jnp.mean(stream * stream, axis=-1, keepdims=True) + epsilon)
         normed = (stream * rinv * gains[i]).astype(bf16)
         before = shift(normed[rows - HALO :], "tensor", 1)
-        nrm = jnp.concatenate([before, normed], axis=0)
         nrmt = jnp.concatenate(
             [normed, before, jnp.zeros((LANES - HALO, model), bf16)], axis=0
         ).T
@@ -819,7 +828,8 @@
             partial(scan_in_kernel, heads, own, taps_n, len(w_x[i])),
             grid=(groups,),
             in_specs=[
-                whole((ext, model)),
+                whole((HALO, model)),
+                whole((rows, model)),
                 *[kind_block(depth, part) for part in w_x[i]],
                 whole((model, wide)),
                 prm_spec,
@@ -848,16 +858,16 @@
             ],
             name="scan_in",
             **params(3 * flops, 4 * rows * full * 3),
-        )(nrm, *[part for part, _ in w_x[i]], wb, pr, cbc[i], hp[i], segc, segr)
+        )(before, normed, *[part for part, _ in w_x[i]], wb, pr, cbc[i], hp[i], segc, segr)
         y_loc, xin, state, ftot = outs[:4]
         rest = outs[4:]
         shared, b_m, c_m, b_t, c_t, dtp, cumt, dts, es, fs, fd, cums = rest
-        s_in = carry_states(state, "tensor", False)
+        s_in, _ = carry_states(state, "tensor", False)
         z, y, branch, grms, nxt = pl.pallas_call(
             partial(gate_kernel, heads, own, full),
             grid=(groups,),
             in_specs=[
-                whole((ext, model)),
+                whole((rows, model)),
                 kind_block(depth, w_z[i]),
                 pl.BlockSpec((groups, shards, depth, width), lambda g, k=w_o[i][1]: (0, 0, k, 0)),
                 by_column(rows, width),
@@ -887,12 +897,32 @@
             ],
             name="gate",
             **params(4 * rows * model * full, 4 * rows * full * 5),
-        )(nrm, w_z[i][0], w_o[i][0], y_loc, c_m, fd, s_in, pr, stream)
+        )(normed, w_z[i][0], w_o[i][0], y_loc, c_m, fd, s_in, pr, stream)
         saved.append((stream, rinv, nrmt, xin, ftot, rest, s_in, z, y, branch, grms))
         stream = nxt
 
     def grad_block(count):
         return pl.BlockSpec((None, shards, count, width), lambda g: (g, 0, 0, 0))
+
+    def finish(i, grad, dn, after):
+        stream_in, rinv = saved[i][:2]
+        dnormed = jnp.concatenate(
+            [dn[: rows - HALO], dn[rows - HALO : rows] + after], axis=0
+        )
+        scaled_in = stream_in * rinv
+        gain_grads.append(jnp.sum(dnormed * scaled_in, axis=0))
+        scaled = dnormed * gains[i]
+        return grad + rinv * (
+            scaled - scaled_in * jnp.mean(scaled * scaled_in, axis=-1, keepdims=True)
+        )
+
+    def keep_small(g_gain, g_prm, g_cbc, g_hp):
+        prm_grads.append(g_prm.at[:, 5].set(g_gain[0].reshape(groups, width)))
+        cbc_grads.append(g_cbc)
+        hp_grads.append(g_hp)
+
+    def stacked(items):
+        return jnp.stack(items[::-1], axis=0)
 
     grad = cotangent
     x_part = None
@@ -945,17 +975,6 @@
             g_zo, dy, dnz, dstate, g_gain, x_got = lax.optimization_barrier(
                 (g_zo, dy, dnz, dstate, g_gain, x_got)
             )
-        ds_in = carry_states(dstate, "tensor", True)
-        if x_part is not None:
-            x_part, _ = scatter_step(x_part, x_names, tb[1], x_got)
-            later_sum = jnp.concatenate([z_part, o_part, x_part], axis=len(db))
-            ds_in, later_sum = lax.optimization_barrier((ds_in, later_sum))
-            later_sum = lax.psum_scatter(
-                later_sum.reshape((shards,) + later_sum.shape[len(db) :]),
-                "dp",
-                scatter_dimension=0,
-                tiled=False,
-            )
         chains = []
         for part, order in (
             (g_zo[:, :, :depth], order_x),
@@ -963,10 +982,22 @@
         ):
             part, names = scatter_step(*scatter_start(part, axes), order[0])
             chains.append((part, names, order[1], outgoing(part, names, order[1])))
-        (z_part, z_names, z_pair, z_send), (o_part, o_names, o_pair, o_send) = chains
-        ds_in, z_part, o_part, z_send, o_send = lax.optimization_barrier(
-            (ds_in, z_part, o_part, z_send, o_send)
+        (z_new, z_names, z_pair, z_send), (o_new, o_names, o_pair, o_send) = chains
+        held = [z_new, o_new, z_send, o_send]
+        if x_part is not None:
+            x_part, _ = scatter_step(x_part, x_names, tb[1], x_got)
+            held.append(jnp.concatenate([z_part, o_part, x_part], axis=len(db)))
+        ds_in, held = carry_states(
+            dstate, "tensor", True, lambda got: lax.optimization_barrier((got, held))
         )
+        z_part, o_part, z_send, o_send = held[:4]
+        if x_part is not None:
+            later_sum = lax.psum_scatter(
+                held[4].reshape((shards,) + held[4].shape[len(db) :]),
+                "dp",
+                scatter_dimension=0,
+                tiled=False,
+            )
         z_got = exchange(z_send, *z_pair)
         o_got = exchange(o_send, *o_pair)
         g_x, g_b, dn, g_prm, g_cbc, g_hp = pl.pallas_call(
@@ -978,6 +1009,7 @@
                 by_column(rows, width),
                 by_column(state_n, width),
                 by_column(state_n, width),
+                whole((rows, model)),
                 *[kind_block(depth, part) for part in w_x[i]],
                 whole((model, wide)),
                 prm_spec,
@@ -990,7 +1022,7 @@
             + [whole(s) for n, (s, _) in enumerate(small) if n != 10],
             out_specs=[
                 grad_block(depth),
-                whole((model, wide)),
+                whole((model, width)),
                 whole((ext, model)),
                 pl.BlockSpec((1, 8, width), lambda g: (g, 0, 0)),
                 whole((8, bc)),
@@ -998,7 +1030,7 @@
             ],
             out_shape=[
                 struct(groups, shards, depth + rows_b, width, dtype=bf16),
-                struct(model, wide),
+                struct(model, width, dtype=bf16),
                 struct(ext, model),
                 struct(groups, 8, width),
                 struct(8, bc),
@@ -1019,7 +1051,7 @@
             name="scan_back",
             **params(8 * rows * model * full, 4 * rows * full * 6),
         )(
-            xin, dy, y, s_in, ds_in, *[part for part, _ in w_x[i]], wb, pr, cbc[i], hp[i], segc, segr, nrmt,
+            xin, dy, y, s_in, ds_in, dnz, *[part for part, _ in w_x[i]], wb, pr, cbc[i], hp[i], segc, segr, nrmt,
             shared, b_m, c_m, b_t, c_t, dtp, cumt, dts, es, fs, cums,
         )
         g_x, g_b, dn, g_prm, g_cbc, g_hp, z_got, o_got = lax.optimization_barrier(
@@ -1027,77 +1059,93 @@
         )
         z_part, z_names = scatter_step(z_part, z_names, z_pair, z_got)
         o_part, o_names = scatter_step(o_part, o_names, o_pair, o_got)
-        parts_b = low(jnp.pad(g_b[:, : bc + heads], ((0, 0), (0, width - bc - heads))))
-        parts_b = jnp.moveaxis(parts_b.reshape(shards, groups, rows_b, width), 1, 0)
+        parts_b = jnp.moveaxis(g_b.reshape(shards, groups, rows_b, width), 1, 0)
         g_x = lax.dynamic_update_slice(g_x, parts_b, (0, 0, depth, 0))
         if i > 0:
             x_part, x_names = scatter_step(*scatter_start(g_x, axes), tb[0])
             x_send = outgoing(x_part, x_names, tb[1])
         else:
-            x_full, x_names = scatter_start(g_x, axes)
-            x_got = exchange(outgoing(x_full, x_names, tb[0]), *tb[0])
-            chains = []
-            for cut, order in ((slice(None, half), order_x), (slice(half, None), order_y)):
-                part, names = scatter_step(x_full[..., cut], x_names, tb[0], x_got[..., cut])
-                chains.append([part, names, list(order[1:])])
-            chains.append([z_part, z_names, list(order_x[2:])])
-            chains.append([o_part, o_names, [p for p in order_y if p in o_names]])
-            later = (dn, g_prm, g_cbc, g_hp, g_gain)
-            while any(order for _, _, order in chains):
-                sends = [
-                    outgoing(part, names, order[0]) if order else part for part, names, order in chains
-                ]
-                if later is None:
-                    sends = lax.optimization_barrier(sends)
-                else:
-                    sends, later = lax.optimization_barrier((sends, later))
-                    dn, g_prm, g_cbc, g_hp, g_gain = later
-                    later = None
-                gots = [
-                    exchange(send, *order[0]) if order else send
-                    for send, (_, _, order) in zip(sends, chains)
-                ]
-                for chain, got in zip(chains, gots):
-                    part, names, order = chain
-                    if order:
-                        kind = bf16 if len(order) > 1 else f32
-                        chain[0], chain[1] = scatter_step(part, names, order[0], got, kind)
-                        chain[2] = order[1:]
+            break
         after = shift(dn[rows:], "tensor", -1)
-        dnormed = dnz + dn[:rows]
-        dnormed = jnp.concatenate(
-            [dnormed[: rows - HALO], dnormed[rows - HALO :] + after], axis=0
-        )
-        scaled_in = stream_in * rinv
-        gain_grads.append(jnp.sum(dnormed * scaled_in, axis=0))
-        scaled = dnormed * gains[i]
-        grad = grad + rinv * (
-            scaled - scaled_in * jnp.mean(scaled * scaled_in, axis=-1, keepdims=True)
-        )
-
-        g_prm = g_prm.at[:, 5].set(g_gain[0].reshape(groups, width))
-        prm_grads.append(g_prm)
-        cbc_grads.append(g_cbc)
-        hp_grads.append(g_hp)
-
-    def stacked(items):
-        return jnp.stack(items[::-1], axis=0)
-
-    x_done = jnp.concatenate([chains[0][0], chains[1][0]], axis=1)
-    z_done, o_done = chains[2][0], chains[3][0]
-    done = [jnp.concatenate([z_done, o_done, x_done], axis=0), later_sum.astype(f32)]
-
-    g_prm = stacked(prm_grads).swapaxes(0, 1)
-    g_prm = scatter_rest(*scatter_start(g_prm, ("tensor",)), tb, f32)
+        grad = finish(i, grad, dn, after)
+        keep_small(g_gain, g_prm, g_cbc, g_hp)
+
+    def together(sends, pairs, beside=()):
+        sends = lax.optimization_barrier(sends)
+        gots = []
+        for send, pair in zip(sends, pairs):
+            if pair is None:
+                gots.append(shift(send, "tensor", -1))
+            elif len(pair) == 3:
+                size = lax.axis_size(pair[0])
+                gots.append(lax.ppermute(send, pair[0], [(k, k ^ pair[1]) for k in range(size)]))
+            else:
+                gots.append(exchange(send, *pair))
+        return lax.optimization_barrier([*gots, *beside])
+
+    keep_small(g_gain, g_prm, g_cbc, g_hp)
+    x_full, x_names = scatter_start(g_x, axes)
+    x_got, after = together([outgoing(x_full, x_names, tb[0]), dn[rows:]], [tb[0], None])
+    x_part, x_names = scatter_step(x_full, x_names, tb[0], x_got)
+    chains = [
+        [x_part[..., :half], x_names, list(order_x[1:])],
+        [x_part[..., half:], x_names, list(order_y[1:])],
+    ]
+    chains.append([z_part, z_names, list(order_x[2:])])
+    chains.append([o_part, o_names, [p for p in order_y if p in o_names]])
+    grad = finish(0, grad, dn, after)
     rest_sum = jnp.concatenate(
         [
             stacked(gain_grads).reshape(-1),
             stacked(cbc_grads).reshape(-1),
             stacked(hp_grads).reshape(-1),
         ]
-    )
-    rest_sum = all_sum(rest_sum.reshape(-1, width), tb)
-    rest_sum = all_sum(jnp.concatenate([g_prm.reshape(-1, width), rest_sum], axis=0), db)
+    ).reshape(-1, width)
+    small, small_names = scatter_start(stacked(prm_grads).swapaxes(0, 1), ("tensor",))
+    rounds = [[bit] for bit in tb + db[:-2]] + [db[-2:]]
+    while rounds or any(order for _, _, order in chains):
+        live = [chain for chain in chains if chain[2]]
+        bits = rounds.pop(0) if rounds else []
+        sends = [outgoing(part, names, order[0]) for part, names, order in live]
+        pairs = [order[0] for _, _, order in live]
+        beside = []
+        if bits and bits[0] in tb:
+            if bits[0] == tb[0]:
+                beside = [later_sum]
+            leaving = outgoing(small, small_names, bits[0])
+            sends.append(jnp.concatenate([leaving.reshape(-1, width), rest_sum], axis=0))
+            pairs.append(bits[0])
+        elif bits:
+            if small is not None:
+                rest_sum = jnp.concatenate([small.reshape(-1, width), rest_sum], axis=0)
+                small = None
+            steps = [0]
+            for _, bit in bits:
+                steps += [step | (1 << bit) for step in steps]
+            for step in steps[1:]:
+                sends.append(rest_sum)
+                pairs.append((bits[0][0], step, None))
+        gots = together(sends, pairs, beside)
+        if beside:
+            *gots, later_sum = gots
+        for chain, got in zip(live, gots):
+            part, names, order = chain
+            kind = f32 if len(order) == 1 else bf16
+            chain[0], chain[1] = scatter_step(part, names, order[0], got, kind)
+            chain[2] = order[1:]
+        gots = gots[len(live) :]
+        if bits and bits[0] in tb:
+            count = gots[0].shape[0] - rest_sum.shape[0]
+            kept_shape = outgoing(small, small_names, bits[0]).shape
+            arrived = gots[0][:count].reshape(kept_shape)
+            small, small_names = scatter_step(small, small_names, bits[0], arrived, f32)
+            rest_sum = rest_sum + gots[0][count:]
+        else:
+            for got in gots:
+                rest_sum = rest_sum + got
+    x_done = jnp.concatenate([chains[0][0], chains[1][0]], axis=1)
+    z_done, o_done = chains[2][0], chains[3][0]
+    done = [jnp.concatenate([z_done, o_done, x_done], axis=0), later_sum.astype(f32)]
     mine = rest_sum[: 8 * layers].reshape(layers, 8, width)
     flat = rest_sum[8 * layers :].reshape(-1)
     gain_all = flat[: layers * model].reshape(layers, model)

time: 693 us -> 648 us (0.935)
  other arithmetic: 93.5 us -> 73.7 us
  waiting for transfers between devices: 164 us -> 148 us
    ppermute x42 -> x37, waiting for transfers between devices: 113 us -> 94.1 us  [exchange(): lax.ppermute(x, axis, [(i, i ^ 1 << bit) for i in range(lax.axis_size(axi...]
    ppermute x42 -> x37, starting transfers between devices: 50.4 us -> 40.1 us  [exchange(): lax.ppermute(x, axis, [(i, i ^ 1 << bit) for i in range(lax.axis_size(axi...]
    add x10 -> x6, other arithmetic: 12.7 us -> 2.86 us  [the longest x1 1.95 us: finish(): grad + rinv * (scaled - scaled_in * jnp.mean(scaled * scaled_in, axis=-1,...]
    ppermute x8 -> x12, starting transfers between devices: 26.4 us -> 32.6 us  [the longest x8 26.8 us: carry_states(): got = lax.ppermute(packed, axis, pairs)]
    squeeze x25 -> x22, local copies, waits for them, and re-layouts: 17.3 us -> 12 us  [outgoing(): return lax.dynamic_index_in_dim(x, 1 - mine, names.index(pair), False)]
    ppermute x8 -> x12, waiting for transfers between devices: 51.4 us -> 53.6 us  [the longest x8 47.4 us: carry_states(): got = lax.ppermute(packed, axis, pairs)]
    unnamed x160 -> x175, local copies, waits for them, and re-layouts: 21.1 us -> 21.8 us
  transfers between devices with their start and end apart: 57 -> 56, of which waited for: 24 -> 22; matrix products, arithmetic and copies ran while one was open for 22% -> 20% of each run, Pallas kernels for 26% -> 28%
where the time goes in v3:
time: 648 us; the launch traced here: 641 us
  Pallas kernels  216 us (33%)
  waiting for transfers between devices  148 us (23%)
  local copies, waits for them, and re-layouts  103 us (16%)
  starting transfers between devices  79 us (12%)
  other arithmetic  73.7 us (11%)
  between operations  16.1 us (2%)
    pallas_call x2, Pallas kernels, body(): pl.pallas_call(partial(scan_back_kernel, heads, own, taps_n, len(w_x[i]))...  95.7 us
    ppermute x37, waiting for transfers between devices, exchange(): lax.ppermute(x, axis, [(i, i ^ 1 << bit) for i in range(lax.axis_size(axi...  94.1 us
    ppermute x8, waiting for transfers between devices, carry_states(): got = lax.ppermute(packed, axis, pairs)  47.4 us
    pallas_call x2, Pallas kernels, body(): pl.pallas_call(partial(scan_in_kernel, heads, own, taps_n, len(w_x[i])),...  47.1 us
    pallas_call x2, Pallas kernels, body(): pl.pallas_call(partial(gate_back_kernel, heads, own, full), grid=(groups,...  41.8 us
    ppermute x37, starting transfers between devices, exchange(): lax.ppermute(x, axis, [(i, i ^ 1 << bit) for i in range(lax.axis_size(axi...  40.1 us
    pallas_call x2, Pallas kernels, body(): pl.pallas_call(partial(gate_kernel, heads, own, full), grid=(groups,), in...  31.5 us
    ppermute x8, starting transfers between devices, carry_states(): got = lax.ppermute(packed, axis, pairs)  26.8 us
  transfers between devices with their start and end apart: 56, of which 22 were waited for; matrix products, arithmetic and copies ran while one was open for 20% of the time, Pallas kernels for 28%

profile of v3, /device:TPU:0, one launch (start us, length us, event | category | flops | bytes accessed | tf_op | source)
XLA Modules:
  0.0 640.7 jit_solution(15319134761696587242)
XLA Ops:
  17.1 5.4 all-gather.1
  27.7 7.6 %collective-permute-done = bf16[160,256]{1,0:T(8,128)(2,1)S(1)} collective-permute-done((bf16[160,256]{1,0:T(8,128)(2,1)S(1)}, bf16[160,256]{1,0:T(8,128)(2,1)S(1)}, u32[]{:S(2)}, u32[]{:S(2)}) %collective-permute-start) | collective-permute-done | bytes 81952 | tf_op jit(solution)/shard_map/ppermute | solution.py:599
  35.4 11.2 %collective-permute-done.7 = bf16[2,160,256]{2,1,0:T(8,128)(2,1)S(1)} collective-permute-done((bf16[2,160,256]{2,1,0:T(8,128)(2,1)S(1)}, bf16[2,160,256]{2,1,0:T(8,128)(2,1)S(1)}, u32[]{:S(2)}, u32[]{:S(2)}) %collective-permute-start.7) | collective-permute-done | bytes 163872 | tf_op jit(solution)/shard_map/ppermute | solution.py:599
  52.7 5.7 collective-permute-done.8
  59.0 9.5 %collective-permute-done.2 = bf16[2,2,160,256]{3,2,1,0:T(8,128)(2,1)} collective-permute-done((bf16[2,2,160,256]{3,2,1,0:T(8,128)(2,1)S(1)}, bf16[2,2,160,256]{3,2,1,0:T(8,128)(2,1)}, u32[]{:S(2)}, u32[]{:S(2)}) %collective-permute-start.2) | collective-permute-done | bytes 327712 | tf_op jit(solution)/shard_map/ppermute | solution.py:599
  72.0 15.1 %collective-permute-done.9 = bf16[2,2,2,160,256]{4,3,1,0,2:T(8,128)(2,1)S(1)} collective-permute-done((bf16[2,2,2,160,256]{4,3,1,0,2:T(8,128)(2,1)S(1)}, bf16[2,2,2,160,256]{4,3,1,0,2:T(8,128)(2,1)S(1)}, u32[]{:S(2)}, u32[]{:S(2)}) %collective-permute-start.9) | collective-permute-done | bytes 655392 | tf_op jit(solution)/shard_map/ppermute | solution.py:599
  113.0 23.7 %scan_in.2 = (f32[512,2048]{1,0:T(8,128)}, f32[528,2048]{1,0:T(8,128)}, bf16[144,2048]{1,0:T(8,128)(2,1)}, f32[8,2048]{1,0:T(8,128)}, f32[528,384]{1,0:T(8,128)}...) custom-call(bf16[16,1024]{1,0:T(8,128)(2,1)} %copy.212.halo, ...), custom_call_target="tpu_custom_call" | custom-call | flops 7889485824 | bytes 12582912 | tf_op jit(solution)/shard_map/scan_in/pallas_call | solution.py:827
  136.7 5.7 collective-permute-start.11
  144.8 5.5 collective-permute-start.12
  150.3 13.9 %collective-permute-done.12 = bf16[144,2048]{1,0:T(8,128)(2,1)} collective-permute-done((bf16[144,2048]{1,0:T(8,128)(2,1)S(1)}, bf16[144,2048]{1,0:T(8,128)(2,1)}, u32[]{:S(2)}, u32[]{:S(2)}) %collective-permute-start.12) | collective-permute-done | bytes 589856 | tf_op jit(solution)/shard_map/ppermute | solution.py:654
  169.6 15.8 %gate.2 = (f32[512,2048]{1,0:T(8,128)}, f32[512,2048]{1,0:T(8,128)}, f32[512,1024]{1,0:T(8,128)}, f32[512,128]{1,0:T(8,128)}, f32[512,1024]{1,0:T(8,128)}) custom-call(bf16[512,1024]{1,0:T(8,128)(2,1)} %copy.215.nrm, bf16[4,8,416,512]{3,2,1,0:T(8,128)(2,1)} %bitcast.340, bf16[4,8,416,512]{3,2,1,0:T(8,128)(2,1)} %bitcast.341, ...), custom_call_target="tpu_custom_call" | custom-call | flops 4294967296 | bytes 20971520 | tf_op jit(solution)/shard_map/gate/pallas_call | solution.py:866
  198.9 23.4 %scan_in.3 = (f32[512,2048]{1,0:T(8,128)}, f32[528,2048]{1,0:T(8,128)}, bf16[144,2048]{1,0:T(8,128)(2,1)}, f32[8,2048]{1,0:T(8,128)}, f32[528,384]{1,0:T(8,128)}...) custom-call(bf16[16,1024]{1,0:T(8,128)(2,1)} %copy.221.halo, ...), custom_call_target="tpu_custom_call" | custom-call | flops 7889485824 | bytes 12582912 | tf_op jit(solution)/shard_map/scan_in/pallas_call | solution.py:827
  222.4 7.4 %collective-permute-start.14 = (bf16[144,2048]{1,0:T(8,128)(2,1)}, bf16[144,2048]{1,0:T(8,128)(2,1)}, u32[]{:S(2)}, u32[]{:S(2)}) collective-permute-start(bf16[144,2048]{1,0:T(8,128)(2,1)} %get-tuple-element.189), channel_id=1, source_target_pairs={{0,1},{1,0},{2,3},{3,2},{4,5},{5,4},{6,7},{7,6},{8,9},{9,8},{10,11... | collective-permute-start | bytes 1769480 | tf_op jit(solution)/shard_map/ppermute | solution.py:654
  238.0 4.8 collective-permute-start.15
  246.1 9.5 %collective-permute-done.15 = bf16[144,2048]{1,0:T(8,128)(2,1)S(1)} collective-permute-done((bf16[144,2048]{1,0:T(8,128)(2,1)S(1)}, bf16[144,2048]{1,0:T(8,128)(2,1)S(1)}, u32[]{:S(2)}, u32[]{:S(2)}) %collective-permute-start.15) | collective-permute-done | bytes 589856 | tf_op jit(solution)/shard_map/ppermute | solution.py:654
  256.6 15.6 %gate.3 = (f32[512,2048]{1,0:T(8,128)}, f32[512,2048]{1,0:T(8,128)}, f32[512,1024]{1,0:T(8,128)}, f32[512,128]{1,0:T(8,128)}, f32[512,1024]{1,0:T(8,128)}) custom-call(bf16[512,1024]{1,0:T(8,128)(2,1)} %copy.224.nrm, bf16[4,8,256,512]{3,2,1,0:T(8,128)(2,1)} %bitcast.346, bf16[4,8,256,512]{3,2,1,0:T(8,128)(2,1)} %bitcast.347, ...), custom_call_target="tpu_custom_call" | custom-call | flops 4294967296 | bytes 20971520 | tf_op jit(solution)/shard_map/gate/pallas_call | solution.py:866
  272.2 20.9 %gate_back.2 = (bf16[4,8,256,512]{3,2,1,0:T(8,128)(2,1)}, f32[512,2048]{1,0:T(8,128)}, f32[512,1024]{1,0:T(8,128)}, bf16[144,2048]{1,0:T(8,128)(2,1)}, f32[8,2048]{1,0:T(8,128)}) custom-call(bf16[512,1024]{1,0:T(8,128)(2,1)} %copy.226.dbr, bf16[1024,512]{1,0:T(8,128)(2,1)} %convert_bitcast_fusion.dbrt, f32[512,1024]{1,0:T(8,128)} %get-tuple-element.192.branch, ...), custom_call_target="tpu_custom_call" | custom-call | flops 8589934592 | bytes 25165824 | tf_op jit(solution)/shard_map/gate_back/pallas_call | solution.py:939
  305.6 11.0 %collective-permute-done.17 = bf16[144,2048]{1,0:T(8,128)(2,1)S(1)} collective-permute-done((bf16[144,2048]{1,0:T(8,128)(2,1)S(1)}, bf16[144,2048]{1,0:T(8,128)(2,1)S(1)}, u32[]{:S(2)}, u32[]{:S(2)}) %collective-permute-start.17) | collective-permute-done | bytes 589856 | tf_op jit(solution)/shard_map/ppermute | solution.py:654
  319.6 47.8 %scan_back.2 = (bf16[4,8,160,512]{3,2,1,0:T(8,128)(2,1)}, bf16[1024,512]{1,0:T(8,128)(2,1)}, f32[528,1024]{1,0:T(8,128)}, f32[4,8,512]{2,1,0:T(8,128)}, f32[8,256]{1,0:T(8,128)}, /*index=5*/f32[8,128]{1,0:T(8,128)}) custom-call(f32[528,2048]{1,0:T(8,128)} %get-tuple-element.191.xin, f32[512,2048]{1,0:T(8,128)} %get-tuple-element.197.dy_in, ...), custom_call_target="tpu_custom_call" | custom-call | flops 8589934592 | bytes 25165824 | tf_op jit(solution)/shard_map/scan_back/pallas_call | solution.py:1003
  399.2 20.9 %gate_back.3 = (bf16[4,8,256,512]{3,2,1,0:T(8,128)(2,1)}, f32[512,2048]{1,0:T(8,128)}, f32[512,1024]{1,0:T(8,128)}, bf16[144,2048]{1,0:T(8,128)(2,1)}, f32[8,2048]{1,0:T(8,128)}) custom-call(bf16[512,1024]{1,0:T(8,128)(2,1)} %copy.235.dbr, bf16[1024,512]{1,0:T(8,128)(2,1)} %bitcast.357, f32[512,1024]{1,0:T(8,128)} %get-tuple-element.224.branch, ...), custom_call_target="tpu_custom_call" | custom-call | flops 8589934592 | bytes 25165824 | tf_op jit(solution)/shard_map/gate_back/pallas_call | solution.py:939
  440.1 12.4 %collective-permute-done.26 = bf16[144,2048]{1,0:T(8,128)(2,1)S(1)} collective-permute-done((bf16[144,2048]{1,0:T(8,128)(2,1)S(1)}, bf16[144,2048]{1,0:T(8,128)(2,1)S(1)}, u32[]{:S(2)}, u32[]{:S(2)}) %collective-permute-start.26) | collective-permute-done | bytes 589856 | tf_op jit(solution)/shard_map/ppermute | solution.py:654
  457.1 47.8 %scan_back.3 = (bf16[4,8,160,512]{3,2,1,0:T(8,128)(2,1)}, bf16[1024,512]{1,0:T(8,128)(2,1)}, f32[528,1024]{1,0:T(8,128)}, f32[4,8,512]{2,1,0:T(8,128)}, f32[8,256]{1,0:T(8,128)}, /*index=5*/f32[8,128]{1,0:T(8,128)}) custom-call(f32[528,2048]{1,0:T(8,128)} %get-tuple-element.220.xin, f32[512,2048]{1,0:T(8,128)} %get-tuple-element.235.dy_in, ...), custom_call_target="tpu_custom_call" | custom-call | flops 8589934592 | bytes 25165824 | tf_op jit(solution)/shard_map/scan_back/pallas_call | solution.py:1003
  508.1 4.6 constant_dynamic-slice_fusion.3
  545.2 23.7 %collective-permute-done.35 = bf16[2,2,128,512]{3,2,0,1:T(8,128)(2,1)} collective-permute-done((bf16[2,2,128,512]{3,2,0,1:T(8,128)(2,1)}, bf16[2,2,128,512]{3,2,0,1:T(8,128)(2,1)}, u32[]{:S(2)}, u32[]{:S(2)}) %collective-permute-start.35) | collective-permute-done | bytes 524320 | tf_op jit(solution)/shard_map/ppermute | solution.py:599
  (540 shorter events, 255.5 us)
Async XLA Ops:
  7.2 159.0 %all-gather.6.cloned.1.call-start = ((), (), s32[]{:S(2)}) async-start(), calls=%async_computation.2 | async-start | bytes 14057472 | tf_op jit(solution)/shard_map/all_gather | solution.py:757
  12.5 244.1 %all-gather.8.cloned.1.call-start = ((), (), s32[]{:S(2)}) async-start(), calls=%async_computation.3 | async-start | bytes 8650752 | tf_op jit(solution)/shard_map/all_gather | solution.py:757
  16.8 552.1 %reduce-scatter.2.cloned.1.call-start = ((), (), s32[]{:S(2)}) async-start(), calls=%async_computation.1 | async-start | bytes 3833856 | tf_op jit(solution)/shard_map/reduce_scatter | solution.py:995
  24.6 22.0 %collective-permute-start.7 = (bf16[2,160,256]{2,1,0:T(8,128)(2,1)S(1)}, bf16[2,160,256]{2,1,0:T(8,128)(2,1)S(1)}, u32[]{:S(2)}, u32[]{:S(2)}) collective-permute-start(bf16[2,160,256]{2,1,0:T(8,128)(2,1)S(1)} %pad_maximum_fusion.17), channel_id=1, source_target_pairs={{0,16},{4,20},{8,24},{12,28},{16,0},{20,4},{24,8},{28,12},{1,17},{... | collective-permute-start | bytes 491528 | tf_op jit(solution)/shard_map/ppermute | solution.py:599
  35.3 15.8 %collective-permute-start.1 = (bf16[2,160,256]{2,1,0:T(8,128)(2,1)S(1)}, bf16[2,160,256]{2,1,0:T(8,128)(2,1)S(1)}, u32[]{:S(2)}, u32[]{:S(2)}) collective-permute-start(bf16[2,160,256]{2,1,0:T(8,128)(2,1)S(1)} %pad_maximum_fusion.16), channel_id=1, source_target_pairs={{0,16},{4,20},{8,24},{12,28},{16,0},{20,4},{24,8},{28,12},{1,17},{... | collective-permute-start | bytes 491528 | tf_op jit(solution)/shard_map/ppermute | solution.py:599
  51.2 17.4 %collective-permute-start.2 = (bf16[2,2,160,256]{3,2,1,0:T(8,128)(2,1)S(1)}, bf16[2,2,160,256]{3,2,1,0:T(8,128)(2,1)}, u32[]{:S(2)}, u32[]{:S(2)}) collective-permute-start(bf16[2,2,160,256]{3,2,1,0:T(8,128)(2,1)S(1)} %pad_maximum_fusion.13), channel_id=1, source_target_pairs={{0,2},{1,3},{2,0},{3,1},{4,6},{5,7},{6,4},{7,5},{8,10},{9,11},{10,... | collective-permute-start | bytes 983048 | tf_op jit(solution)/shard_map/ppermute | solution.py:599
  58.6 28.5 %collective-permute-start.9 = (bf16[2,2,2,160,256]{4,3,1,0,2:T(8,128)(2,1)S(1)}, bf16[2,2,2,160,256]{4,3,1,0,2:T(8,128)(2,1)S(1)}, u32[]{:S(2)}, u32[]{:S(2)}) collective-permute-start(bf16[2,2,2,160,256]{4,3,1,0,2:T(8,128)(2,1)S(1)} %pad_maximum_fusion.11), channel_id=1, source_target_pairs={{0,2},{1,3},{2,0},{3,1},{4,6},{5,7},{6,4},{7,5},{8,10},{9,11},{10,... | collective-permute-start | bytes 1966088 | tf_op jit(solution)/shard_map/ppermute | solution.py:599
  70.5 20.6 %collective-permute-start.3 = (bf16[2,2,2,160,256]{4,3,2,1,0:T(8,128)(2,1)}, bf16[2,2,2,160,256]{4,3,2,1,0:T(8,128)(2,1)}, u32[]{:S(2)}, u32[]{:S(2)}) collective-permute-start(bf16[2,2,2,160,256]{4,3,2,1,0:T(8,128)(2,1)} %pad_maximum_fusion.10), channel_id=1, source_target_pairs={{0,4},{4,0},{8,12},{12,8},{16,20},{20,16},{24,28},{28,24},{1,5},{5... | collective-permute-start | bytes 1966088 | tf_op jit(solution)/shard_map/ppermute | solution.py:599
  144.8 19.4 %collective-permute-start.12 = (bf16[144,2048]{1,0:T(8,128)(2,1)S(1)}, bf16[144,2048]{1,0:T(8,128)(2,1)}, u32[]{:S(2)}, u32[]{:S(2)}) collective-permute-start(bf16[144,2048]{1,0:T(8,128)(2,1)S(1)} %maximum_maximum_fusion), channel_id=1, source_target_pairs={{0,2},{1,3},{4,6},{5,7},{8,10},{9,11},{12,14},{13,15},{16,18},{17,... | collective-permute-start | bytes 1769480 | tf_op jit(solution)/shard_map/ppermute | solution.py:654
  238.0 17.6 %collective-permute-start.15 = (bf16[144,2048]{1,0:T(8,128)(2,1)S(1)}, bf16[144,2048]{1,0:T(8,128)(2,1)S(1)}, u32[]{:S(2)}, u32[]{:S(2)}) collective-permute-start(bf16[144,2048]{1,0:T(8,128)(2,1)S(1)} %maximum_maximum_fusion.1), channel_id=1, source_target_pairs={{0,2},{1,3},{4,6},{5,7},{8,10},{9,11},{12,14},{13,15},{16,18},{17,... | collective-permute-start | bytes 1769480 | tf_op jit(solution)/shard_map/ppermute | solution.py:654
  298.8 17.7 %collective-permute-start.17 = (bf16[144,2048]{1,0:T(8,128)(2,1)S(1)}, bf16[144,2048]{1,0:T(8,128)(2,1)S(1)}, u32[]{:S(2)}, u32[]{:S(2)}) collective-permute-start(bf16[144,2048]{1,0:T(8,128)(2,1)S(1)} %maximum_maximum_fusion.2), channel_id=1, source_target_pairs={{2,0},{3,1},{6,4},{7,5},{10,8},{11,9},{14,12},{15,13},{18,16},{19,... | collective-permute-start | bytes 1769480 | tf_op jit(solution)/shard_map/ppermute | solution.py:654
  316.5 50.9 %collective-permute-start.20 = (bf16[2,2,2,128,512]{4,3,2,1,0:T(8,128)(2,1)S(1)}, bf16[2,2,2,128,512]{4,3,2,1,0:T(8,128)(2,1)S(1)}, u32[]{:S(2)}, u32[]{:S(2)}) collective-permute-start(bf16[2,2,2,128,512]{4,3,2,1,0:T(8,128)(2,1)S(1)} %dynamic-slice_bitcast_fusion.7), channel_id=1, source_target_pairs={{0,2},{1,3},{2,0},{3,1},{4,6},{5,7},{6,4},{7,5},{8,10},{9,11},{10,... | collective-permute-start | bytes 3145736 | tf_op jit(solution)/shard_map/ppermute | solution.py:599
  316.5 50.9 %collective-permute-start.21 = (bf16[2,2,2,128,512]{4,3,2,1,0:T(8,128)(2,1)S(1)}, bf16[2,2,2,128,512]{4,3,2,1,0:T(8,128)(2,1)S(1)}, u32[]{:S(2)}, u32[]{:S(2)}) collective-permute-start(bf16[2,2,2,128,512]{4,3,2,1,0:T(8,128)(2,1)S(1)} %dynamic-slice_bitcast_fusion.6), channel_id=1, source_target_pairs={{0,2},{1,3},{2,0},{3,1},{4,6},{5,7},{6,4},{7,5},{8,10},{9,11},{10,... | collective-permute-start | bytes 3145736 | tf_op jit(solution)/shard_map/ppermute | solution.py:599
  390.1 33.1 %collective-permute-start.24 = (bf16[2,2,2,160,512]{4,3,2,1,0:T(8,128)(2,1)}, bf16[2,2,2,160,512]{4,3,2,1,0:T(8,128)(2,1)}, u32[]{:S(2)}, u32[]{:S(2)}) collective-permute-start(bf16[2,2,2,160,512]{4,3,2,1,0:T(8,128)(2,1)} %dynamic-slice_bitcast_fusion.3), channel_id=1, source_target_pairs={{0,2},{1,3},{2,0},{3,1},{4,6},{5,7},{6,4},{7,5},{8,10},{9,11},{10,... | collective-permute-start | bytes 3932168 | tf_op jit(solution)/shard_map/ppermute | solution.py:599
  435.3 17.2 %collective-permute-start.26 = (bf16[144,2048]{1,0:T(8,128)(2,1)S(1)}, bf16[144,2048]{1,0:T(8,128)(2,1)S(1)}, u32[]{:S(2)}, u32[]{:S(2)}) collective-permute-start(bf16[144,2048]{1,0:T(8,128)(2,1)S(1)} %maximum_maximum_fusion.3), channel_id=1, source_target_pairs={{2,0},{3,1},{6,4},{7,5},{10,8},{11,9},{14,12},{15,13},{18,16},{19,... | collective-permute-start | bytes 1769480 | tf_op jit(solution)/shard_map/ppermute | solution.py:654
  453.4 51.5 %collective-permute-start.29 = (bf16[2,2,2,128,512]{4,3,0,1,2:T(8,128)(2,1)S(1)}, bf16[2,2,2,128,512]{4,3,0,1,2:T(8,128)(2,1)S(1)}, u32[]{:S(2)}, u32[]{:S(2)}) collective-permute-start(bf16[2,2,2,128,512]{4,3,0,1,2:T(8,128)(2,1)S(1)} %dynamic-slice_bitcast_fusion.5), channel_id=1, source_target_pairs={{0,2},{1,3},{2,0},{3,1},{4,6},{5,7},{6,4},{7,5},{8,10},{9,11},{10,... | collective-permute-start | bytes 3145736 | tf_op jit(solution)/shard_map/ppermute | solution.py:599
  453.5 51.5 %collective-permute-start.30 = (bf16[2,2,2,128,512]{4,3,1,2,0:T(8,128)(2,1)S(1)}, bf16[2,2,2,128,512]{4,3,1,2,0:T(8,128)(2,1)S(1)}, u32[]{:S(2)}, u32[]{:S(2)}) collective-permute-start(bf16[2,2,2,128,512]{4,3,1,2,0:T(8,128)(2,1)S(1)} %dynamic-slice_bitcast_fusion.4), channel_id=1, source_target_pairs={{0,4},{4,0},{8,12},{12,8},{16,20},{20,16},{24,28},{28,24},{1,5},{5... | collective-permute-start | bytes 3145736 | tf_op jit(solution)/shard_map/ppermute | solution.py:599
  537.0 31.9 %collective-permute-start.33 = (bf16[2,2,2,160,256]{4,3,0,1,2:T(8,128)(2,1)}, bf16[2,2,2,160,256]{4,3,0,1,2:T(8,128)(2,1)}, u32[]{:S(2)}, u32[]{:S(2)}) collective-permute-start(bf16[2,2,2,160,256]{4,3,0,1,2:T(8,128)(2,1)} %dynamic-slice_bitcast_fusion.9), channel_id=1, source_target_pairs={{0,2},{1,3},{2,0},{3,1},{4,6},{5,7},{6,4},{7,5},{8,10},{9,11},{10,... | collective-permute-start | bytes 1966088 | tf_op jit(solution)/shard_map/ppermute | solution.py:599
  540.3 28.6 %collective-permute-start.34 = (bf16[2,2,2,160,256]{4,3,1,2,0:T(8,128)(2,1)}, bf16[2,2,2,160,256]{4,3,1,2,0:T(8,128)(2,1)}, u32[]{:S(2)}, u32[]{:S(2)}) collective-permute-start(bf16[2,2,2,160,256]{4,3,1,2,0:T(8,128)(2,1)} %dynamic-slice_bitcast_fusion.8), channel_id=1, source_target_pairs={{0,4},{4,0},{8,12},{12,8},{16,20},{20,16},{24,28},{28,24},{1,5},{5... | collective-permute-start | bytes 1966088 | tf_op jit(solution)/shard_map/ppermute | solution.py:599
  540.8 28.1 %collective-permute-start.35 = (bf16[2,2,128,512]{3,2,0,1:T(8,128)(2,1)}, bf16[2,2,128,512]{3,2,0,1:T(8,128)(2,1)}, u32[]{:S(2)}, u32[]{:S(2)}) collective-permute-start(bf16[2,2,128,512]{3,2,0,1:T(8,128)(2,1)} %dynamic-slice_bitcast_fusion.11), channel_id=1, source_target_pairs={{0,4},{4,0},{8,12},{12,8},{16,20},{20,16},{24,28},{28,24},{1,5},{5... | collective-permute-start | bytes 1572872 | tf_op jit(solution)/shard_map/ppermute | solution.py:599
  542.3 26.6 %collective-permute-start.36 = (bf16[2,2,128,512]{3,2,0,1:T(8,128)(2,1)}, bf16[2,2,128,512]{3,2,0,1:T(8,128)(2,1)}, u32[]{:S(2)}, u32[]{:S(2)}) collective-permute-start(bf16[2,2,128,512]{3,2,0,1:T(8,128)(2,1)} %dynamic-slice_bitcast_fusion.10), channel_id=1, source_target_pairs={{0,2},{1,3},{2,0},{3,1},{4,6},{5,7},{6,4},{7,5},{8,10},{9,11},{10,... | collective-permute-start | bytes 1572872 | tf_op jit(solution)/shard_map/ppermute | solution.py:599
  581.1 14.6 %collective-permute-start.38 = (bf16[2,2,160,256]{3,2,0,1:T(8,128)(2,1)}, bf16[2,2,160,256]{3,2,0,1:T(8,128)(2,1)S(1)}, u32[]{:S(2)}, u32[]{:S(2)}) collective-permute-start(bf16[2,2,160,256]{3,2,0,1:T(8,128)(2,1)} %dynamic-slice_bitcast_fusion.13), channel_id=1, source_target_pairs={{0,4},{4,0},{8,12},{12,8},{16,20},{20,16},{24,28},{28,24},{1,5},{5... | collective-permute-start | bytes 983048 | tf_op jit(solution)/shard_map/ppermute | solution.py:599
  599.1 15.1 %collective-permute-start.43 = (bf16[2,160,256]{2,1,0:T(8,128)(2,1)S(1)}, bf16[2,160,256]{2,1,0:T(8,128)(2,1)S(1)}, u32[]{:S(2)}, u32[]{:S(2)}) collective-permute-start(bf16[2,160,256]{2,1,0:T(8,128)(2,1)S(1)} %dynamic-slice_bitcast_fusion.17), channel_id=1, source_target_pairs={{0,8},{4,12},{8,0},{12,4},{16,24},{20,28},{24,16},{28,20},{1,9},{5... | collective-permute-start | bytes 491528 | tf_op jit(solution)/shard_map/ppermute | solution.py:599
  599.4 14.8 %collective-permute-start.44 = (bf16[2,160,256]{2,1,0:T(8,128)(2,1)S(1)}, bf16[2,160,256]{2,1,0:T(8,128)(2,1)S(1)}, u32[]{:S(2)}, u32[]{:S(2)}) collective-permute-start(bf16[2,160,256]{2,1,0:T(8,128)(2,1)S(1)} %dynamic-slice_bitcast_fusion.16), channel_id=1, source_target_pairs={{0,8},{4,12},{8,0},{12,4},{16,24},{20,28},{24,16},{28,20},{1,9},{5... | collective-permute-start | bytes 491528 | tf_op jit(solution)/shard_map/ppermute | solution.py:599
  (112 other events, 628.5 us)
Sparse Core Ops, SparseCore 0:
  12.6 125.5 all-gather.5
  141.2 79.9 all-gather.7
  453.5 80.5 reduce-scatter.1

commit v4 on v3

--- a/solution.py
+++ b/solution.py
@@ -452,9 +452,10 @@
     ds = ds_in[...].astype(f32)
     for c in reversed(range(chunks)):
         lo, hi = c * SPAN, (c + 1) * SPAN
-        dxs = ex[lo:hi] * mm3(b_in[lo:hi], ds)
-        db_scr[lo:hi] += mmt3(exd[lo:hi], ds)
-        dc_scr[lo:hi] += mmt3(fdy[lo:hi], states[c])
+        dsb, fdyb = low(ds), low(fdy[lo:hi])
+        dxs = ex[lo:hi] * mm(low(b_in[lo:hi]), dsb)
+        db_scr[lo:hi] += mmt(low(exd[lo:hi]), dsb)
+        dc_scr[lo:hi] += mmt(fdyb, low(states[c]))
         mt, gt = mt_scr[c], gt_scr[c]
         parts = []
         dgt = None
@@ -487,7 +488,7 @@
         dcum_scr[hi - 8 : hi] += tail8 * lastrow
         ddt_scr[lo:hi] += gather_heads(xcc * dxd, group, own)
         dxc_scr[lo:hi] = dtx[lo:hi] * dxd + skip * dy[lo:hi]
-        ds = fx[hi - 1 : hi] * ds + mm3(ct[:, lo:hi], fdy[lo:hi])
+        ds = fx[hi - 1 : hi] * ds + mm(low(ct[:, lo:hi]), fdyb)
     du = dxc_scr[...] * (sg + xc * (1.0 - sg))
     sums, bias = conv_back(du, xin[...], prm[0], keep, rows, taps_n, dx_scr)
     g_skip = jnp.sum(dy * xc, axis=0, keepdims=True)

time: 648 us -> 642 us (level)
  transfers between devices with their start and end apart: 56 -> 56, of which waited for: 22 -> 23; matrix products, arithmetic and copies ran while one was open for 20% -> 20% of each run, Pallas kernels for 28% -> 27%
where the time goes in v4:
time: 642 us; the launch traced here: 635 us
  Pallas kernels  210 us (33%)
  waiting for transfers between devices  148 us (23%)
  local copies, waits for them, and re-layouts  103 us (16%)
  starting transfers between devices  79.1 us (12%)
  other arithmetic  73.8 us (11%)
  between operations  16.1 us (3%)
    ppermute x37, waiting for transfers between devices, exchange(): lax.ppermute(x, axis, [(i, i ^ 1 << bit) for i in range(lax.axis_size(axi...  94 us
    pallas_call x2, Pallas kernels, body(): pl.pallas_call(partial(scan_back_kernel, heads, own, taps_n, len(w_x[i]))...  89.5 us
    ppermute x8, waiting for transfers between devices, carry_states(): got = lax.ppermute(packed, axis, pairs)  47.4 us
    pallas_call x2, Pallas kernels, body(): pl.pallas_call(partial(scan_in_kernel, heads, own, taps_n, len(w_x[i])),...  47.1 us
    pallas_call x2, Pallas kernels, body(): pl.pallas_call(partial(gate_back_kernel, heads, own, full), grid=(groups,...  41.8 us
    ppermute x37, starting transfers between devices, exchange(): lax.ppermute(x, axis, [(i, i ^ 1 << bit) for i in range(lax.axis_size(axi...  40.1 us
    pallas_call x2, Pallas kernels, body(): pl.pallas_call(partial(gate_kernel, heads, own, full), grid=(groups,), in...  31.5 us
    ppermute x8, starting transfers between devices, carry_states(): got = lax.ppermute(packed, axis, pairs)  26.8 us
  transfers between devices with their start and end apart: 56, of which 23 were waited for; matrix products, arithmetic and copies ran while one was open for 20% of the time, Pallas kernels for 27%

profile of v4, /device:TPU:0, one launch (start us, length us, event | category | flops | bytes accessed | tf_op | source)
XLA Modules:
  0.0 634.7 jit_solution(9601771708754797401)
XLA Ops:
  17.1 5.4 all-gather.1
  27.7 7.6 %collective-permute-done = bf16[160,256]{1,0:T(8,128)(2,1)S(1)} collective-permute-done((bf16[160,256]{1,0:T(8,128)(2,1)S(1)}, bf16[160,256]{1,0:T(8,128)(2,1)S(1)}, u32[]{:S(2)}, u32[]{:S(2)}) %collective-permute-start) | collective-permute-done | bytes 81952 | tf_op jit(solution)/shard_map/ppermute | solution.py:600
  35.4 11.2 %collective-permute-done.7 = bf16[2,160,256]{2,1,0:T(8,128)(2,1)S(1)} collective-permute-done((bf16[2,160,256]{2,1,0:T(8,128)(2,1)S(1)}, bf16[2,160,256]{2,1,0:T(8,128)(2,1)S(1)}, u32[]{:S(2)}, u32[]{:S(2)}) %collective-permute-start.7) | collective-permute-done | bytes 163872 | tf_op jit(solution)/shard_map/ppermute | solution.py:600
  52.7 5.7 collective-permute-done.8
  59.0 9.5 %collective-permute-done.2 = bf16[2,2,160,256]{3,2,1,0:T(8,128)(2,1)} collective-permute-done((bf16[2,2,160,256]{3,2,1,0:T(8,128)(2,1)S(1)}, bf16[2,2,160,256]{3,2,1,0:T(8,128)(2,1)}, u32[]{:S(2)}, u32[]{:S(2)}) %collective-permute-start.2) | collective-permute-done | bytes 327712 | tf_op jit(solution)/shard_map/ppermute | solution.py:600
  72.0 15.1 %collective-permute-done.9 = bf16[2,2,2,160,256]{4,3,1,0,2:T(8,128)(2,1)S(1)} collective-permute-done((bf16[2,2,2,160,256]{4,3,1,0,2:T(8,128)(2,1)S(1)}, bf16[2,2,2,160,256]{4,3,1,0,2:T(8,128)(2,1)S(1)}, u32[]{:S(2)}, u32[]{:S(2)}) %collective-permute-start.9) | collective-permute-done | bytes 655392 | tf_op jit(solution)/shard_map/ppermute | solution.py:600
  113.0 23.7 %scan_in.2 = (f32[512,2048]{1,0:T(8,128)}, f32[528,2048]{1,0:T(8,128)}, bf16[144,2048]{1,0:T(8,128)(2,1)}, f32[8,2048]{1,0:T(8,128)}, f32[528,384]{1,0:T(8,128)}...) custom-call(bf16[16,1024]{1,0:T(8,128)(2,1)} %copy.212.halo, ...), custom_call_target="tpu_custom_call" | custom-call | flops 7889485824 | bytes 12582912 | tf_op jit(solution)/shard_map/scan_in/pallas_call | solution.py:828
  136.7 5.7 collective-permute-start.11
  144.8 5.5 collective-permute-start.12
  150.3 13.9 %collective-permute-done.12 = bf16[144,2048]{1,0:T(8,128)(2,1)} collective-permute-done((bf16[144,2048]{1,0:T(8,128)(2,1)S(1)}, bf16[144,2048]{1,0:T(8,128)(2,1)}, u32[]{:S(2)}, u32[]{:S(2)}) %collective-permute-start.12) | collective-permute-done | bytes 589856 | tf_op jit(solution)/shard_map/ppermute | solution.py:655
  169.6 15.8 %gate.2 = (f32[512,2048]{1,0:T(8,128)}, f32[512,2048]{1,0:T(8,128)}, f32[512,1024]{1,0:T(8,128)}, f32[512,128]{1,0:T(8,128)}, f32[512,1024]{1,0:T(8,128)}) custom-call(bf16[512,1024]{1,0:T(8,128)(2,1)} %copy.215.nrm, bf16[4,8,416,512]{3,2,1,0:T(8,128)(2,1)} %bitcast.340, bf16[4,8,416,512]{3,2,1,0:T(8,128)(2,1)} %bitcast.341, ...), custom_call_target="tpu_custom_call" | custom-call | flops 4294967296 | bytes 20971520 | tf_op jit(solution)/shard_map/gate/pallas_call | solution.py:867
  198.9 23.4 %scan_in.3 = (f32[512,2048]{1,0:T(8,128)}, f32[528,2048]{1,0:T(8,128)}, bf16[144,2048]{1,0:T(8,128)(2,1)}, f32[8,2048]{1,0:T(8,128)}, f32[528,384]{1,0:T(8,128)}...) custom-call(bf16[16,1024]{1,0:T(8,128)(2,1)} %copy.221.halo, ...), custom_call_target="tpu_custom_call" | custom-call | flops 7889485824 | bytes 12582912 | tf_op jit(solution)/shard_map/scan_in/pallas_call | solution.py:828
  222.4 7.4 %collective-permute-start.14 = (bf16[144,2048]{1,0:T(8,128)(2,1)}, bf16[144,2048]{1,0:T(8,128)(2,1)}, u32[]{:S(2)}, u32[]{:S(2)}) collective-permute-start(bf16[144,2048]{1,0:T(8,128)(2,1)} %get-tuple-element.189), channel_id=1, source_target_pairs={{0,1},{1,0},{2,3},{3,2},{4,5},{5,4},{6,7},{7,6},{8,9},{9,8},{10,11... | collective-permute-start | bytes 1769480 | tf_op jit(solution)/shard_map/ppermute | solution.py:655
  238.0 4.8 collective-permute-start.15
  246.1 9.5 %collective-permute-done.15 = bf16[144,2048]{1,0:T(8,128)(2,1)S(1)} collective-permute-done((bf16[144,2048]{1,0:T(8,128)(2,1)S(1)}, bf16[144,2048]{1,0:T(8,128)(2,1)S(1)}, u32[]{:S(2)}, u32[]{:S(2)}) %collective-permute-start.15) | collective-permute-done | bytes 589856 | tf_op jit(solution)/shard_map/ppermute | solution.py:655
  256.6 15.6 %gate.3 = (f32[512,2048]{1,0:T(8,128)}, f32[512,2048]{1,0:T(8,128)}, f32[512,1024]{1,0:T(8,128)}, f32[512,128]{1,0:T(8,128)}, f32[512,1024]{1,0:T(8,128)}) custom-call(bf16[512,1024]{1,0:T(8,128)(2,1)} %copy.224.nrm, bf16[4,8,256,512]{3,2,1,0:T(8,128)(2,1)} %bitcast.346, bf16[4,8,256,512]{3,2,1,0:T(8,128)(2,1)} %bitcast.347, ...), custom_call_target="tpu_custom_call" | custom-call | flops 4294967296 | bytes 20971520 | tf_op jit(solution)/shard_map/gate/pallas_call | solution.py:867
  272.2 20.9 %gate_back.2 = (bf16[4,8,256,512]{3,2,1,0:T(8,128)(2,1)}, f32[512,2048]{1,0:T(8,128)}, f32[512,1024]{1,0:T(8,128)}, bf16[144,2048]{1,0:T(8,128)(2,1)}, f32[8,2048]{1,0:T(8,128)}) custom-call(bf16[512,1024]{1,0:T(8,128)(2,1)} %copy.226.dbr, bf16[1024,512]{1,0:T(8,128)(2,1)} %convert_bitcast_fusion.dbrt, f32[512,1024]{1,0:T(8,128)} %get-tuple-element.192.branch, ...), custom_call_target="tpu_custom_call" | custom-call | flops 8589934592 | bytes 25165824 | tf_op jit(solution)/shard_map/gate_back/pallas_call | solution.py:940
  305.6 11.0 %collective-permute-done.17 = bf16[144,2048]{1,0:T(8,128)(2,1)S(1)} collective-permute-done((bf16[144,2048]{1,0:T(8,128)(2,1)S(1)}, bf16[144,2048]{1,0:T(8,128)(2,1)S(1)}, u32[]{:S(2)}, u32[]{:S(2)}) %collective-permute-start.17) | collective-permute-done | bytes 589856 | tf_op jit(solution)/shard_map/ppermute | solution.py:655
  319.6 44.8 %scan_back.2 = (bf16[4,8,160,512]{3,2,1,0:T(8,128)(2,1)}, bf16[1024,512]{1,0:T(8,128)(2,1)}, f32[528,1024]{1,0:T(8,128)}, f32[4,8,512]{2,1,0:T(8,128)}, f32[8,256]{1,0:T(8,128)}, /*index=5*/f32[8,128]{1,0:T(8,128)}) custom-call(f32[528,2048]{1,0:T(8,128)} %get-tuple-element.191.xin, f32[512,2048]{1,0:T(8,128)} %get-tuple-element.197.dy_in, ...), custom_call_target="tpu_custom_call" | custom-call | flops 8589934592 | bytes 25165824 | tf_op jit(solution)/shard_map/scan_back/pallas_call | solution.py:1004
  396.1 20.9 %gate_back.3 = (bf16[4,8,256,512]{3,2,1,0:T(8,128)(2,1)}, f32[512,2048]{1,0:T(8,128)}, f32[512,1024]{1,0:T(8,128)}, bf16[144,2048]{1,0:T(8,128)(2,1)}, f32[8,2048]{1,0:T(8,128)}) custom-call(bf16[512,1024]{1,0:T(8,128)(2,1)} %copy.235.dbr, bf16[1024,512]{1,0:T(8,128)(2,1)} %bitcast.357, f32[512,1024]{1,0:T(8,128)} %get-tuple-element.224.branch, ...), custom_call_target="tpu_custom_call" | custom-call | flops 8589934592 | bytes 25165824 | tf_op jit(solution)/shard_map/gate_back/pallas_call | solution.py:940
  437.0 12.4 %collective-permute-done.26 = bf16[144,2048]{1,0:T(8,128)(2,1)S(1)} collective-permute-done((bf16[144,2048]{1,0:T(8,128)(2,1)S(1)}, bf16[144,2048]{1,0:T(8,128)(2,1)S(1)}, u32[]{:S(2)}, u32[]{:S(2)}) %collective-permute-start.26) | collective-permute-done | bytes 589856 | tf_op jit(solution)/shard_map/ppermute | solution.py:655
  454.0 44.8 %scan_back.3 = (bf16[4,8,160,512]{3,2,1,0:T(8,128)(2,1)}, bf16[1024,512]{1,0:T(8,128)(2,1)}, f32[528,1024]{1,0:T(8,128)}, f32[4,8,512]{2,1,0:T(8,128)}, f32[8,256]{1,0:T(8,128)}, /*index=5*/f32[8,128]{1,0:T(8,128)}) custom-call(f32[528,2048]{1,0:T(8,128)} %get-tuple-element.220.xin, f32[512,2048]{1,0:T(8,128)} %get-tuple-element.235.dy_in, ...), custom_call_target="tpu_custom_call" | custom-call | flops 8589934592 | bytes 25165824 | tf_op jit(solution)/shard_map/scan_back/pallas_call | solution.py:1004
  501.9 4.5 constant_dynamic-slice_fusion.3
  539.2 23.7 %collective-permute-done.35 = bf16[2,2,128,512]{3,2,0,1:T(8,128)(2,1)} collective-permute-done((bf16[2,2,128,512]{3,2,0,1:T(8,128)(2,1)}, bf16[2,2,128,512]{3,2,0,1:T(8,128)(2,1)}, u32[]{:S(2)}, u32[]{:S(2)}) %collective-permute-start.35) | collective-permute-done | bytes 524320 | tf_op jit(solution)/shard_map/ppermute | solution.py:600
  (540 shorter events, 255.7 us)
Async XLA Ops:
  7.2 159.0 %all-gather.6.cloned.1.call-start = ((), (), s32[]{:S(2)}) async-start(), calls=%async_computation.2 | async-start | bytes 14057472 | tf_op jit(solution)/shard_map/all_gather | solution.py:758
  12.5 244.1 %all-gather.8.cloned.1.call-start = ((), (), s32[]{:S(2)}) async-start(), calls=%async_computation.3 | async-start | bytes 8650752 | tf_op jit(solution)/shard_map/all_gather | solution.py:758
  16.8 546.0 %reduce-scatter.2.cloned.1.call-start = ((), (), s32[]{:S(2)}) async-start(), calls=%async_computation.1 | async-start | bytes 3833856 | tf_op jit(solution)/shard_map/reduce_scatter | solution.py:996
  24.6 22.0 %collective-permute-start.7 = (bf16[2,160,256]{2,1,0:T(8,128)(2,1)S(1)}, bf16[2,160,256]{2,1,0:T(8,128)(2,1)S(1)}, u32[]{:S(2)}, u32[]{:S(2)}) collective-permute-start(bf16[2,160,256]{2,1,0:T(8,128)(2,1)S(1)} %pad_maximum_fusion.17), channel_id=1, source_target_pairs={{0,16},{4,20},{8,24},{12,28},{16,0},{20,4},{24,8},{28,12},{1,17},{... | collective-permute-start | bytes 491528 | tf_op jit(solution)/shard_map/ppermute | solution.py:600
  35.3 15.8 %collective-permute-start.1 = (bf16[2,160,256]{2,1,0:T(8,128)(2,1)S(1)}, bf16[2,160,256]{2,1,0:T(8,128)(2,1)S(1)}, u32[]{:S(2)}, u32[]{:S(2)}) collective-permute-start(bf16[2,160,256]{2,1,0:T(8,128)(2,1)S(1)} %pad_maximum_fusion.16), channel_id=1, source_target_pairs={{0,16},{4,20},{8,24},{12,28},{16,0},{20,4},{24,8},{28,12},{1,17},{... | collective-permute-start | bytes 491528 | tf_op jit(solution)/shard_map/ppermute | solution.py:600
  51.2 17.4 %collective-permute-start.2 = (bf16[2,2,160,256]{3,2,1,0:T(8,128)(2,1)S(1)}, bf16[2,2,160,256]{3,2,1,0:T(8,128)(2,1)}, u32[]{:S(2)}, u32[]{:S(2)}) collective-permute-start(bf16[2,2,160,256]{3,2,1,0:T(8,128)(2,1)S(1)} %pad_maximum_fusion.13), channel_id=1, source_target_pairs={{0,2},{1,3},{2,0},{3,1},{4,6},{5,7},{6,4},{7,5},{8,10},{9,11},{10,... | collective-permute-start | bytes 983048 | tf_op jit(solution)/shard_map/ppermute | solution.py:600
  58.6 28.5 %collective-permute-start.9 = (bf16[2,2,2,160,256]{4,3,1,0,2:T(8,128)(2,1)S(1)}, bf16[2,2,2,160,256]{4,3,1,0,2:T(8,128)(2,1)S(1)}, u32[]{:S(2)}, u32[]{:S(2)}) collective-permute-start(bf16[2,2,2,160,256]{4,3,1,0,2:T(8,128)(2,1)S(1)} %pad_maximum_fusion.11), channel_id=1, source_target_pairs={{0,2},{1,3},{2,0},{3,1},{4,6},{5,7},{6,4},{7,5},{8,10},{9,11},{10,... | collective-permute-start | bytes 1966088 | tf_op jit(solution)/shard_map/ppermute | solution.py:600
  70.5 20.6 %collective-permute-start.3 = (bf16[2,2,2,160,256]{4,3,2,1,0:T(8,128)(2,1)}, bf16[2,2,2,160,256]{4,3,2,1,0:T(8,128)(2,1)}, u32[]{:S(2)}, u32[]{:S(2)}) collective-permute-start(bf16[2,2,2,160,256]{4,3,2,1,0:T(8,128)(2,1)} %pad_maximum_fusion.10), channel_id=1, source_target_pairs={{0,4},{4,0},{8,12},{12,8},{16,20},{20,16},{24,28},{28,24},{1,5},{5... | collective-permute-start | bytes 1966088 | tf_op jit(solution)/shard_map/ppermute | solution.py:600
  144.8 19.4 %collective-permute-start.12 = (bf16[144,2048]{1,0:T(8,128)(2,1)S(1)}, bf16[144,2048]{1,0:T(8,128)(2,1)}, u32[]{:S(2)}, u32[]{:S(2)}) collective-permute-start(bf16[144,2048]{1,0:T(8,128)(2,1)S(1)} %maximum_maximum_fusion), channel_id=1, source_target_pairs={{0,2},{1,3},{4,6},{5,7},{8,10},{9,11},{12,14},{13,15},{16,18},{17,... | collective-permute-start | bytes 1769480 | tf_op jit(solution)/shard_map/ppermute | solution.py:655
  238.0 17.6 %collective-permute-start.15 = (bf16[144,2048]{1,0:T(8,128)(2,1)S(1)}, bf16[144,2048]{1,0:T(8,128)(2,1)S(1)}, u32[]{:S(2)}, u32[]{:S(2)}) collective-permute-start(bf16[144,2048]{1,0:T(8,128)(2,1)S(1)} %maximum_maximum_fusion.1), channel_id=1, source_target_pairs={{0,2},{1,3},{4,6},{5,7},{8,10},{9,11},{12,14},{13,15},{16,18},{17,... | collective-permute-start | bytes 1769480 | tf_op jit(solution)/shard_map/ppermute | solution.py:655
  298.8 17.7 %collective-permute-start.17 = (bf16[144,2048]{1,0:T(8,128)(2,1)S(1)}, bf16[144,2048]{1,0:T(8,128)(2,1)S(1)}, u32[]{:S(2)}, u32[]{:S(2)}) collective-permute-start(bf16[144,2048]{1,0:T(8,128)(2,1)S(1)} %maximum_maximum_fusion.2), channel_id=1, source_target_pairs={{2,0},{3,1},{6,4},{7,5},{10,8},{11,9},{14,12},{15,13},{18,16},{19,... | collective-permute-start | bytes 1769480 | tf_op jit(solution)/shard_map/ppermute | solution.py:655
  316.5 47.8 %collective-permute-start.20 = (bf16[2,2,2,128,512]{4,3,2,1,0:T(8,128)(2,1)S(1)}, bf16[2,2,2,128,512]{4,3,2,1,0:T(8,128)(2,1)S(1)}, u32[]{:S(2)}, u32[]{:S(2)}) collective-permute-start(bf16[2,2,2,128,512]{4,3,2,1,0:T(8,128)(2,1)S(1)} %dynamic-slice_bitcast_fusion.7), channel_id=1, source_target_pairs={{0,2},{1,3},{2,0},{3,1},{4,6},{5,7},{6,4},{7,5},{8,10},{9,11},{10,... | collective-permute-start | bytes 3145736 | tf_op jit(solution)/shard_map/ppermute | solution.py:600
  316.5 47.8 %collective-permute-start.21 = (bf16[2,2,2,128,512]{4,3,2,1,0:T(8,128)(2,1)S(1)}, bf16[2,2,2,128,512]{4,3,2,1,0:T(8,128)(2,1)S(1)}, u32[]{:S(2)}, u32[]{:S(2)}) collective-permute-start(bf16[2,2,2,128,512]{4,3,2,1,0:T(8,128)(2,1)S(1)} %dynamic-slice_bitcast_fusion.6), channel_id=1, source_target_pairs={{0,2},{1,3},{2,0},{3,1},{4,6},{5,7},{6,4},{7,5},{8,10},{9,11},{10,... | collective-permute-start | bytes 3145736 | tf_op jit(solution)/shard_map/ppermute | solution.py:600
  387.0 33.1 %collective-permute-start.24 = (bf16[2,2,2,160,512]{4,3,2,1,0:T(8,128)(2,1)}, bf16[2,2,2,160,512]{4,3,2,1,0:T(8,128)(2,1)}, u32[]{:S(2)}, u32[]{:S(2)}) collective-permute-start(bf16[2,2,2,160,512]{4,3,2,1,0:T(8,128)(2,1)} %dynamic-slice_bitcast_fusion.3), channel_id=1, source_target_pairs={{0,2},{1,3},{2,0},{3,1},{4,6},{5,7},{6,4},{7,5},{8,10},{9,11},{10,... | collective-permute-start | bytes 3932168 | tf_op jit(solution)/shard_map/ppermute | solution.py:600
  432.2 17.2 %collective-permute-start.26 = (bf16[144,2048]{1,0:T(8,128)(2,1)S(1)}, bf16[144,2048]{1,0:T(8,128)(2,1)S(1)}, u32[]{:S(2)}, u32[]{:S(2)}) collective-permute-start(bf16[144,2048]{1,0:T(8,128)(2,1)S(1)} %maximum_maximum_fusion.3), channel_id=1, source_target_pairs={{2,0},{3,1},{6,4},{7,5},{10,8},{11,9},{14,12},{15,13},{18,16},{19,... | collective-permute-start | bytes 1769480 | tf_op jit(solution)/shard_map/ppermute | solution.py:655
  450.3 48.4 %collective-permute-start.29 = (bf16[2,2,2,128,512]{4,3,0,1,2:T(8,128)(2,1)S(1)}, bf16[2,2,2,128,512]{4,3,0,1,2:T(8,128)(2,1)S(1)}, u32[]{:S(2)}, u32[]{:S(2)}) collective-permute-start(bf16[2,2,2,128,512]{4,3,0,1,2:T(8,128)(2,1)S(1)} %dynamic-slice_bitcast_fusion.5), channel_id=1, source_target_pairs={{0,2},{1,3},{2,0},{3,1},{4,6},{5,7},{6,4},{7,5},{8,10},{9,11},{10,... | collective-permute-start | bytes 3145736 | tf_op jit(solution)/shard_map/ppermute | solution.py:600
  450.4 48.4 %collective-permute-start.30 = (bf16[2,2,2,128,512]{4,3,1,2,0:T(8,128)(2,1)S(1)}, bf16[2,2,2,128,512]{4,3,1,2,0:T(8,128)(2,1)S(1)}, u32[]{:S(2)}, u32[]{:S(2)}) collective-permute-start(bf16[2,2,2,128,512]{4,3,1,2,0:T(8,128)(2,1)S(1)} %dynamic-slice_bitcast_fusion.4), channel_id=1, source_target_pairs={{0,4},{4,0},{8,12},{12,8},{16,20},{20,16},{24,28},{28,24},{1,5},{5... | collective-permute-start | bytes 3145736 | tf_op jit(solution)/shard_map/ppermute | solution.py:600
  530.8 32.0 %collective-permute-start.33 = (bf16[2,2,2,160,256]{4,3,0,1,2:T(8,128)(2,1)}, bf16[2,2,2,160,256]{4,3,0,1,2:T(8,128)(2,1)}, u32[]{:S(2)}, u32[]{:S(2)}) collective-permute-start(bf16[2,2,2,160,256]{4,3,0,1,2:T(8,128)(2,1)} %dynamic-slice_bitcast_fusion.9), channel_id=1, source_target_pairs={{0,2},{1,3},{2,0},{3,1},{4,6},{5,7},{6,4},{7,5},{8,10},{9,11},{10,... | collective-permute-start | bytes 1966088 | tf_op jit(solution)/shard_map/ppermute | solution.py:600
  534.1 28.8 %collective-permute-start.34 = (bf16[2,2,2,160,256]{4,3,1,2,0:T(8,128)(2,1)}, bf16[2,2,2,160,256]{4,3,1,2,0:T(8,128)(2,1)}, u32[]{:S(2)}, u32[]{:S(2)}) collective-permute-start(bf16[2,2,2,160,256]{4,3,1,2,0:T(8,128)(2,1)} %dynamic-slice_bitcast_fusion.8), channel_id=1, source_target_pairs={{0,4},{4,0},{8,12},{12,8},{16,20},{20,16},{24,28},{28,24},{1,5},{5... | collective-permute-start | bytes 1966088 | tf_op jit(solution)/shard_map/ppermute | solution.py:600
  534.6 28.2 %collective-permute-start.35 = (bf16[2,2,128,512]{3,2,0,1:T(8,128)(2,1)}, bf16[2,2,128,512]{3,2,0,1:T(8,128)(2,1)}, u32[]{:S(2)}, u32[]{:S(2)}) collective-permute-start(bf16[2,2,128,512]{3,2,0,1:T(8,128)(2,1)} %dynamic-slice_bitcast_fusion.11), channel_id=1, source_target_pairs={{0,4},{4,0},{8,12},{12,8},{16,20},{20,16},{24,28},{28,24},{1,5},{5... | collective-permute-start | bytes 1572872 | tf_op jit(solution)/shard_map/ppermute | solution.py:600
  536.1 26.7 %collective-permute-start.36 = (bf16[2,2,128,512]{3,2,0,1:T(8,128)(2,1)}, bf16[2,2,128,512]{3,2,0,1:T(8,128)(2,1)}, u32[]{:S(2)}, u32[]{:S(2)}) collective-permute-start(bf16[2,2,128,512]{3,2,0,1:T(8,128)(2,1)} %dynamic-slice_bitcast_fusion.10), channel_id=1, source_target_pairs={{0,2},{1,3},{2,0},{3,1},{4,6},{5,7},{6,4},{7,5},{8,10},{9,11},{10,... | collective-permute-start | bytes 1572872 | tf_op jit(solution)/shard_map/ppermute | solution.py:600
  575.0 14.5 %collective-permute-start.38 = (bf16[2,2,160,256]{3,2,0,1:T(8,128)(2,1)}, bf16[2,2,160,256]{3,2,0,1:T(8,128)(2,1)S(1)}, u32[]{:S(2)}, u32[]{:S(2)}) collective-permute-start(bf16[2,2,160,256]{3,2,0,1:T(8,128)(2,1)} %dynamic-slice_bitcast_fusion.13), channel_id=1, source_target_pairs={{0,4},{4,0},{8,12},{12,8},{16,20},{20,16},{24,28},{28,24},{1,5},{5... | collective-permute-start | bytes 983048 | tf_op jit(solution)/shard_map/ppermute | solution.py:600
  592.9 15.1 %collective-permute-start.43 = (bf16[2,160,256]{2,1,0:T(8,128)(2,1)S(1)}, bf16[2,160,256]{2,1,0:T(8,128)(2,1)S(1)}, u32[]{:S(2)}, u32[]{:S(2)}) collective-permute-start(bf16[2,160,256]{2,1,0:T(8,128)(2,1)S(1)} %dynamic-slice_bitcast_fusion.17), channel_id=1, source_target_pairs={{0,8},{4,12},{8,0},{12,4},{16,24},{20,28},{24,16},{28,20},{1,9},{5... | collective-permute-start | bytes 491528 | tf_op jit(solution)/shard_map/ppermute | solution.py:600
  593.2 14.7 %collective-permute-start.44 = (bf16[2,160,256]{2,1,0:T(8,128)(2,1)S(1)}, bf16[2,160,256]{2,1,0:T(8,128)(2,1)S(1)}, u32[]{:S(2)}, u32[]{:S(2)}) collective-permute-start(bf16[2,160,256]{2,1,0:T(8,128)(2,1)S(1)} %dynamic-slice_bitcast_fusion.16), channel_id=1, source_target_pairs={{0,8},{4,12},{8,0},{12,4},{16,24},{20,28},{24,16},{28,20},{1,9},{5... | collective-permute-start | bytes 491528 | tf_op jit(solution)/shard_map/ppermute | solution.py:600
  (112 other events, 628.9 us)
Sparse Core Ops, SparseCore 0:
  12.6 125.5 all-gather.5
  141.2 79.9 all-gather.7
  450.4 80.5 reduce-scatter.1
